TPU v7x, 256 devices: a whole 4x4x8 slice. The times are simulated.
256 devices in a mesh: ctx: 32 (over z, y_lo, core), tp: 8 (over x, y_hi).
Axes of the slice: x: 4, y: 4 (y_hi: 2, y_lo: 2; y = y_hi * 2 + y_lo), z: 8, core: 2. Of those that a mesh axis runs over, the one named last changes fastest.
Arguments:
- queries: bfloat16 [4096, 64, 128], P('ctx', 'tp'), may hold values from -5 to 5
- key_states: bfloat16 [4096, 8, 128], P('ctx', 'tp'), may hold values from -5 to 5
- value_vectors: bfloat16 [4096, 8, 128], P('ctx', 'tp'), may hold values from -6 to 6
- grad_output: bfloat16 [4096, 8192], P(('ctx', 'tp')), may hold values from -6 to 6
- out_weight: bfloat16 [8192, 8192], P('ctx', 'tp'), may hold values from -0.0625 to 0.0625
- doc_lengths: int32 [8], replicated, may hold values from 1 to 2560, as said below
Outputs:
- query_grads: bfloat16 [4096, 64, 128], P('ctx', 'tp')
- key_gradient: bfloat16 [4096, 8, 128], P('ctx', 'tp')
- value_gradient: bfloat16 [4096, 8, 128], P('ctx', 'tp')
Inputs may be any that keep to these rules, and one draw needn't show every extreme that they name: `doc_lengths`: the lengths sum to 4096; exactly one document is 2560 positions long, every other one is shorter.
All inputs are finite; a program needn't handle non-finite values.
Results may differ from a plain program's by a relative error of at most 0.02.
Values may be sent and summed in bfloat16 or wider, within the bound.
No kernel may reach another device: no remote copies, remote signals or barrier semaphores. Data moves between devices by JAX's collectives and lax.ppermute only.
A program may use at most 64 MiB of HBM per device.

v0:
```python
import math

import jax
import jax.numpy as jnp
from jax import lax
from jax.sharding import PartitionSpec as P

NEG_FILL = -1e30


def doc_of(doc_ends, position):
    return jnp.sum((doc_ends[None, :] <= position[:, None]).astype(jnp.int32), axis=1)


def by_blocks(step_fn, running, pieces):
    row_count = pieces[0].shape[0]
    block_rows = math.gcd(row_count, 128)
    blocks = row_count // block_rows

    def one_block(number, current):
        offset = number * block_rows
        sliced = tuple(
            (lax.dynamic_slice_in_dim(member, offset, block_rows, 0) for member in pieces)
        )
        return step_fn(current, sliced, offset, offset)

    return lax.fori_loop(0, blocks, one_block, running)


def add_at(target, addend, position):
    current = lax.dynamic_slice_in_dim(target, position, addend.shape[0], 0)
    return lax.dynamic_update_slice_in_dim(target, current + addend, position, 0)


def local(queries, key_states, value_vectors, grad_output, out_weight, doc_lengths):
    tok_rows, heads_here, head_dim = queries.shape
    kv_here = key_states.shape[1]
    group_width = heads_here // kv_here
    score_scale = head_dim ** (-0.5)
    highest = lax.Precision.HIGHEST
    ctx_count = lax.axis_size("ctx")
    ctx_rank = lax.axis_index("ctx")
    doc_ends = jnp.cumsum(doc_lengths)
    query_pos = ctx_rank * tok_rows + jnp.arange(tok_rows, dtype=jnp.int32)
    query_doc = doc_of(doc_ends, query_pos)
    query_four = queries.reshape(tok_rows, kv_here, group_width, head_dim)

    def allowed_pairs(anchor, row_count):
        key_index = anchor + jnp.arange(row_count, dtype=jnp.int32)
        key_doc = doc_of(doc_ends, key_index)
        same_doc = query_doc[:, None] == key_doc[None, :]
        return same_doc & (key_index[None, :] <= query_pos[:, None]) & (key_index[None, :] >= 0)

    def raw_scores(key_block):
        return (
            jnp.einsum("tgjd,sgd->gjts", query_four, key_block, preferred_element_type=jnp.float32)
            * score_scale
        )

    def guarded(compute, running):
        result = compute(running)
        return result

    def forward_step(running, pieces, anchor, offset):
        key_block, value_block = pieces
        allowed = allowed_pairs(anchor, key_block.shape[0])

        def compute(softmax_state):
            row_top, row_total, weighted = softmax_state
            scores = jnp.where(allowed, raw_scores(key_block), NEG_FILL)
            top_new = jnp.maximum(row_top, jnp.max(scores, axis=-1))
            shrink = jnp.exp(row_top - top_new)
            prob_tile = jnp.where(allowed, jnp.exp(scores - top_new[..., None]), 0.0)
            row_total = row_total * shrink + jnp.sum(prob_tile, axis=-1)
            weighted = weighted * shrink[..., None] + jnp.einsum(
                "gjts,sgd->gjtd", prob_tile, value_block.astype(jnp.float32), precision=highest
            )
            return (top_new, row_total, weighted)

        return guarded(compute, running)

    state_init = (
        jnp.full((kv_here, group_width, tok_rows), NEG_FILL, jnp.float32),
        jnp.zeros((kv_here, group_width, tok_rows), jnp.float32),
        jnp.zeros((kv_here, group_width, tok_rows, head_dim), jnp.float32),
    )
    softmax_state = by_blocks(
        forward_step,
        state_init,
        (
            lax.all_gather(key_states, "ctx", axis=0, tiled=True),
            lax.all_gather(value_vectors, "ctx", axis=0, tiled=True),
        ),
    )
    row_top, row_total, weighted = softmax_state
    log_total = row_top + jnp.log(row_total)
    attention = weighted / row_total[..., None]
    grad_rows = lax.all_gather(grad_output, "tp", axis=0, tiled=True)
    out_grad = jnp.dot(
        grad_rows,
        lax.all_gather(out_weight, "ctx", axis=0, tiled=True),
        preferred_element_type=jnp.float32,
    )
    out_grad = out_grad.astype(jnp.bfloat16)
    out_grad = out_grad.reshape(tok_rows, kv_here, group_width, head_dim)
    row_delta = jnp.einsum(
        "tgjd,gjtd->gjt", out_grad.astype(jnp.float32), attention, precision=highest
    )

    def tile_grads(dq_sum, key_block, value_block, allowed):
        scores = raw_scores(key_block)
        prob_tile = jnp.where(allowed, jnp.exp(scores - log_total[..., None]), 0.0)
        value_portion = jnp.einsum(
            "gjts,tgjd->sgd",
            prob_tile.astype(jnp.bfloat16),
            out_grad,
            preferred_element_type=jnp.float32,
        )
        prob_grads = jnp.einsum(
            "tgjd,sgd->gjts", out_grad, value_block, preferred_element_type=jnp.float32
        )
        score_grads = (prob_tile * (prob_grads - row_delta[..., None])).astype(jnp.bfloat16)
        dq_sum = (
            dq_sum
            + jnp.einsum(
                "gjts,sgd->tgjd", score_grads, key_block, preferred_element_type=jnp.float32
            )
            * score_scale
        )
        key_portion = (
            jnp.einsum(
                "gjts,tgjd->sgd", score_grads, query_four, preferred_element_type=jnp.float32
            )
            * score_scale
        )
        return (dq_sum, key_portion, value_portion)

    def make_backward():

        def backward_step(running, pieces, anchor, offset):
            key_block, value_block = pieces
            allowed = allowed_pairs(anchor, key_block.shape[0])
            position = anchor

            def compute(grad_state):
                dq_sum, key_acc, value_acc = grad_state
                dq_sum, key_portion, value_portion = tile_grads(
                    dq_sum, key_block, value_block, allowed
                )
                return (
                    dq_sum,
                    add_at(key_acc, key_portion, position),
                    add_at(value_acc, value_portion, position),
                )

            return guarded(compute, running)

        return backward_step

    global_step = make_backward()
    dq_init = jnp.zeros((tok_rows, kv_here, group_width, head_dim), jnp.float32)
    whole_zero = jnp.zeros((ctx_count * tok_rows, kv_here, head_dim), jnp.float32)
    dq_sum, key_acc, value_acc = by_blocks(
        global_step,
        (dq_init, whole_zero, whole_zero),
        (
            lax.all_gather(key_states, "ctx", axis=0, tiled=True),
            lax.all_gather(value_vectors, "ctx", axis=0, tiled=True),
        ),
    )
    key_mine, value_mine = (
        lax.psum_scatter(
            key_acc.astype(jnp.bfloat16), "ctx", scatter_dimension=0, tiled=True
        ).astype(jnp.float32),
        lax.psum_scatter(
            value_acc.astype(jnp.bfloat16), "ctx", scatter_dimension=0, tiled=True
        ).astype(jnp.float32),
    )
    query_grads = dq_sum.astype(jnp.bfloat16).reshape(tok_rows, heads_here, head_dim)
    key_low = key_mine.astype(jnp.bfloat16)
    value_low = value_mine.astype(jnp.bfloat16)
    return (query_grads, key_low, value_low)


def solution(mesh):
    return jax.shard_map(
        local,
        mesh=mesh,
        in_specs=(
            P("ctx", "tp", None),
            P("ctx", "tp", None),
            P("ctx", "tp", None),
            P(("ctx", "tp"), None),
            P("ctx", "tp"),
            P(),
        ),
        out_specs=(P("ctx", "tp", None), P("ctx", "tp", None), P("ctx", "tp", None)),
        check_vma=False,
    )
```

profile of v0, /device:TPU:2, one launch (start us, length us, event | category | flops | bytes accessed | tf_op | source)
XLA Modules:
  0.0 727.0 jit_solution(6197451220977778954)
XLA Ops:
  12.0 64.5 %all-gather.5.cloned.1.call-done = bf16[4096,1,128]{2,0,1:T(8,128)(2,1)} async-done(((bf16[128,1,128]{2,0,1:T(8,128)(2,1)}), bf16[4096,1,128]{2,0,1:T(8,128)(2,1)}) %all-gather.5.cloned.1.call-update) | async-done | bytes 1048592 | tf_op jit(solution)/shard_map/all_gather | solution.py:167
  76.5 65.2 %all-gather.7.cloned.1.call-done = bf16[4096,1,128]{2,0,1:T(8,128)(2,1)} async-done(((bf16[128,1,128]{2,0,1:T(8,128)(2,1)}), bf16[4096,1,128]{2,0,1:T(8,128)(2,1)}) %all-gather.7.cloned.1.call-update) | async-done | bytes 1048592 | tf_op jit(solution)/shard_map/all_gather | solution.py:168
  141.6 92.7 %while.36 = (s32[]{:T(128)}, f32[1,8,128]{2,1,0:T(8,128)S(1)}, f32[1,8,128]{2,1,0:T(8,128)S(1)}, f32[1,8,128,128]{3,2,1,0:T(8,128)S(1)}, s32[128]{0:T(128)S(1)},...) while((s32[]{:T(128)}, f32[1,8,128]{2,1,0:T(8,128)S(1)}, ...), condition=%wide.region_6.7_spmd.clone, body=%wide.region_2.6_spmd.clone.sunk | while | flops 236397952 | bytes 3084795 | solution.py:27
  143.0 1.5 fusion.85
  145.9 1.5 fusion.85
  148.8 1.5 fusion.85
  151.7 1.5 fusion.85
  154.6 1.5 fusion.85
  157.5 1.5 fusion.85
  160.4 1.5 fusion.85
  163.3 1.5 fusion.85
  166.2 1.5 fusion.85
  169.1 1.5 fusion.85
  172.0 1.5 fusion.85
  174.9 1.5 fusion.85
  177.8 1.5 fusion.85
  180.7 1.5 fusion.85
  183.6 1.5 fusion.85
  186.5 1.5 fusion.85
  189.4 1.5 fusion.85
  192.3 1.5 fusion.85
  195.2 1.5 fusion.85
  198.1 1.5 fusion.85
  221.2 1.5 fusion.85
  224.1 1.5 fusion.85
  234.4 70.2 %all-gather.11.cloned.1.call-done = bf16[8192,1024]{1,0:T(8,128)(2,1)} async-done(((bf16[256,1024]{1,0:T(8,128)(2,1)}), bf16[8192,1024]{1,0:T(8,128)(2,1)}) %all-gather.11.cloned.1.call-update) | async-done | bytes 16777232 | tf_op jit(solution)/shard_map/all_gather | solution.py:101
  304.6 8.7 %fusion.52 = bf16[16,8,8,128]{3,1,2,0:T(8,128)(2,1)S(1)} fusion(bf16[128,8192]{1,0:T(8,128)(2,1)} %all-gather.9.cloned.1.call-done, bf16[8192,1024]{1,0:T(8,128)(2,1)} %all-gather.11.cloned.1.call-done), kind=kOutput, calls=%fused_computation.74 | convolution fusion | flops 2147614720 | bytes 19136512 | tf_op jit(solution)/shard_map/dot_general | solution.py:99
  314.1 1.5 broadcast_in_dim.107
  315.6 168.3 %while.37 = (s32[]{:T(128)}, f32[128,1,8,128]{0,3,2,1:T(8,128)S(1)}, f32[4096,1,128]{2,0,1:T(8,128)}, f32[4096,1,128]{2,0,1:T(8,128)S(1)}, bf16[4096,1,128]{2,0,...) while((s32[]{:T(128)}, ...), condition=%wide.region_9.10_spmd.clone, body=%wide.region_7.9_spmd.clone.sunk | while | flops 169201024 | bytes 4862493 | solution.py:27
  319.1 1.7 fusion.99
  324.4 1.7 fusion.99
  329.6 1.7 fusion.99
  334.9 1.7 fusion.99
  340.1 1.7 fusion.99
  345.4 1.7 fusion.99
  350.7 1.7 fusion.99
  355.9 1.7 fusion.99
  361.2 1.7 fusion.99
  366.5 1.7 fusion.99
  371.7 1.7 fusion.99
  377.0 1.7 fusion.99
  382.2 1.7 fusion.99
  387.5 1.7 fusion.99
  392.7 1.7 fusion.99
  398.0 1.7 fusion.99
  403.3 1.7 fusion.99
  408.5 1.7 fusion.99
  413.8 1.7 fusion.99
  419.1 1.7 fusion.99
  424.3 1.7 fusion.99
  429.6 1.7 fusion.99
  434.8 1.7 fusion.99
  440.1 1.7 fusion.99
  445.4 1.7 fusion.99
  450.6 1.7 fusion.99
  455.9 1.7 fusion.99
  461.1 1.7 fusion.99
  466.4 1.7 fusion.99
  471.6 1.7 fusion.99
  476.9 1.7 fusion.99
  482.2 1.7 fusion.99
  485.0 2.7 convert_element_type.54
  488.6 113.6 %reduce-scatter.5.cloned.1.call-done = bf16[128,1,128]{2,0,1:T(8,128)(2,1)} async-done(((bf16[4096,1,128]{2,0,1:T(8,128)(2,1)}), bf16[128,1,128]{2,0,1:T(8,128)(2,1)}) %reduce-scatter.5.cloned.1.call-update) | async-done | bytes 32784 | tf_op jit(solution)/shard_map/reduce_scatter | solution.py:175
  602.2 117.9 %reduce-scatter.3.cloned.1.call-done = bf16[128,1,128]{2,0,1:T(8,128)(2,1)} async-done(((bf16[4096,1,128]{2,0,1:T(8,128)(2,1)}), bf16[128,1,128]{2,0,1:T(8,128)(2,1)}) %reduce-scatter.3.cloned.1.call-update) | async-done | bytes 32784 | tf_op jit(solution)/shard_map/reduce_scatter | solution.py:172
  (583 shorter events, 178.4 us)
Async XLA Ops:
  7.2 69.3 %all-gather.5.cloned.1.call-start = ((), (), s32[]{:S(2)}) async-start(), calls=%async_computation.2 | async-start | bytes 1081344 | tf_op jit(solution)/shard_map/all_gather | solution.py:167
  7.9 133.7 %all-gather.7.cloned.1.call-start = ((), (), s32[]{:S(2)}) async-start(), calls=%async_computation.3 | async-start | bytes 1081344 | tf_op jit(solution)/shard_map/all_gather | solution.py:168
  8.6 225.7 %all-gather.9.cloned.1.call-start = ((), (), s32[]{:S(2)}) async-start(), calls=%async_computation.4 | async-start | bytes 2359296 | tf_op jit(solution)/shard_map/all_gather | solution.py:98
  9.4 295.3 %all-gather.11.cloned.1.call-start = ((), (), s32[]{:S(2)}) async-start(), calls=%async_computation.5 | async-start | bytes 17301504 | tf_op jit(solution)/shard_map/all_gather | solution.py:101
  10.0 592.3 %reduce-scatter.5.cloned.1.call-start = ((), (), s32[]{:S(2)}) async-start(), calls=%async_computation.7 | async-start | bytes 1081344 | tf_op jit(solution)/shard_map/reduce_scatter | solution.py:175
  485.0 235.2 %reduce-scatter.3.cloned.1.call-start = ((), (), s32[]{:S(2)}) async-start(), calls=%async_computation.6 | async-start | bytes 1081344 | tf_op jit(solution)/shard_map/reduce_scatter | solution.py:172
Sparse Core Ops, SparseCore 0:
  9.9 66.5 all-gather.4
  78.3 63.2 all-gather.6
  144.3 59.6 all-gather.8
  205.7 98.9 all-gather.10
  485.1 117.0 reduce-scatter.4
  605.3 114.8 reduce-scatter.2
where the time goes:
time: 740 us; the launch traced here: 727 us
  waiting for transfers between devices  434 us (59%)
  matrix products  248 us (34%)
  other arithmetic  22.9 us (3%)
  between operations  14.2 us (2%)
    reduce_scatter x1, waiting for transfers between devices, local(): lax.psum_scatter(key_acc.astype(jnp.bfloat16), 'ctx', scatter_dimension=0...  118 us
    reduce_scatter x1, waiting for transfers between devices, local(): lax.psum_scatter(value_acc.astype(jnp.bfloat16), 'ctx', scatter_dimension...  114 us
    all_gather x1, waiting for transfers between devices, local(): lax.all_gather(out_weight, 'ctx', axis=0, tiled=True)  70.2 us
    all_gather x1, waiting for transfers between devices, local(): lax.all_gather(value_vectors, 'ctx', axis=0, tiled=True)  65.2 us
    dot_general x64, matrix products, raw_scores(): jnp.einsum('tgjd,sgd->gjts', query_four, key_block, preferred_element_typ...  64.7 us
    all_gather x1, waiting for transfers between devices, local(): lax.all_gather(key_states, 'ctx', axis=0, tiled=True)  64.5 us
    dot_general x32, matrix products, tile_grads(): jnp.einsum('gjts,tgjd->sgd', score_grads, query_four, preferred_element_t...  54 us
    dot_general x32, matrix products, compute(): jnp.einsum('gjts,sgd->gjtd', prob_tile, value_block.astype(jnp.float32),...  47.2 us
  transfers between devices with their start and end apart: 6, of which 5 were waited for; matrix products, arithmetic and copies ran while one was open for 13% of the time, Pallas kernels for 0%

commit v1 on v0

v1 whole, which is shorter than its diff:
```python
import math

import jax
import jax.numpy as jnp
from jax import lax
from jax.experimental import pallas as pl
from jax.experimental.pallas import tpu as pltpu
from jax.sharding import Mesh, PartitionSpec as P

BF = jnp.bfloat16
F32 = jnp.float32
NEG = -1e30
HD = 128
SCALE = HD**-0.5
C2 = SCALE * math.log2(math.e)
PLANE = 512
PLANES = 6
ROWS = 1024
CHUNK = 256
VMEM = 58 * 1024 * 1024

NT = (((1,), (1,)), ((), ()))
NN = (((1,), (0,)), ((), ()))
TN = (((0,), (0,)), ((), ()))


def dot(a, b, dims):
    return lax.dot_general(a, b, dims, preferred_element_type=F32)


def key_positions(z, d):
    r = lax.broadcasted_iota(jnp.int32, (PLANE, 1), 0)
    part = r >> 7
    block = ((part & 1) << 1) | (part >> 1)
    return (z - d) * PLANE + block * 128 + (r & 127)


def project_kernel(s_ref, gh, gu, gd, gu2, gd2, w0, w1, w2, w3, w4, w5, w6, w7, send, keep, a_scr):
    me = s_ref[0]
    for rel in range(4):
        src = pl.multiple_of((me ^ rel) * 16, 16)
        for half in range(2):
            base = pl.multiple_of(src + half * 64, 16)
            for relx, ref, at in (
                (0, gh, base),
                (1, gd, base),
                (2, (gu2, gd2)[half], src),
                (3, gu, base),
            ):
                row = rel * 128 + (relx * 2 + half) * 16
                a_scr[row : row + 16, :] = ref[pl.ds(at, 16), :]
    ws = (w0, w1, w2, w3, w4, w5, w6, w7)
    for n in range(4):
        cols = slice(n * 256, n * 256 + 256)
        total = None
        for k in range(8):
            part = dot(a_scr[:, k * 256 : k * 256 + 256], ws[k][:, cols], NN)
            total = part if total is None else total + part
        keep[0, :, cols] = total[0:128]
        send[0, :, cols] = total[128:256].astype(BF)
        keep[1, :, cols] = total[256:384]
        send[1, :, cols] = total[384:512].astype(BF)


def forward_kernel(s_ref, q, kv, start, att, lse, m_scr, l_scr):
    z, count, pos0 = s_ref[0], s_ref[1], s_ref[2]
    m_scr[...] = jnp.full((1, ROWS), NEG, F32)
    l_scr[...] = jnp.zeros((1, ROWS), F32)
    att[...] = jnp.zeros((HD, ROWS), F32)

    def plane(d, carry):
        keys = key_positions(z, d)
        k = kv[d, :, 0:HD]
        v = kv[d, :, HD : 2 * HD]
        for n in range(ROWS // CHUNK):
            cols = slice(n * CHUNK, n * CHUNK + CHUNK)
            row_pos = pos0 + (lax.broadcasted_iota(jnp.int32, (1, CHUNK), 1) & 127)
            s = dot(k, q[cols, :], NT) * C2
            ok = (keys >= start[:, cols]) & (keys <= row_pos)
            s = jnp.where(ok, s, NEG)
            old = m_scr[:, cols]
            new = jnp.maximum(old, jnp.max(s, axis=0, keepdims=True))
            shrink = jnp.exp2(old - new)
            p = jnp.exp2(s - new)
            l_scr[:, cols] = l_scr[:, cols] * shrink + jnp.sum(p, axis=0, keepdims=True)
            m_scr[:, cols] = new
            att[:, cols] = att[:, cols] * shrink + dot(v, p.astype(BF), TN)
        return carry

    lax.fori_loop(0, count, plane, 0)
    lse[...] = m_scr[...] + jnp.log2(l_scr[...])
    att[...] = att[...] / l_scr[...]


def backward_kernel(
    s_ref, q, o, att, lse, kv, start, dq, keep, send, do_scr, delta, dq_scr, dk_scr, dv_scr
):
    z, count, pos0, c, x, yh = (s_ref[i] for i in range(6))
    for rel in range(8):
        tp = ((x + rel // 2) & 3) * 2 + (yh ^ (rel & 1))
        for h in range(8):
            at = pl.multiple_of(h * 128 + tp * 16, 16)
            do_scr[pl.ds(at, 16), :] = o[rel * 16 : rel * 16 + 16, h * HD : h * HD + HD]
    for h in range(8):
        cols = slice(h * 128, h * 128 + 128)
        do_t = do_scr[cols, :].astype(F32).T
        delta[:, cols] = jnp.sum(do_t * att[:, cols], axis=0, keepdims=True)
    dq_scr[...] = jnp.zeros((HD, ROWS), F32)

    def store(d, value):
        group = jnp.where((d >= 1) & (d <= 3), 0, 1)
        slot = jnp.where(d == 0, 2, jnp.where(d <= 3, d - 1, d - 4))

        @pl.when(group == c)
        def _():
            keep[slot] = value()

        @pl.when(group != c)
        def _():
            send[slot] = value()

    def plane(d, carry):
        keys = key_positions(z, d)
        k = kv[d, :, 0:HD]
        v = kv[d, :, HD : 2 * HD]
        k_t = k.astype(F32).T.astype(BF)
        for n in range(ROWS // CHUNK):
            cols = slice(n * CHUNK, n * CHUNK + CHUNK)
            row_pos = pos0 + (lax.broadcasted_iota(jnp.int32, (1, CHUNK), 1) & 127)
            qn = q[cols, :]
            don = do_scr[cols, :]
            s = dot(k, qn, NT) * C2 - lse[:, cols]
            ok = (keys >= start[:, cols]) & (keys <= row_pos)
            p = jnp.where(ok, jnp.exp2(s), 0.0)
            dv = dot(p.astype(BF), don, NN)
            dp = dot(v, don, NT)
            ds = (p * (dp - delta[:, cols])).astype(BF)
            dk = dot(ds, qn, NN)
            dq_scr[:, cols] += dot(k_t, ds, NN)
            if n == 0:
                dk_scr[...] = dk
                dv_scr[...] = dv
            else:
                dk_scr[...] += dk
                dv_scr[...] += dv
        store(d, lambda: jnp.concatenate([dk_scr[...] * SCALE, dv_scr[...]], axis=1).astype(BF))
        return carry

    lax.fori_loop(0, count, plane, 0)

    def blank(d, carry):
        store(d, lambda: jnp.zeros((PLANE, 2 * HD), BF))
        return carry

    lax.fori_loop(count, PLANES, blank, 0)
    for h in range(8):
        cols = slice(h * 128, h * 128 + 128)
        dq[:, cols] = (dq_scr[:, cols] * SCALE).T.astype(BF)


def in_vmem(n):
    return [pl.BlockSpec(memory_space=pltpu.SMEM)] + [pl.BlockSpec(memory_space=pltpu.VMEM)] * n


def call(kernel, n_in, outs, scratch, flops):
    return pl.pallas_call(
        kernel,
        out_shape=outs,
        in_specs=in_vmem(n_in),
        out_specs=[pl.BlockSpec(memory_space=pltpu.VMEM)] * len(outs),
        scratch_shapes=scratch,
        compiler_params=pltpu.CompilerParams(vmem_limit_bytes=VMEM),
        cost_estimate=pl.CostEstimate(flops=flops, bytes_accessed=6 << 20, transcendentals=0),
    )


def shape(dims, dtype):
    return jax.ShapeDtypeStruct(dims, dtype)


def swap(x, axis):
    return lax.ppermute(x, axis, [(0, 1), (1, 0)])


def turn(x, step):
    return lax.ppermute(x, "x", [(i, (i + step) % 4) for i in range(4)])


def along_z(x, step0, step1):
    pairs = [(2 * z, 2 * ((z + step0) % 8)) for z in range(8)]
    if step1 is not None:
        pairs += [(2 * z + 1, 2 * ((z + step1) % 8) + 1) for z in range(8)]
    return lax.ppermute(x, ("z", "c"), pairs)


def add(a, b):
    return a.astype(F32) + b.astype(F32)


def local(queries, key_states, value_vectors, grad_output, out_weight, doc_lengths):
    z, yl, c = lax.axis_index("z"), lax.axis_index("yl"), lax.axis_index("c")
    x, yh = lax.axis_index("x"), lax.axis_index("yh")
    first = c == 0
    pos0 = ((z * 2 + yl) * 2 + c) * 128

    kv = jnp.concatenate([key_states.reshape(128, HD), value_vectors.reshape(128, HD)], axis=1)
    other = swap(kv, "yl")
    half = jnp.where(yl == 0, jnp.concatenate([kv, other]), jnp.concatenate([other, kv]))
    other = swap(half, "c")
    plane = jnp.where(first, jnp.concatenate([half, other]), jnp.concatenate([other, half]))

    own, mate = out_weight, swap(out_weight, "c")
    weights = [own]
    w_own, w_mate, kv_step = own, mate, plane
    kv_got = []
    for step in range(3):
        w_own = along_z(w_own, 1, 7)
        w_mate = along_z(w_mate, 1, 7)
        weights += [w_own, w_mate]
        kv_step = along_z(kv_step, 1, (5, 7, None)[step])
        kv_got.append(kv_step)
    weights.append(along_z(w_own, 1, 7))

    rolled = lax.dynamic_slice(
        jnp.concatenate([grad_output, grad_output], axis=1), (0, z * 1024), (16, 8192)
    )

    def columns(to_yl, to_c):
        order = [(0, to_c)]
        for s in (1, 2, 3):
            far = s if to_c else 8 - s
            order += [(far, to_c), (far, 1 - to_c)]
        order.append((4, to_c))
        return jnp.concatenate(
            [rolled[:, s * 1024 + to_yl * 512 + par * 256 :][:, :256] for s, par in order], axis=1
        )

    sent = jnp.concatenate([columns(a, b) for a in (0, 1) for b in (0, 1)])
    got = lax.all_to_all(sent, ("yl", "c"), 0, 0, tiled=True)
    gh = jnp.concatenate([got, swap(got, "yh")])
    gu, gd = turn(gh, 1), turn(gh, 3)
    gu2, gd2 = turn(gu[:64], 1), turn(gd[64:], 3)

    me = jnp.stack([yl * 2 + c]).astype(jnp.int32)
    send, keep = call(
        project_kernel,
        13,
        [shape((2, 128, 1024), BF), shape((2, 128, 1024), F32)],
        [pltpu.VMEM((512, 2048), BF)],
        2 * 512 * 2048 * 1024,
    )(me, gh, gu, gd, gu2, gd2, *weights)
    both = keep + swap(send, "c").astype(F32)
    out_grad = (both[0] + swap(both[1].astype(BF), "yl").astype(F32)).astype(BF)

    ends = jnp.cumsum(doc_lengths)
    row_pos = pos0 + jnp.arange(128, dtype=jnp.int32)
    start = jnp.max(jnp.where(ends[None, :] <= row_pos[:, None], ends[None, :], 0), axis=1)
    count = z - start[0] // PLANE + 1
    starts = jnp.tile(start, 8).reshape(1, ROWS)
    scalars = jnp.stack([z, count, pos0, c, x, yh]).astype(jnp.int32)

    mine = jnp.stack(kv_got)
    theirs = swap(mine, "c")
    planes = jnp.concatenate(
        [
            plane[None],
            jnp.where(first, mine, theirs),
            jnp.where(first, theirs, mine)[1::-1],
        ]
    )
    q = queries.transpose(1, 0, 2).reshape(ROWS, HD)
    att, lse = call(
        forward_kernel,
        3,
        [shape((HD, ROWS), F32), shape((1, ROWS), F32)],
        [pltpu.VMEM((1, ROWS), F32)] * 2,
        4 * 1024 * 2560 * 128,
    )(scalars, q, planes, starts)

    dq, keep, send = call(
        backward_kernel,
        6,
        [shape((128, 1024), BF), shape((3, PLANE, 2 * HD), BF), shape((3, PLANE, 2 * HD), BF)],
        [
            pltpu.VMEM((ROWS, HD), BF),
            pltpu.VMEM((1, ROWS), F32),
            pltpu.VMEM((HD, ROWS), F32),
            pltpu.VMEM((PLANE, HD), F32),
            pltpu.VMEM((PLANE, HD), F32),
        ],
        10 * 1024 * 2560 * 128,
    )(scalars, q, out_grad, att, lse, planes, starts)

    terms = add(keep, swap(send, "c")).astype(BF)
    run = along_z(jnp.where(first, terms[2], terms[0]), 7, 1)
    run = along_z(add(run, terms[1]).astype(BF), 7, 3)
    run = add(run, jnp.where(first, terms[0], terms[2])).astype(BF)
    last = along_z(run, 7, None)
    run = jnp.where(first, last, run)
    total = add(
        jnp.where(first, run[:256], run[256:]),
        swap(jnp.where(first, run[256:], run[:256]), "c"),
    )
    there = swap(jnp.where(yl == 0, total[128:], total[:128]).astype(BF), "yl")
    kv_grad = (jnp.where(yl == 0, total[:128], total[128:]) + there.astype(F32)).astype(BF)
    return (
        dq.reshape(128, 8, HD),
        kv_grad[:, :HD].reshape(128, 1, HD),
        kv_grad[:, HD:].reshape(128, 1, HD),
    )


def solution(mesh):
    grid = Mesh(mesh.devices.reshape(8, 2, 2, 4, 2), ("z", "yl", "c", "x", "yh"))
    ctx, tp = ("z", "yl", "c"), ("x", "yh")
    return jax.shard_map(
        local,
        mesh=grid,
        in_specs=(
            P(ctx, tp, None),
            P(ctx, tp, None),
            P(ctx, tp, None),
            P(ctx + tp, None),
            P(ctx, tp),
            P(),
        ),
        out_specs=(P(ctx, tp, None), P(ctx, tp, None), P(ctx, tp, None)),
        check_vma=False,
    )
```

time: 740 us -> 144 us (0.19)
  the two profiles are of different devices: /device:TPU:2 before, /device:TPU:1 now
where the time goes in v1:
time: 144 us; the launch traced here: 143 us
  waiting for transfers between devices  62.7 us (44%)
  starting transfers between devices  47.3 us (33%)
  Pallas kernels  15.6 us (11%)
  other arithmetic  10.4 us (7%)
  local copies, waits for them, and re-layouts  5.93 us (4%)
    ppermute x13, waiting for transfers between devices, along_z(): return lax.ppermute(x, ('z', 'c'), pairs)  50.6 us
    ppermute x13, starting transfers between devices, along_z(): return lax.ppermute(x, ('z', 'c'), pairs)  26.2 us
    ppermute x10, starting transfers between devices, swap(): return lax.ppermute(x, axis, [(0, 1), (1, 0)])  11.7 us
    ppermute x10, waiting for transfers between devices, swap(): return lax.ppermute(x, axis, [(0, 1), (1, 0)])  8.57 us
    pallas_call x1, Pallas kernels, local(): call(project_kernel, 13, [shape((2, 128, 1024), BF), shape((2, 128, 1024)...  6.24 us
    ppermute x4, starting transfers between devices, turn(): return lax.ppermute(x, 'x', [(i, (i + step) % 4) for i in range(4)])  6.09 us
    pallas_call x1, Pallas kernels, local(): call(backward_kernel, 6, [shape((128, 1024), BF), shape((3, PLANE, 2 * HD...  5.24 us
    pallas_call x1, Pallas kernels, local(): call(forward_kernel, 3, [shape((HD, ROWS), F32), shape((1, ROWS), F32)],...  4.09 us
  transfers between devices with their start and end apart: 28, of which 15 were waited for; matrix products, arithmetic and copies ran while one was open for 7% of the time, Pallas kernels for 7%

profile of v1, /device:TPU:1, one launch (start us, length us, event | category | flops | bytes accessed | tf_op | source)
XLA Modules:
  0.0 143.1 jit_solution(5493110665401275379)
XLA Ops:
  0.6 6.5 %collective-permute-start.5 = (bf16[256,1024]{1,0:T(8,128)(2,1)}, bf16[256,1024]{1,0:T(8,128)(2,1)S(1)}, u32[]{:S(2)}, u32[]{:S(2)}) collective-permute-start(bf16[256,1024]{1,0:T(8,128)(2,1)} %w0.1), channel_id=1, source_target_pairs={{0,32},{32,64},{64,96},{96,128},{128,160},{160,192},{192,224},{224... | collective-permute-start | bytes 1572872 | tf_op jit(solution)/shard_map/ppermute | solution.py:193
  7.1 0.8 pad_maximum_fusion.4
  7.9 1.4 collective-permute-start.15
  9.3 1.1 fusion.4
  10.5 0.9 collective-permute-done.15
  11.4 0.9 maximum_select_fusion.2
  12.3 1.4 %collective-permute-start.16 = (bf16[256,256]{1,0:T(8,128)(2,1)S(1)}, bf16[256,256]{1,0:T(8,128)(2,1)S(1)}, u32[]{:S(2)}, u32[]{:S(2)}) collective-permute-start(bf16[256,256]{1,0:T(8,128)(2,1)S(1)} %maximum_select_fusion.2), channel_id=1, source_target_pairs={{0,8},{8,0},{1,9},{9,1},{2,10},{10,2},{3,11},{11,3},{4,12},{12,4},... | collective-permute-start | bytes 393224 | tf_op jit(solution)/shard_map/ppermute | solution.py:182
  13.7 1.0 collective-permute-done.16
  14.7 0.1 maximum_select_fusion.1
  14.8 2.4 %collective-permute-start.17 = (bf16[512,256]{1,0:T(8,128)(2,1)S(1)}, bf16[512,256]{1,0:T(8,128)(2,1)S(1)}, u32[]{:S(2)}, u32[]{:S(2)}) collective-permute-start(bf16[512,256]{1,0:T(8,128)(2,1)S(1)} %maximum_select_fusion.1), channel_id=1, source_target_pairs={{0,32},{32,64},{64,96},{96,128},{128,160},{160,192},{192,224},{224... | collective-permute-start | bytes 786440 | tf_op jit(solution)/shard_map/ppermute | solution.py:193
  17.2 0.7 collective-permute-start.7
  17.9 1.9 %collective-permute-start.8 = (bf16[256,1024]{1,0:T(8,128)(2,1)S(1)}, bf16[256,1024]{1,0:T(8,128)(2,1)}, u32[]{:S(2)}, u32[]{:S(2)}) collective-permute-start(bf16[256,1024]{1,0:T(8,128)(2,1)S(1)} %collective-permute-done.5.w1), channel_id=1, source_target_pairs={{0,32},{32,64},{64,96},{96,128},{128,160},{160,192},{192,224},{224... | collective-permute-start | bytes 1572872 | tf_op jit(solution)/shard_map/ppermute | solution.py:193
  19.9 0.7 pad_maximum_fusion.3
  20.6 3.4 %all-to-all-start = ((bf16[4,16,2048]{2,1,0:T(8,128)(2,1)}), bf16[4,16,2048]{2,1,0:T(8,128)(2,1)S(1)}, u32[]{:S(2)}, u32[]{:S(2)}) async-start(bf16[4,16,2048]{2,1,0:T(8,128)(2,1)} %bitcast.12), calls=%async_computation | async-start | bytes 524288 | tf_op jit(solution)/shard_map/all_to_all | solution.py:239
  24.0 2.8 %collective-permute-done.17 = bf16[512,256]{1,0:T(8,128)(2,1)S(1)} collective-permute-done((bf16[512,256]{1,0:T(8,128)(2,1)S(1)}, bf16[512,256]{1,0:T(8,128)(2,1)S(1)}, u32[]{:S(2)}, u32[]{:S(2)}) %collective-permute-start.17) | collective-permute-done | bytes 262176 | tf_op jit(solution)/shard_map/ppermute | solution.py:193
  26.8 2.8 %collective-permute-start.18 = (bf16[512,256]{1,0:T(8,128)(2,1)S(1)}, bf16[512,256]{1,0:T(8,128)(2,1)S(1)}, u32[]{:S(2)}, u32[]{:S(2)}) collective-permute-start(bf16[512,256]{1,0:T(8,128)(2,1)S(1)} %collective-permute-done.17), channel_id=1, source_target_pairs={{0,32},{32,64},{64,96},{96,128},{128,160},{160,192},{192,224},{224... | collective-permute-start | bytes 786440 | tf_op jit(solution)/shard_map/ppermute | solution.py:193
  29.6 2.9 %collective-permute-start = (bf16[64,2048]{1,0:T(8,128)(2,1)S(1)}, bf16[64,2048]{1,0:T(8,128)(2,1)S(1)}, u32[]{:S(2)}, u32[]{:S(2)}) collective-permute-start(bf16[64,2048]{1,0:T(8,128)(2,1)S(1)} %bitcast.54), channel_id=1, source_target_pairs={{0,1},{1,0},{2,3},{3,2},{4,5},{5,4},{6,7},{7,6},{8,9},{9,8},{10,11... | collective-permute-start | bytes 786440 | tf_op jit(solution)/shard_map/ppermute | solution.py:182
  32.5 8.8 %collective-permute-done.18 = bf16[512,256]{1,0:T(8,128)(2,1)S(1)} collective-permute-done((bf16[512,256]{1,0:T(8,128)(2,1)S(1)}, bf16[512,256]{1,0:T(8,128)(2,1)S(1)}, u32[]{:S(2)}, u32[]{:S(2)}) %collective-permute-start.18) | collective-permute-done | bytes 262176 | tf_op jit(solution)/shard_map/ppermute | solution.py:193
  41.3 0.7 collective-permute-start.19
  42.0 2.0 %collective-permute-start.9 = (bf16[256,1024]{1,0:T(8,128)(2,1)}, bf16[256,1024]{1,0:T(8,128)(2,1)}, u32[]{:S(2)}, u32[]{:S(2)}) collective-permute-start(bf16[256,1024]{1,0:T(8,128)(2,1)} %collective-permute-done.7.w2), channel_id=1, source_target_pairs={{0,32},{32,64},{64,96},{96,128},{128,160},{160,192},{192,224},{224... | collective-permute-start | bytes 1572872 | tf_op jit(solution)/shard_map/ppermute | solution.py:193
  44.1 0.1 collective-permute-start.10
  44.3 1.3 collective-permute-start.1
  45.5 1.5 %collective-permute-start.2 = (bf16[128,2048]{1,0:T(8,128)(2,1)S(1)}, bf16[128,2048]{1,0:T(8,128)(2,1)}, u32[]{:S(2)}, u32[]{:S(2)}) collective-permute-start(bf16[128,2048]{1,0:T(8,128)(2,1)S(1)} %pad_maximum_fusion.2.gh), channel_id=1, source_target_pairs={{0,6},{2,0},{4,2},{6,4},{1,7},{3,1},{5,3},{7,5},{8,14},{10,8},{12,... | collective-permute-start | bytes 1572872 | tf_op jit(solution)/shard_map/ppermute | solution.py:186
  47.0 0.7 copy-done.3
  47.8 0.1 collective-permute-start.20
  47.9 2.8 %collective-permute-done.9.w4 = bf16[256,1024]{1,0:T(8,128)(2,1)} collective-permute-done((bf16[256,1024]{1,0:T(8,128)(2,1)}, bf16[256,1024]{1,0:T(8,128)(2,1)}, u32[]{:S(2)}, u32[]{:S(2)}) %collective-permute-start.9) | collective-permute-done | bytes 524320 | tf_op jit(solution)/shard_map/ppermute | solution.py:193
  50.7 3.1 %collective-permute-start.11 = (bf16[256,1024]{1,0:T(8,128)(2,1)}, bf16[256,1024]{1,0:T(8,128)(2,1)}, u32[]{:S(2)}, u32[]{:S(2)}) collective-permute-start(bf16[256,1024]{1,0:T(8,128)(2,1)} %collective-permute-done.9.w4), channel_id=1, source_target_pairs={{0,32},{32,64},{64,96},{96,128},{128,160},{160,192},{192,224},{224... | collective-permute-start | bytes 1572872 | tf_op jit(solution)/shard_map/ppermute | solution.py:193
  53.8 2.6 %collective-permute-done.10.w5 = bf16[256,1024]{1,0:T(8,128)(2,1)} collective-permute-done((bf16[256,1024]{1,0:T(8,128)(2,1)}, bf16[256,1024]{1,0:T(8,128)(2,1)}, u32[]{:S(2)}, u32[]{:S(2)}) %collective-permute-start.10) | collective-permute-done | bytes 524320 | tf_op jit(solution)/shard_map/ppermute | solution.py:193
  56.4 2.9 %collective-permute-start.12 = (bf16[256,1024]{1,0:T(8,128)(2,1)}, bf16[256,1024]{1,0:T(8,128)(2,1)}, u32[]{:S(2)}, u32[]{:S(2)}) collective-permute-start(bf16[256,1024]{1,0:T(8,128)(2,1)} %collective-permute-done.10.w5), channel_id=1, source_target_pairs={{0,32},{32,64},{64,96},{96,128},{128,160},{160,192},{192,224},{224... | collective-permute-start | bytes 1572872 | tf_op jit(solution)/shard_map/ppermute | solution.py:193
  59.3 1.5 %collective-permute-start.3 = (bf16[64,2048]{1,0:T(8,128)(2,1)S(1)}, bf16[64,2048]{1,0:T(8,128)(2,1)}, u32[]{:S(2)}, u32[]{:S(2)}) collective-permute-start(bf16[64,2048]{1,0:T(8,128)(2,1)S(1)} %slice.269), channel_id=1, source_target_pairs={{0,2},{2,4},{4,6},{6,0},{1,3},{3,5},{5,7},{7,1},{8,10},{10,12},{12... | collective-permute-start | bytes 786440 | tf_op jit(solution)/shard_map/ppermute | solution.py:186
  60.7 1.0 slice.270
  61.7 1.9 %collective-permute-start.4 = (bf16[64,2048]{1,0:T(8,128)(2,1)S(1)}, bf16[64,2048]{1,0:T(8,128)(2,1)S(1)}, u32[]{:S(2)}, u32[]{:S(2)}) collective-permute-start(bf16[64,2048]{1,0:T(8,128)(2,1)S(1)} %slice.270), channel_id=1, source_target_pairs={{0,6},{2,0},{4,2},{6,4},{1,7},{3,1},{5,3},{7,5},{8,14},{10,8},{12,... | collective-permute-start | bytes 786440 | tf_op jit(solution)/shard_map/ppermute | solution.py:186
  63.6 0.2 reduce-window.8
  64.0 0.7 copy.10
  64.8 0.7 stack.42.s_ref
  65.4 0.1 maximum_select_fusion
  65.5 2.5 %collective-permute-done.3.gu2 = bf16[64,2048]{1,0:T(8,128)(2,1)} collective-permute-done((bf16[64,2048]{1,0:T(8,128)(2,1)S(1)}, bf16[64,2048]{1,0:T(8,128)(2,1)}, u32[]{:S(2)}, u32[]{:S(2)}) %collective-permute-start.3) | collective-permute-done | bytes 262176 | tf_op jit(solution)/shard_map/ppermute | solution.py:186
  68.1 0.9 collective-permute-done.4.gd2
  69.0 0.7 copy-done.9
  69.7 6.2 %shard_map.85 = (bf16[2,128,1024]{2,1,0:T(8,128)(2,1)}, f32[2,128,1024]{2,1,0:T(8,128)}) custom-call(s32[1]{0:T(128)} %bitcast.11.s_ref, bf16[128,2048]{1,0:T(8,128)(2,1)} %copy-done.4, bf16[128,2048]{1,0:T(8,128)(2,1)} %copy-done.7, bf16[128,2048]{1,0:T(8,128)(2,1)} %collective-permute-done.2.gd, bf16[64,2048]{1,0:T(8,128)(2,1)} %collective-permute-done.3.gu2, ...), custom_call_target="tpu_custom_call" | custom-call | flops 2147483648 | bytes 6291456 | tf_op jit(solution)/shard_map/pallas_call | solution.py:245
  76.1 1.3 broadcast_select_fusion
  77.4 0.8 collective-permute-done.13
  78.2 1.2 convert_add_fusion
  79.4 1.4 collective-permute-start.14
  80.8 1.3 pad_maximum_fusion.kv
  82.2 0.6 tile.2
  82.8 4.1 %shard_map.86 = (f32[128,1024]{1,0:T(8,128)}, f32[1,1024]{1,0:T(1,128)}) custom-call(s32[6]{0:T(128)} %stack.42.s_ref, bf16[1024,128]{1,0:T(8,128)(2,1)} %bitcast.58, bf16[6,512,256]{2,1,0:T(8,128)(2,1)} %pad_maximum_fusion.kv, s32[1,1024]{1,0:T(1,128)} %bitcast.66), custom_call_target="tpu_custom_call" | custom-call | flops 1342177280 | bytes 6291456 | tf_op jit(solution)/shard_map/pallas_call | solution.py:272
  86.9 0.4 collective-permute-done.14
  87.3 0.8 fusion.1.o
  88.1 5.2 %shard_map.87 = (bf16[128,1024]{1,0:T(8,128)(2,1)}, bf16[3,512,256]{2,1,0:T(8,128)(2,1)}, bf16[3,512,256]{2,1,0:T(8,128)(2,1)}) custom-call(s32[6]{0:T(128)} %stack.42.s_ref, bf16[1024,128]{1,0:T(8,128)(2,1)} %bitcast.59, bf16[128,1024]{1,0:T(8,128)(2,1)} %fusion.1.o, f32[128,1024]{1,0:T(8,128)} %get-tuple-element.12.att, f32[1,1024]{1,0:T(1,128)} %get-tuple-element.13.lse, ...), custom_call_target="tpu_custom_call" | custom-call | flops 3355443200 | bytes 6291456 | tf_op jit(solution)/shard_map/pallas_call | solution.py:280
  93.3 1.0 collective-permute-start.21
  94.3 2.1 %collective-permute-done.21 = bf16[3,512,256]{2,1,0:T(8,128)(2,1)S(1)} collective-permute-done((bf16[3,512,256]{2,1,0:T(8,128)(2,1)}, bf16[3,512,256]{2,1,0:T(8,128)(2,1)S(1)}, u32[]{:S(2)}, u32[]{:S(2)}) %collective-permute-start.21) | collective-permute-done | bytes 786464 | tf_op jit(solution)/shard_map/ppermute | solution.py:182
  96.4 1.3 add_convert_fusion
  97.7 2.3 %collective-permute-start.22 = (bf16[512,256]{1,0:T(8,128)(2,1)S(1)}, bf16[512,256]{1,0:T(8,128)(2,1)S(1)}, u32[]{:S(2)}, u32[]{:S(2)}) collective-permute-start(bf16[512,256]{1,0:T(8,128)(2,1)S(1)} %select_bitcast_fusion), channel_id=1, source_target_pairs={{0,224},{32,0},{64,32},{96,64},{128,96},{160,128},{192,160},{224,1... | collective-permute-start | bytes 786440 | tf_op jit(solution)/shard_map/ppermute | solution.py:193
  100.1 19.8 %collective-permute-done.22 = bf16[512,256]{1,0:T(8,128)(2,1)S(1)} collective-permute-done((bf16[512,256]{1,0:T(8,128)(2,1)S(1)}, bf16[512,256]{1,0:T(8,128)(2,1)S(1)}, u32[]{:S(2)}, u32[]{:S(2)}) %collective-permute-start.22) | collective-permute-done | bytes 262176 | tf_op jit(solution)/shard_map/ppermute | solution.py:193
  120.1 13.8 %collective-permute-done.23 = bf16[512,256]{1,0:T(8,128)(2,1)S(1)} collective-permute-done((bf16[512,256]{1,0:T(8,128)(2,1)S(1)}, bf16[512,256]{1,0:T(8,128)(2,1)S(1)}, u32[]{:S(2)}, u32[]{:S(2)}) %collective-permute-start.23) | collective-permute-done | bytes 262176 | tf_op jit(solution)/shard_map/ppermute | solution.py:193
  133.9 0.1 fusion.2
  134.0 0.7 collective-permute-start.24
  134.8 3.4 %collective-permute-start.25 = (bf16[256,256]{1,0:T(8,128)(2,1)S(1)}, bf16[256,256]{1,0:T(8,128)(2,1)S(1)}, u32[]{:S(2)}, u32[]{:S(2)}) collective-permute-start(bf16[256,256]{1,0:T(8,128)(2,1)S(1)} %broadcast_select_fusion.2), channel_id=1, source_target_pairs={{0,8},{8,0},{1,9},{9,1},{2,10},{10,2},{3,11},{11,3},{4,12},{12,4},... | collective-permute-start | bytes 393224 | tf_op jit(solution)/shard_map/ppermute | solution.py:182
  138.1 1.0 collective-permute-done.25
  139.2 0.1 collective-permute-start.26
  139.3 0.8 copy.11
  140.1 2.3 %collective-permute-done.26 = bf16[128,256]{1,0:T(8,128)(2,1)S(1)} collective-permute-done((bf16[128,256]{1,0:T(8,128)(2,1)S(1)}, bf16[128,256]{1,0:T(8,128)(2,1)S(1)}, u32[]{:S(2)}, u32[]{:S(2)}) %collective-permute-start.26) | collective-permute-done | bytes 65568 | tf_op jit(solution)/shard_map/ppermute | solution.py:182
  142.4 0.6 slice_bitcast_fusion.2
  (63 shorter events, 0.8 us)
Async XLA Ops:
  0.6 17.3 %collective-permute-start.5 = (bf16[256,1024]{1,0:T(8,128)(2,1)}, bf16[256,1024]{1,0:T(8,128)(2,1)S(1)}, u32[]{:S(2)}, u32[]{:S(2)}) collective-permute-start(bf16[256,1024]{1,0:T(8,128)(2,1)} %w0.1), channel_id=1, source_target_pairs={{0,32},{32,64},{64,96},{96,128},{128,160},{160,192},{192,224},{224... | collective-permute-start | bytes 1572872 | tf_op jit(solution)/shard_map/ppermute | solution.py:193
  7.1 10.1 %collective-permute-start.6 = (bf16[256,1024]{1,0:T(8,128)(2,1)}, bf16[256,1024]{1,0:T(8,128)(2,1)S(1)}, u32[]{:S(2)}, u32[]{:S(2)}) collective-permute-start(bf16[256,1024]{1,0:T(8,128)(2,1)} %w0.1), channel_id=1, source_target_pairs={{0,8},{8,0},{1,9},{9,1},{2,10},{10,2},{3,11},{11,3},{4,12},{12,4},... | collective-permute-start | bytes 1572872 | tf_op jit(solution)/shard_map/ppermute | solution.py:182
  7.9 3.5 %collective-permute-start.15 = (bf16[128,256]{1,0:T(8,128)(2,1)S(1)}, bf16[128,256]{1,0:T(8,128)(2,1)S(1)}, u32[]{:S(2)}, u32[]{:S(2)}) collective-permute-start(bf16[128,256]{1,0:T(8,128)(2,1)S(1)} %pad_maximum_fusion.4), channel_id=1, source_target_pairs={{0,16},{16,0},{1,17},{17,1},{2,18},{18,2},{3,19},{19,3},{4,20},{20... | collective-permute-start | bytes 196616 | tf_op jit(solution)/shard_map/ppermute | solution.py:182
  12.3 2.4 %collective-permute-start.16 = (bf16[256,256]{1,0:T(8,128)(2,1)S(1)}, bf16[256,256]{1,0:T(8,128)(2,1)S(1)}, u32[]{:S(2)}, u32[]{:S(2)}) collective-permute-start(bf16[256,256]{1,0:T(8,128)(2,1)S(1)} %maximum_select_fusion.2), channel_id=1, source_target_pairs={{0,8},{8,0},{1,9},{9,1},{2,10},{10,2},{3,11},{11,3},{4,12},{12,4},... | collective-permute-start | bytes 393224 | tf_op jit(solution)/shard_map/ppermute | solution.py:182
  14.8 12.0 %collective-permute-start.17 = (bf16[512,256]{1,0:T(8,128)(2,1)S(1)}, bf16[512,256]{1,0:T(8,128)(2,1)S(1)}, u32[]{:S(2)}, u32[]{:S(2)}) collective-permute-start(bf16[512,256]{1,0:T(8,128)(2,1)S(1)} %maximum_select_fusion.1), channel_id=1, source_target_pairs={{0,32},{32,64},{64,96},{96,128},{128,160},{160,192},{192,224},{224... | collective-permute-start | bytes 786440 | tf_op jit(solution)/shard_map/ppermute | solution.py:193
  17.2 24.8 %collective-permute-start.7 = (bf16[256,1024]{1,0:T(8,128)(2,1)S(1)}, bf16[256,1024]{1,0:T(8,128)(2,1)}, u32[]{:S(2)}, u32[]{:S(2)}) collective-permute-start(bf16[256,1024]{1,0:T(8,128)(2,1)S(1)} %collective-permute-done.6), channel_id=1, source_target_pairs={{0,32},{32,64},{64,96},{96,128},{128,160},{160,192},{192,224},{224... | collective-permute-start | bytes 1572872 | tf_op jit(solution)/shard_map/ppermute | solution.py:193
  17.9 26.2 %copy-start.8 = (bf16[256,1024]{1,0:T(8,128)(2,1)}, bf16[256,1024]{1,0:T(8,128)(2,1)S(1)}, u32[]{:S(2)}) copy-start(bf16[256,1024]{1,0:T(8,128)(2,1)S(1)} %collective-permute-done.5.w1) | copy-start | bytes 1572868
  17.9 26.1 %collective-permute-start.8 = (bf16[256,1024]{1,0:T(8,128)(2,1)S(1)}, bf16[256,1024]{1,0:T(8,128)(2,1)}, u32[]{:S(2)}, u32[]{:S(2)}) collective-permute-start(bf16[256,1024]{1,0:T(8,128)(2,1)S(1)} %collective-permute-done.5.w1), channel_id=1, source_target_pairs={{0,32},{32,64},{64,96},{96,128},{128,160},{160,192},{192,224},{224... | collective-permute-start | bytes 1572872 | tf_op jit(solution)/shard_map/ppermute | solution.py:193
  20.6 9.0 %all-to-all-start = ((bf16[4,16,2048]{2,1,0:T(8,128)(2,1)}), bf16[4,16,2048]{2,1,0:T(8,128)(2,1)S(1)}, u32[]{:S(2)}, u32[]{:S(2)}) async-start(bf16[4,16,2048]{2,1,0:T(8,128)(2,1)} %bitcast.12), calls=%async_computation | async-start | bytes 524288 | tf_op jit(solution)/shard_map/all_to_all | solution.py:239
  26.8 20.2 %copy-start.1 = (bf16[512,256]{1,0:T(8,128)(2,1)}, bf16[512,256]{1,0:T(8,128)(2,1)S(1)}, u32[]{:S(2)}) copy-start(bf16[512,256]{1,0:T(8,128)(2,1)S(1)} %collective-permute-done.17) | copy-start | bytes 786436
  26.8 14.5 %collective-permute-start.18 = (bf16[512,256]{1,0:T(8,128)(2,1)S(1)}, bf16[512,256]{1,0:T(8,128)(2,1)S(1)}, u32[]{:S(2)}, u32[]{:S(2)}) collective-permute-start(bf16[512,256]{1,0:T(8,128)(2,1)S(1)} %collective-permute-done.17), channel_id=1, source_target_pairs={{0,32},{32,64},{64,96},{96,128},{128,160},{160,192},{192,224},{224... | collective-permute-start | bytes 786440 | tf_op jit(solution)/shard_map/ppermute | solution.py:193
  29.6 14.5 %collective-permute-start = (bf16[64,2048]{1,0:T(8,128)(2,1)S(1)}, bf16[64,2048]{1,0:T(8,128)(2,1)S(1)}, u32[]{:S(2)}, u32[]{:S(2)}) collective-permute-start(bf16[64,2048]{1,0:T(8,128)(2,1)S(1)} %bitcast.54), channel_id=1, source_target_pairs={{0,1},{1,0},{2,3},{3,2},{4,5},{5,4},{6,7},{7,6},{8,9},{9,8},{10,11... | collective-permute-start | bytes 786440 | tf_op jit(solution)/shard_map/ppermute | solution.py:182
  41.3 5.7 %copy-start.2 = (bf16[512,256]{1,0:T(8,128)(2,1)}, bf16[512,256]{1,0:T(8,128)(2,1)S(1)}, u32[]{:S(2)}) copy-start(bf16[512,256]{1,0:T(8,128)(2,1)S(1)} %collective-permute-done.18) | copy-start | bytes 786436
  41.3 5.7 %collective-permute-start.19 = (bf16[512,256]{1,0:T(8,128)(2,1)S(1)}, bf16[512,256]{1,0:T(8,128)(2,1)S(1)}, u32[]{:S(2)}, u32[]{:S(2)}) collective-permute-start(bf16[512,256]{1,0:T(8,128)(2,1)S(1)} %collective-permute-done.18), channel_id=1, source_target_pairs={{0,32},{32,64},{64,96},{96,128},{128,160},{160,192},{192,224},{224... | collective-permute-start | bytes 786440 | tf_op jit(solution)/shard_map/ppermute | solution.py:193
  42.0 8.7 %collective-permute-start.9 = (bf16[256,1024]{1,0:T(8,128)(2,1)}, bf16[256,1024]{1,0:T(8,128)(2,1)}, u32[]{:S(2)}, u32[]{:S(2)}) collective-permute-start(bf16[256,1024]{1,0:T(8,128)(2,1)} %collective-permute-done.7.w2), channel_id=1, source_target_pairs={{0,32},{32,64},{64,96},{96,128},{128,160},{160,192},{192,224},{224... | collective-permute-start | bytes 1572872 | tf_op jit(solution)/shard_map/ppermute | solution.py:193
  44.1 12.3 %collective-permute-start.10 = (bf16[256,1024]{1,0:T(8,128)(2,1)}, bf16[256,1024]{1,0:T(8,128)(2,1)}, u32[]{:S(2)}, u32[]{:S(2)}) collective-permute-start(bf16[256,1024]{1,0:T(8,128)(2,1)} %collective-permute-done.8.w3), channel_id=1, source_target_pairs={{0,32},{32,64},{64,96},{96,128},{128,160},{160,192},{192,224},{224... | collective-permute-start | bytes 1572872 | tf_op jit(solution)/shard_map/ppermute | solution.py:193
  44.2 24.8 %copy-start.4 = (bf16[128,2048]{1,0:T(8,128)(2,1)}, bf16[128,2048]{1,0:T(8,128)(2,1)S(1)}, u32[]{:S(2)}) copy-start(bf16[128,2048]{1,0:T(8,128)(2,1)S(1)} %pad_maximum_fusion.2.gh) | copy-start | bytes 1572868
  44.2 19.4 %copy-start.10 = (s32[8]{0:T(128)S(1)}, s32[8]{0:T(128)}, u32[]{:S(2)}) copy-start(s32[8]{0:T(128)} %param.11) | copy-start | bytes 100
  44.2 19.8 %copy-start.5 = (bf16[128,8,128]{2,1,0:T(8,128)(2,1)S(1)}, bf16[128,8,128]{2,1,0:T(8,128)(2,1)}, u32[]{:S(2)}) copy-start(bf16[128,8,128]{2,1,0:T(8,128)(2,1)} %param.6) | copy-start | bytes 786436
  44.3 15.0 %collective-permute-start.1 = (bf16[128,2048]{1,0:T(8,128)(2,1)S(1)}, bf16[128,2048]{1,0:T(8,128)(2,1)S(1)}, u32[]{:S(2)}, u32[]{:S(2)}) collective-permute-start(bf16[128,2048]{1,0:T(8,128)(2,1)S(1)} %pad_maximum_fusion.2.gh), channel_id=1, source_target_pairs={{0,2},{2,4},{4,6},{6,0},{1,3},{3,5},{5,7},{7,1},{8,10},{10,12},{12... | collective-permute-start | bytes 1572872 | tf_op jit(solution)/shard_map/ppermute | solution.py:186
  45.5 15.2 %collective-permute-start.2 = (bf16[128,2048]{1,0:T(8,128)(2,1)S(1)}, bf16[128,2048]{1,0:T(8,128)(2,1)}, u32[]{:S(2)}, u32[]{:S(2)}) collective-permute-start(bf16[128,2048]{1,0:T(8,128)(2,1)S(1)} %pad_maximum_fusion.2.gh), channel_id=1, source_target_pairs={{0,6},{2,0},{4,2},{6,4},{1,7},{3,1},{5,3},{7,5},{8,14},{10,8},{12,... | collective-permute-start | bytes 1572872 | tf_op jit(solution)/shard_map/ppermute | solution.py:186
  47.0 0.7 copy-start.3
  47.8 28.2 %collective-permute-start.20 = (bf16[3,512,256]{2,1,0:T(8,128)(2,1)S(1)}, bf16[3,512,256]{2,1,0:T(8,128)(2,1)S(1)}, u32[]{:S(2)}, u32[]{:S(2)}) collective-permute-start(bf16[3,512,256]{2,1,0:T(8,128)(2,1)S(1)} %pad_maximum_fusion.1), channel_id=1, source_target_pairs={{0,8},{8,0},{1,9},{9,1},{2,10},{10,2},{3,11},{11,3},{4,12},{12,4},... | collective-permute-start | bytes 2359304 | tf_op jit(solution)/shard_map/ppermute | solution.py:182
  50.7 18.3 %collective-permute-start.11 = (bf16[256,1024]{1,0:T(8,128)(2,1)}, bf16[256,1024]{1,0:T(8,128)(2,1)}, u32[]{:S(2)}, u32[]{:S(2)}) collective-permute-start(bf16[256,1024]{1,0:T(8,128)(2,1)} %collective-permute-done.9.w4), channel_id=1, source_target_pairs={{0,32},{32,64},{64,96},{96,128},{128,160},{160,192},{192,224},{224... | collective-permute-start | bytes 1572872 | tf_op jit(solution)/shard_map/ppermute | solution.py:193
  56.4 12.7 %collective-permute-start.12 = (bf16[256,1024]{1,0:T(8,128)(2,1)}, bf16[256,1024]{1,0:T(8,128)(2,1)}, u32[]{:S(2)}, u32[]{:S(2)}) collective-permute-start(bf16[256,1024]{1,0:T(8,128)(2,1)} %collective-permute-done.10.w5), channel_id=1, source_target_pairs={{0,32},{32,64},{64,96},{96,128},{128,160},{160,192},{192,224},{224... | collective-permute-start | bytes 1572872 | tf_op jit(solution)/shard_map/ppermute | solution.py:193
  59.2 1.5 %copy-start.7 = (bf16[128,2048]{1,0:T(8,128)(2,1)}, bf16[128,2048]{1,0:T(8,128)(2,1)S(1)}, u32[]{:S(2)}) copy-start(bf16[128,2048]{1,0:T(8,128)(2,1)S(1)} %collective-permute-done.1.gu) | copy-start | bytes 1572868
  59.3 8.8 %collective-permute-start.3 = (bf16[64,2048]{1,0:T(8,128)(2,1)S(1)}, bf16[64,2048]{1,0:T(8,128)(2,1)}, u32[]{:S(2)}, u32[]{:S(2)}) collective-permute-start(bf16[64,2048]{1,0:T(8,128)(2,1)S(1)} %slice.269), channel_id=1, source_target_pairs={{0,2},{2,4},{4,6},{6,0},{1,3},{3,5},{5,7},{7,1},{8,10},{10,12},{12... | collective-permute-start | bytes 786440 | tf_op jit(solution)/shard_map/ppermute | solution.py:186
  61.7 7.3 %collective-permute-start.4 = (bf16[64,2048]{1,0:T(8,128)(2,1)S(1)}, bf16[64,2048]{1,0:T(8,128)(2,1)S(1)}, u32[]{:S(2)}, u32[]{:S(2)}) collective-permute-start(bf16[64,2048]{1,0:T(8,128)(2,1)S(1)} %slice.270), channel_id=1, source_target_pairs={{0,6},{2,0},{4,2},{6,4},{1,7},{3,1},{5,3},{7,5},{8,14},{10,8},{12,... | collective-permute-start | bytes 786440 | tf_op jit(solution)/shard_map/ppermute | solution.py:186
  69.0 0.7 copy-start.9
  76.0 2.3 %collective-permute-start.13 = (bf16[2,128,1024]{2,1,0:T(8,128)(2,1)}, bf16[2,128,1024]{2,1,0:T(8,128)(2,1)}, u32[]{:S(2)}, u32[]{:S(2)}) collective-permute-start(bf16[2,128,1024]{2,1,0:T(8,128)(2,1)} %get-tuple-element.11), channel_id=1, source_target_pairs={{0,8},{8,0},{1,9},{9,1},{2,10},{10,2},{3,11},{11,3},{4,12},{12,4},... | collective-permute-start | bytes 1572872 | tf_op jit(solution)/shard_map/ppermute | solution.py:182
  76.1 2.2 %copy-start = (f32[2,128,1024]{2,1,0:T(8,128)S(1)}, f32[2,128,1024]{2,1,0:T(8,128)}, u32[]{:S(2)}) copy-start(f32[2,128,1024]{2,1,0:T(8,128)} %get-tuple-element.10) | copy-start | bytes 3145732
  79.4 7.9 %collective-permute-start.14 = (bf16[128,1024]{1,0:T(8,128)(2,1)S(1)}, bf16[128,1024]{1,0:T(8,128)(2,1)S(1)}, u32[]{:S(2)}, u32[]{:S(2)}) collective-permute-start(bf16[128,1024]{1,0:T(8,128)(2,1)S(1)} %fusion.5), channel_id=1, source_target_pairs={{0,16},{16,0},{1,17},{17,1},{2,18},{18,2},{3,19},{19,3},{4,20},{20... | collective-permute-start | bytes 786440 | tf_op jit(solution)/shard_map/ppermute | solution.py:182
  93.3 3.1 %collective-permute-start.21 = (bf16[3,512,256]{2,1,0:T(8,128)(2,1)}, bf16[3,512,256]{2,1,0:T(8,128)(2,1)S(1)}, u32[]{:S(2)}, u32[]{:S(2)}) collective-permute-start(bf16[3,512,256]{2,1,0:T(8,128)(2,1)} %get-tuple-element.16), channel_id=1, source_target_pairs={{0,8},{8,0},{1,9},{9,1},{2,10},{10,2},{3,11},{11,3},{4,12},{12,4},... | collective-permute-start | bytes 2359304 | tf_op jit(solution)/shard_map/ppermute | solution.py:182
  97.7 22.1 %collective-permute-start.22 = (bf16[512,256]{1,0:T(8,128)(2,1)S(1)}, bf16[512,256]{1,0:T(8,128)(2,1)S(1)}, u32[]{:S(2)}, u32[]{:S(2)}) collective-permute-start(bf16[512,256]{1,0:T(8,128)(2,1)S(1)} %select_bitcast_fusion), channel_id=1, source_target_pairs={{0,224},{32,0},{64,32},{96,64},{128,96},{160,128},{192,160},{224,1... | collective-permute-start | bytes 786440 | tf_op jit(solution)/shard_map/ppermute | solution.py:193
  120.0 19.3 %copy-start.6 = (bf16[128,1024]{1,0:T(8,128)(2,1)S(1)}, bf16[128,1024]{1,0:T(8,128)(2,1)}, u32[]{:S(2)}) copy-start(bf16[128,1024]{1,0:T(8,128)(2,1)} %get-tuple-element.14) | copy-start | bytes 786436
  120.0 13.9 %collective-permute-start.23 = (bf16[512,256]{1,0:T(8,128)(2,1)S(1)}, bf16[512,256]{1,0:T(8,128)(2,1)S(1)}, u32[]{:S(2)}, u32[]{:S(2)}) collective-permute-start(bf16[512,256]{1,0:T(8,128)(2,1)S(1)} %fusion.3), channel_id=1, source_target_pairs={{0,224},{32,0},{64,32},{96,64},{128,96},{160,128},{192,160},{224,1... | collective-permute-start | bytes 786440 | tf_op jit(solution)/shard_map/ppermute | solution.py:193
  134.0 0.7 collective-permute-start.24
  134.8 4.4 %collective-permute-start.25 = (bf16[256,256]{1,0:T(8,128)(2,1)S(1)}, bf16[256,256]{1,0:T(8,128)(2,1)S(1)}, u32[]{:S(2)}, u32[]{:S(2)}) collective-permute-start(bf16[256,256]{1,0:T(8,128)(2,1)S(1)} %broadcast_select_fusion.2), channel_id=1, source_target_pairs={{0,8},{8,0},{1,9},{9,1},{2,10},{10,2},{3,11},{11,3},{4,12},{12,4},... | collective-permute-start | bytes 393224 | tf_op jit(solution)/shard_map/ppermute | solution.py:182
  139.2 3.2 %collective-permute-start.26 = (bf16[128,256]{1,0:T(8,128)(2,1)S(1)}, bf16[128,256]{1,0:T(8,128)(2,1)S(1)}, u32[]{:S(2)}, u32[]{:S(2)}) collective-permute-start(bf16[128,256]{1,0:T(8,128)(2,1)S(1)} %select_convert_fusion), channel_id=1, source_target_pairs={{0,16},{16,0},{1,17},{17,1},{2,18},{18,2},{3,19},{19,3},{4,20},{20... | collective-permute-start | bytes 196616 | tf_op jit(solution)/shard_map/ppermute | solution.py:182

commit v2 on v1

v2 whole, which is shorter than its diff:
```python
import math

import jax
import jax.numpy as jnp
from jax import lax
from jax.experimental import pallas as pl
from jax.experimental.pallas import tpu as pltpu
from jax.sharding import Mesh, PartitionSpec as P

BF = jnp.bfloat16
F32 = jnp.float32
NEG = -1e30
HD = 128
SCALE = HD**-0.5
C2 = SCALE * math.log2(math.e)
PLANE = 512
PLANES = 6
ROWS = 1024
MIB = 1024 * 1024
P_MIB, F_MIB, B_MIB = 16, 20, 24
HINT = 8

NT = (((1,), (1,)), ((), ()))
NN = (((1,), (0,)), ((), ()))
TN = (((0,), (0,)), ((), ()))


def dot(a, b, dims):
    return lax.dot_general(a, b, dims, preferred_element_type=F32)


def key_positions(z, d):
    r = lax.broadcasted_iota(jnp.int32, (PLANE, 1), 0)
    part = r >> 7
    block = ((part & 1) << 1) | (part >> 1)
    return (z - d) * PLANE + block * 128 + (r & 127)


def where_am_i():
    z, c = lax.axis_index("z"), lax.axis_index("c")
    return z, c, ((z * 2 + lax.axis_index("yl")) * 2 + c) * 128


def documents(lengths, pos0):
    row_pos = pos0 + (lax.broadcasted_iota(jnp.int32, (1, ROWS), 1) & 127)
    start, low, high = jnp.zeros((1, ROWS), jnp.int32), 0, 0
    end = lengths[0]
    for i in range(8):
        start = jnp.where(end <= row_pos, end, start)
        low = jnp.where(end <= pos0, end, low)
        high = jnp.where(end <= pos0 + 127, end, high)
        if i < 7:
            end = end + lengths[i + 1]
    return row_pos, start, low, high


def project_kernel(gh, gu, gd, gu2, gd2, w0, w1, w2, w3, w4, total, rest, a_scr):
    me = lax.axis_index("yl") * 2 + lax.axis_index("c")
    x, yh = lax.axis_index("x"), lax.axis_index("yh")
    for rel in range(4):
        src = pl.multiple_of((me ^ rel) * 16, 16)
        for half in range(2):
            base = pl.multiple_of(src + half * 64, 16)
            for turn_by, ref, at in (
                (0, gh, base),
                (1, gd, base),
                (2, (gu2, gd2)[half], src),
                (3, gu, base),
            ):
                tp = ((x + turn_by) & 3) * 2 + (yh ^ half)
                row = pl.multiple_of(rel * 128 + tp * 16, 16)
                a_scr[pl.ds(row, 16), :] = ref[pl.ds(at, 16), 0:1280]
                rest[pl.ds(row, 16), :] = ref[pl.ds(at, 16), 1280:2048]
    out = None
    for k, w in enumerate((w0, w1, w2, w3, w4)):
        part = dot(a_scr[:, k * 256 : k * 256 + 256], w[...], NN)
        out = part if out is None else out + part
    total[...] = out


def forward_kernel(
    lengths, q, plane, r1, r2, r3, t1, t2, t3, att, lse, kv, m_scr, l_scr
):
    z, c, pos0 = where_am_i()
    row_pos, start, low, high = documents(lengths, pos0)

    def place(d, ref):
        for b in range(4):
            kv[d, b * 128 : b * 128 + 128, :] = ref[:, b * 256 : b * 256 + 256]

    def place_all(near, far):
        for d, ref in ((1, near[0]), (2, near[1]), (3, near[2]), (4, far[1]), (5, far[0])):
            place(d, ref)

    place(0, plane)

    @pl.when(c == 0)
    def _():
        place_all((r1, r2, r3), (t1, t2))

    @pl.when(c != 0)
    def _():
        place_all((t1, t2, t3), (r1, r2))

    m_scr[...] = jnp.full((1, ROWS), NEG, F32)
    l_scr[...] = jnp.zeros((1, ROWS), F32)
    att[...] = jnp.zeros((HD, ROWS), F32)

    def work(d, masked):
        k = kv[d, :, 0:HD]
        v_t = kv[d, :, HD : 2 * HD].astype(F32).T.astype(BF)
        s = dot(k, q[...], NT)
        if masked:
            s = jnp.where(allowed(z, d, row_pos, start), s, NEG)
        old = m_scr[...]
        new = jnp.maximum(old, jnp.max(s, axis=0, keepdims=True) * C2)
        shrink = jnp.exp2(old - new)
        p = jnp.exp2(s * C2 - new)
        l_scr[...] = l_scr[...] * shrink + jnp.sum(p, axis=0, keepdims=True)
        m_scr[...] = new
        att[...] = att[...] * shrink + dot(v_t, p.astype(BF), NN)

    each_plane(work, z, 0, z - low // PLANE + 1, high)
    lse[...] = m_scr[...] + jnp.log2(l_scr[...])
    att[...] = att[...] / l_scr[...]


def allowed(z, d, row_pos, start):
    keys = key_positions(z, d)
    return (keys >= start) & (keys <= row_pos)


def each_plane(work, z, begin, end, clear):
    def plane(d, carry):
        whole = (d > 0) & ((z - d) * PLANE >= clear)

        @pl.when(whole)
        def _():
            work(d, False)

        @pl.when(jnp.logical_not(whole))
        def _():
            work(d, True)

        return carry

    lax.fori_loop(begin, end, plane, 0)


def gradients(lengths, q, do, kv, lse, delta, dq_t, begin, end, store):
    z, c, pos0 = where_am_i()
    row_pos, start, low, high = documents(lengths, pos0)
    count = z - low // PLANE + 1

    def work(d, masked):
        k = kv[d, :, 0:HD]
        v = kv[d, :, HD : 2 * HD]
        k_t = k.astype(F32).T.astype(BF)
        s = dot(k, q[...], NT)
        dp = dot(v, do[...], NT)
        p = jnp.exp2(s * C2 - lse[...])
        if masked:
            p = jnp.where(allowed(z, d, row_pos, start), p, 0.0)
        dv = dot(p.astype(BF), do[...], NN)
        ds = (p * (dp - delta[...])).astype(BF)
        dk = dot(ds, q[...], NN) * SCALE
        dq_t[...] += dot(k_t, ds, NN)
        store(d, jnp.concatenate([dk, dv], axis=1).astype(BF))

    stop = jnp.clip(count, begin, end)
    each_plane(work, z, begin, stop, high)

    def blank(d, carry):
        store(d, jnp.zeros((PLANE, 2 * HD), BF))
        return carry

    lax.fori_loop(stop, end, blank, 0)


def far_kernel(
    lengths, q, o0, o1, o2, att, lse, kv, keep, send, fifth, do, delta, dq_t
):
    c = lax.axis_index("c")
    o = (o0[...] + o1[...].astype(F32) + o2[...].astype(F32)).astype(BF)
    for h in range(8):
        cols = slice(h * 128, h * 128 + 128)
        do[cols, :] = o[:, cols]
        delta[:, cols] = jnp.sum(o[:, cols].astype(F32).T * att[:, cols], axis=0, keepdims=True)
    dq_t[...] = jnp.zeros((HD, ROWS), F32)

    def store(d, value):
        mine = ((d == 3) & (c == 0)) | ((d == 4) & (c != 0))

        @pl.when(mine)
        def _():
            keep[...] = value

        @pl.when((d < 5) & jnp.logical_not(mine))
        def _():
            send[...] = value

        @pl.when(d == 5)
        def _():
            fifth[...] = value

    gradients(lengths, q, do, kv, lse, delta, dq_t, 3, 6, store)


def near_kernel(
    lengths, q, do, lse, delta, kv, dq_far, fifth, dq, keep2, keep1, send2, send1, dq_t
):
    c = lax.axis_index("c")
    dq_t[...] = dq_far[...]

    @pl.when(c == 0)
    def _():
        send2[...] = fifth[...]

    @pl.when(c != 0)
    def _():
        keep2[...] = fifth[...]

    def store(d, value):
        @pl.when((d == 2) & (c == 0))
        def _():
            keep2[...] = value

        @pl.when((d == 2) & (c != 0))
        def _():
            send2[...] = value

        mine = ((d == 1) & (c == 0)) | ((d == 0) & (c != 0))

        @pl.when(mine)
        def _():
            keep1[...] = value

        @pl.when((d < 2) & jnp.logical_not(mine))
        def _():
            send1[...] = value

    gradients(lengths, q, do, kv, lse, delta, dq_t, 0, 3, store)
    for h in range(8):
        cols = slice(h * 128, h * 128 + 128)
        dq[:, cols] = (dq_t[:, cols] * SCALE).T.astype(BF)


def call(kernel, args, outs, scratch, flops, vmem_mib, scalars=None):
    vmem = pl.BlockSpec(memory_space=pltpu.VMEM)
    first = [] if scalars is None else [pl.BlockSpec(memory_space=pltpu.SMEM)]
    return pl.pallas_call(
        kernel,
        out_shape=outs,
        in_specs=first + [vmem] * len(args),
        out_specs=[vmem] * len(outs),
        scratch_shapes=scratch,
        compiler_params=pltpu.CompilerParams(vmem_limit_bytes=vmem_mib * MIB),
        cost_estimate=pl.CostEstimate(flops=flops, bytes_accessed=6 << 20, transcendentals=0),
    )(*([] if scalars is None else [scalars]), *args)


def tie(*xs):
    return lax.optimization_barrier(xs)


def shape(dims, dtype):
    return jax.ShapeDtypeStruct(dims, dtype)


def swap(x, axis):
    return lax.ppermute(x, axis, [(0, 1), (1, 0)])


def turn(x, step):
    return lax.ppermute(x, "x", [(i, (i + step) % 4) for i in range(4)])


def along_z(x, step0, step1):
    pairs = [(2 * z, 2 * ((z + step0) % 8)) for z in range(8)]
    if step1 is not None:
        pairs += [(2 * z + 1, 2 * ((z + step1) % 8) + 1) for z in range(8)]
    return lax.ppermute(x, ("z", "c"), pairs)


def add(a, b):
    return a.astype(F32) + b.astype(F32)


def local(queries, key_states, value_vectors, grad_output, out_weight, doc_lengths):
    z, yl, c = lax.axis_index("z"), lax.axis_index("yl"), lax.axis_index("c")
    first = c == 0

    rolled = lax.dynamic_slice(
        jnp.concatenate([grad_output, grad_output], axis=1), (0, z * 1024), (16, 8192)
    )

    def columns(to_yl, to_c):
        order = [(0, to_c)]
        for s in (1, 2, 3):
            far = s if to_c else 8 - s
            order += [(far, to_c), (far, 1 - to_c)]
        order.append((4, to_c))
        return jnp.concatenate(
            [rolled[:, s * 1024 + to_yl * 512 + par * 256 :][:, :256] for s, par in order], axis=1
        )

    sent = jnp.stack([columns(a, b) for a in (0, 1) for b in (0, 1)])

    t = swap(jnp.where(first, sent[1::2], sent[0::2]).reshape(32, 2048), "c")
    own = jnp.where(first, sent[0::2], sent[1::2]).reshape(32, 2048)
    both = jnp.where(first, jnp.stack([own, t]), jnp.stack([t, own])).reshape(2, 2, 16, 2048)
    away = swap(jnp.where(yl == 0, both[:, 1], both[:, 0]), "yl")
    here = jnp.where(yl == 0, both[:, 0], both[:, 1])
    got = jnp.where(yl == 0, jnp.stack([here, away]), jnp.stack([away, here])).reshape(64, 2048)
    gh = jnp.concatenate([got, swap(got, "yh")])
    gu, gd = turn(gh, 1), turn(gh, 3)
    gu2, gd2 = turn(gu[:64], 1), turn(gd[64:], 3)

    p1 = along_z(out_weight, 1, 7)
    q0 = swap(out_weight, "c")
    kv = jnp.concatenate([key_states.reshape(128, HD), value_vectors.reshape(128, HD)], axis=1)
    other = swap(kv, "yl")
    half = jnp.where(
        yl == 0, jnp.concatenate([kv, other], axis=1), jnp.concatenate([other, kv], axis=1)
    )
    other = swap(half, "c")
    plane = jnp.where(
        first, jnp.concatenate([half, other], axis=1), jnp.concatenate([other, half], axis=1)
    )
    q1 = along_z(q0, 1, 7)
    r1 = along_z(plane, 1, 5)
    p2 = along_z(p1, 1, 7)
    q2 = along_z(q1, 1, 7)
    r2 = along_z(tie(r1, q1, p2)[0], 1, 7)
    p3 = along_z(p2, 1, 7)
    q3 = along_z(q2, 1, 7)
    r3 = along_z(r2, 1, None)
    p4 = along_z(p3, 1, 7)

    t1, t2, t3 = swap(r1, "c"), swap(r2, "c"), swap(r3, "c")

    total, rest = call(
        project_kernel,
        [gh, gu, gd, gu2, gd2, out_weight, p1, q1, p2, q2],
        [shape((512, 1024), F32), shape((512, 768), BF)],
        [pltpu.VMEM((512, 1280), BF)],
        HINT * 2 * 512 * 1280 * 1024,
        P_MIB,
    )
    for k, w in enumerate((p3, q3, p4)):
        total = total + dot(rest[:, k * 256 : k * 256 + 256], w, NN)
    total = total.reshape(2, 2, 128, 1024)
    keep0, keep1 = total[0, 0], total[1, 0]
    send, t3 = tie(total[1, 1].astype(BF), t3)
    from_both = swap(send, "c")
    from_core = swap(total[0, 1].astype(BF), "c")
    from_y = swap(add(keep1, from_both).astype(BF), "yl")

    q = queries.transpose(1, 0, 2).reshape(ROWS, HD)
    q, from_both = tie(q, from_both)
    att, lse, planes = call(
        forward_kernel,
        [q, plane, r1, r2, r3, t1, t2, t3],
        [
            shape((HD, ROWS), F32),
            shape((1, ROWS), F32),
            shape((PLANES, PLANE, 2 * HD), BF),
        ],
        [pltpu.VMEM((1, ROWS), F32)] * 2,
        1,
        F_MIB,
        doc_lengths,
    )

    block = shape((PLANE, 2 * HD), BF)
    keep, send, fifth, do, delta, dq_far = call(
        far_kernel,
        [q, keep0, from_core, from_y, att, lse, planes],
        [block, block, block, shape((ROWS, HD), BF), shape((1, ROWS), F32), shape((HD, ROWS), F32)],
        [],
        5 * 1024 * 2560 * 128,
        B_MIB,
        doc_lengths,
    )

    got = swap(send, "c")
    run = along_z(add(keep, got).astype(BF), 7, 1)
    q, got = tie(q, got)
    dq, keep2, keep1, send2, send1 = call(
        near_kernel,
        [q, do, lse, delta, planes, dq_far, fifth],
        [shape((128, 1024), BF), block, block, block, block],
        [pltpu.VMEM((HD, ROWS), F32)],
        5 * 1024 * 2560 * 128,
        B_MIB,
        doc_lengths,
    )
    middle = add(keep2, swap(send2, "c"))
    final = add(keep1, swap(send1, "c"))
    run = along_z((run.astype(F32) + middle).astype(BF), 7, 2)
    run = jnp.where(first, run.astype(F32) + final, run.astype(F32)).astype(BF)
    run = along_z(run, 7, 1)
    run = jnp.where(first, run.astype(F32), run.astype(F32) + final)
    total = jnp.where(first, run[:256], run[256:]) + swap(
        jnp.where(first, run[256:], run[:256]).astype(BF), "c"
    ).astype(F32)
    there = swap(jnp.where(yl == 0, total[128:], total[:128]).astype(BF), "yl")
    kv_grad = (jnp.where(yl == 0, total[:128], total[128:]) + there.astype(F32)).astype(BF)
    return (
        dq.reshape(128, 8, HD),
        kv_grad[:, :HD].reshape(128, 1, HD),
        kv_grad[:, HD:].reshape(128, 1, HD),
    )


def solution(mesh):
    grid = Mesh(mesh.devices.reshape(8, 2, 2, 4, 2), ("z", "yl", "c", "x", "yh"))
    ctx, tp = ("z", "yl", "c"), ("x", "yh")
    return jax.shard_map(
        local,
        mesh=grid,
        in_specs=(
            P(ctx, tp, None),
            P(ctx, tp, None),
            P(ctx, tp, None),
            P(ctx + tp, None),
            P(ctx, tp),
            P(),
        ),
        out_specs=(P(ctx, tp, None), P(ctx, tp, None), P(ctx, tp, None)),
        check_vma=False,
    )
```

time: 144 us -> 116 us (0.81)
  waiting for transfers between devices: 62.7 us -> 54.2 us
  Pallas kernels: 15.6 us -> 7.19 us
  other arithmetic: 10.4 us -> 2.18 us
  local copies, waits for them, and re-layouts: 5.93 us -> 1.61 us
    ppermute x13, waiting for transfers between devices: 50.6 us -> 37.2 us  [along_z(): return lax.ppermute(x, ('z', 'c'), pairs)]
    ppermute x10 -> x17, waiting for transfers between devices: 8.57 us -> 17 us  [swap(): return lax.ppermute(x, axis, [(0, 1), (1, 0)])]
    pallas_call x3 -> x4, Pallas kernels: 15.6 us -> 7.19 us  [call(): pl.pallas_call(kernel, out_shape=outs, in_specs=first + [vmem] * len(args...]
    ppermute x10 -> x17, starting transfers between devices: 11.7 us -> 17.4 us  [swap(): return lax.ppermute(x, axis, [(0, 1), (1, 0)])]
    ppermute x4, waiting for transfers between devices: 3.48 us -> 0.01 us  [turn(): return lax.ppermute(x, 'x', [(i, (i + step) % 4) for i in range(4)])]
    all_to_all x1 -> x0, starting transfers between devices: 3.4 us -> none  [local(): got = lax.all_to_all(sent, ('yl', 'c'), 0, 0, tiled=True)]
    select_n x8 -> x7, other arithmetic: 2.51 us -> 0.3 us  [the longest x1 0.11 us: local(): run = jnp.where(first, run.astype(F32), run.astype(F32) + final)]
    concatenate x2 -> x0, other arithmetic: 2.06 us -> none  [the longest x1 1.34 us: local(): jnp.concatenate([plane[None], jnp.where(first, mine, theirs), jnp.where(f...]
  transfers between devices with their start and end apart: 28 -> 34, of which waited for: 15 -> 16; matrix products, arithmetic and copies ran while one was open for 7% -> 2% of each run, Pallas kernels for 7% -> 5%
where the time goes in v2:
time: 116 us
  waiting for transfers between devices  54.2 us (47%)
  starting transfers between devices  48.4 us (42%)
  Pallas kernels  7.19 us (6%)
  other arithmetic  2.18 us (2%)
  local copies, waits for them, and re-layouts  1.61 us (1%)
  matrix products  1.43 us (1%)
    ppermute x13, waiting for transfers between devices, along_z(): return lax.ppermute(x, ('z', 'c'), pairs)  37.2 us
    ppermute x13, starting transfers between devices, along_z(): return lax.ppermute(x, ('z', 'c'), pairs)  25.2 us
    ppermute x17, starting transfers between devices, swap(): return lax.ppermute(x, axis, [(0, 1), (1, 0)])  17.4 us
    ppermute x17, waiting for transfers between devices, swap(): return lax.ppermute(x, axis, [(0, 1), (1, 0)])  17 us
    pallas_call x4, Pallas kernels, call(): pl.pallas_call(kernel, out_shape=outs, in_specs=first + [vmem] * len(args...  7.19 us
    ppermute x4, starting transfers between devices, turn(): return lax.ppermute(x, 'x', [(i, (i + step) % 4) for i in range(4)])  5.75 us
  transfers between devices with their start and end apart: 34, of which 16 were waited for; matrix products, arithmetic and copies ran while one was open for 2% of the time, Pallas kernels for 5%

profile of v2, /device:TPU:1, one launch (start us, length us, event | category | flops | bytes accessed | tf_op | source)
XLA Modules:
  0.0 116.1 jit_solution(3558063491426604255)
XLA Ops:
  0.7 1.1 fusion.3
  2.0 3.3 %collective-permute-start = (bf16[32,2048]{1,0:T(8,128)(2,1)S(1)}, bf16[32,2048]{1,0:T(8,128)(2,1)S(1)}, u32[]{:S(2)}, u32[]{:S(2)}) collective-permute-start(bf16[32,2048]{1,0:T(8,128)(2,1)S(1)} %bitcast.63), channel_id=1, source_target_pairs={{0,8},{8,0},{1,9},{9,1},{2,10},{10,2},{3,11},{11,3},{4,12},{12,4},... | collective-permute-start | bytes 393224 | tf_op jit(solution)/shard_map/ppermute | solution.py:271
  5.4 0.1 collective-permute-start.8
  5.5 3.8 %collective-permute-start.7 = (bf16[256,1024]{1,0:T(8,128)(2,1)S(1)}, bf16[256,1024]{1,0:T(8,128)(2,1)S(1)}, u32[]{:S(2)}, u32[]{:S(2)}) collective-permute-start(bf16[256,1024]{1,0:T(8,128)(2,1)S(1)} %copy-done.1), channel_id=1, source_target_pairs={{0,32},{32,64},{64,96},{96,128},{128,160},{160,192},{192,224},{224... | collective-permute-start | bytes 1572872 | tf_op jit(solution)/shard_map/ppermute | solution.py:282
  9.4 1.4 %collective-permute-start.1 = (bf16[2,16,2048]{2,1,0:T(8,128)(2,1)S(1)}, bf16[2,16,2048]{2,1,0:T(8,128)(2,1)S(1)}, u32[]{:S(2)}, u32[]{:S(2)}) collective-permute-start(bf16[2,16,2048]{2,1,0:T(8,128)(2,1)S(1)} %fusion.12), channel_id=1, source_target_pairs={{0,16},{16,0},{1,17},{17,1},{2,18},{18,2},{3,19},{19,3},{4,20},{20... | collective-permute-start | bytes 393224 | tf_op jit(solution)/shard_map/ppermute | solution.py:271
  10.8 2.8 %collective-permute-done.1 = bf16[2,16,2048]{2,1,0:T(8,128)(2,1)S(1)} collective-permute-done((bf16[2,16,2048]{2,1,0:T(8,128)(2,1)S(1)}, bf16[2,16,2048]{2,1,0:T(8,128)(2,1)S(1)}, u32[]{:S(2)}, u32[]{:S(2)}) %collective-permute-start.1) | collective-permute-done | bytes 131104 | tf_op jit(solution)/shard_map/ppermute | solution.py:271
  13.6 3.0 %collective-permute-start.2 = (bf16[64,2048]{1,0:T(8,128)(2,1)S(1)}, bf16[64,2048]{1,0:T(8,128)(2,1)S(1)}, u32[]{:S(2)}, u32[]{:S(2)}) collective-permute-start(bf16[64,2048]{1,0:T(8,128)(2,1)S(1)} %bitcast.59), channel_id=1, source_target_pairs={{0,1},{1,0},{2,3},{3,2},{4,5},{5,4},{6,7},{7,6},{8,9},{9,8},{10,11... | collective-permute-start | bytes 786440 | tf_op jit(solution)/shard_map/ppermute | solution.py:271
  16.6 0.5 collective-permute-start.15
  17.1 1.5 %collective-permute-start.9 = (bf16[256,1024]{1,0:T(8,128)(2,1)S(1)}, bf16[256,1024]{1,0:T(8,128)(2,1)S(1)}, u32[]{:S(2)}, u32[]{:S(2)}) collective-permute-start(bf16[256,1024]{1,0:T(8,128)(2,1)S(1)} %collective-permute-done.8), channel_id=1, source_target_pairs={{0,32},{32,64},{64,96},{96,128},{128,160},{160,192},{192,224},{224... | collective-permute-start | bytes 1572872 | tf_op jit(solution)/shard_map/ppermute | solution.py:282
  18.6 0.5 collective-permute-start.10
  19.1 3.5 %collective-permute-done.2 = bf16[64,2048]{1,0:T(8,128)(2,1)S(1)} collective-permute-done((bf16[64,2048]{1,0:T(8,128)(2,1)S(1)}, bf16[64,2048]{1,0:T(8,128)(2,1)S(1)}, u32[]{:S(2)}, u32[]{:S(2)}) %collective-permute-start.2) | collective-permute-done | bytes 262176 | tf_op jit(solution)/shard_map/ppermute | solution.py:271
  22.7 0.7 collective-permute-start.3
  23.4 2.0 %collective-permute-start.4 = (bf16[128,2048]{1,0:T(8,128)(2,1)S(1)}, bf16[128,2048]{1,0:T(8,128)(2,1)S(1)}, u32[]{:S(2)}, u32[]{:S(2)}) collective-permute-start(bf16[128,2048]{1,0:T(8,128)(2,1)S(1)} %pad_maximum_fusion.gh), channel_id=1, source_target_pairs={{0,6},{2,0},{4,2},{6,4},{1,7},{3,1},{5,3},{7,5},{8,14},{10,8},{12,... | collective-permute-start | bytes 1572872 | tf_op jit(solution)/shard_map/ppermute | solution.py:275
  25.5 0.1 collective-permute-start.16
  25.6 1.3 %collective-permute-done.16 = bf16[128,512]{1,0:T(8,128)(2,1)S(1)} collective-permute-done((bf16[128,512]{1,0:T(8,128)(2,1)S(1)}, bf16[128,512]{1,0:T(8,128)(2,1)S(1)}, u32[]{:S(2)}, u32[]{:S(2)}) %collective-permute-start.16) | collective-permute-done | bytes 131104 | tf_op jit(solution)/shard_map/ppermute | solution.py:271
  26.9 0.1 maximum_select_fusion.2.plane
  27.0 4.4 %collective-permute-start.17 = (bf16[128,1024]{1,0:T(8,128)(2,1)S(1)}, bf16[128,1024]{1,0:T(8,128)(2,1)S(1)}, u32[]{:S(2)}, u32[]{:S(2)}) collective-permute-start(bf16[128,1024]{1,0:T(8,128)(2,1)S(1)} %maximum_select_fusion.2.plane), channel_id=1, source_target_pairs={{0,32},{32,64},{64,96},{96,128},{128,160},{160,192},{192,224},{224... | collective-permute-start | bytes 786440 | tf_op jit(solution)/shard_map/ppermute | solution.py:282
  31.4 0.7 collective-permute-start.11
  32.2 1.6 %collective-permute-start.12 = (bf16[256,1024]{1,0:T(8,128)(2,1)S(1)}, bf16[256,1024]{1,0:T(8,128)(2,1)S(1)}, u32[]{:S(2)}, u32[]{:S(2)}) collective-permute-start(bf16[256,1024]{1,0:T(8,128)(2,1)S(1)} %collective-permute-done.10.w3), channel_id=1, source_target_pairs={{0,32},{32,64},{64,96},{96,128},{128,160},{160,192},{192,224},{224... | collective-permute-start | bytes 1572872 | tf_op jit(solution)/shard_map/ppermute | solution.py:282
  33.8 6.7 %collective-permute-done.17.r1 = bf16[128,1024]{1,0:T(8,128)(2,1)S(1)} collective-permute-done((bf16[128,1024]{1,0:T(8,128)(2,1)S(1)}, bf16[128,1024]{1,0:T(8,128)(2,1)S(1)}, u32[]{:S(2)}, u32[]{:S(2)}) %collective-permute-start.17) | collective-permute-done | bytes 262176 | tf_op jit(solution)/shard_map/ppermute | solution.py:282
  40.4 2.2 %collective-permute-start.18 = (bf16[128,1024]{1,0:T(8,128)(2,1)S(1)}, bf16[128,1024]{1,0:T(8,128)(2,1)S(1)}, u32[]{:S(2)}, u32[]{:S(2)}) collective-permute-start(bf16[128,1024]{1,0:T(8,128)(2,1)S(1)} %collective-permute-done.17.r1), channel_id=1, source_target_pairs={{0,32},{32,64},{64,96},{96,128},{128,160},{160,192},{192,224},{224... | collective-permute-start | bytes 786440 | tf_op jit(solution)/shard_map/ppermute | solution.py:282
  42.8 2.9 %collective-permute-start.6 = (bf16[64,2048]{1,0:T(8,128)(2,1)S(1)}, bf16[64,2048]{1,0:T(8,128)(2,1)S(1)}, u32[]{:S(2)}, u32[]{:S(2)}) collective-permute-start(bf16[64,2048]{1,0:T(8,128)(2,1)S(1)} %slice.291), channel_id=1, source_target_pairs={{0,6},{2,0},{4,2},{6,4},{1,7},{3,1},{5,3},{7,5},{8,14},{10,8},{12,... | collective-permute-start | bytes 786440 | tf_op jit(solution)/shard_map/ppermute | solution.py:275
  45.7 8.7 %collective-permute-done.18.r2 = bf16[128,1024]{1,0:T(8,128)(2,1)S(1)} collective-permute-done((bf16[128,1024]{1,0:T(8,128)(2,1)S(1)}, bf16[128,1024]{1,0:T(8,128)(2,1)S(1)}, u32[]{:S(2)}, u32[]{:S(2)}) %collective-permute-start.18) | collective-permute-done | bytes 262176 | tf_op jit(solution)/shard_map/ppermute | solution.py:282
  54.5 0.7 collective-permute-start.19
  55.1 3.2 %collective-permute-start.13 = (bf16[256,1024]{1,0:T(8,128)(2,1)S(1)}, bf16[256,1024]{1,0:T(8,128)(2,1)S(1)}, u32[]{:S(2)}, u32[]{:S(2)}) collective-permute-start(bf16[256,1024]{1,0:T(8,128)(2,1)S(1)} %collective-permute-done.11.w4), channel_id=1, source_target_pairs={{0,32},{32,64},{64,96},{96,128},{128,160},{160,192},{192,224},{224... | collective-permute-start | bytes 1572872 | tf_op jit(solution)/shard_map/ppermute | solution.py:282
  58.3 0.1 collective-permute-start.14
  58.4 1.6 %shard_map.85 = (f32[512,1024]{1,0:T(8,128)S(1)}, bf16[512,768]{1,0:T(8,128)(2,1)S(1)}) custom-call(bf16[128,2048]{1,0:T(8,128)(2,1)S(1)} %pad_maximum_fusion.gh, bf16[128,2048]{1,0:T(8,128)(2,1)S(1)} %collective-permute-done.3.gu, bf16[128,2048]{1,0:T(8,128)(2,1)S(1)} %collective-permute-done.4.gd, bf16[64,2048]{1,0:T(8,128)(2,1)S(1)} %collective-permute-done.5.gu2, ...), custom_call_target="tpu_custom_call" | custom-call | flops 10737418240 | bytes 6291456 | tf_op jit(solution)/shard_map/pallas_call | solution.py:251
  60.1 0.4 fusion.10
  60.5 0.1 collective-permute-start.20
  60.6 3.8 %collective-permute-done.13 = bf16[256,1024]{1,0:T(8,128)(2,1)S(1)} collective-permute-done((bf16[256,1024]{1,0:T(8,128)(2,1)S(1)}, bf16[256,1024]{1,0:T(8,128)(2,1)S(1)}, u32[]{:S(2)}, u32[]{:S(2)}) %collective-permute-start.13) | collective-permute-done | bytes 524320 | tf_op jit(solution)/shard_map/ppermute | solution.py:282
  64.5 0.4 fusion.8
  64.9 5.2 %collective-permute-done.14 = bf16[256,1024]{1,0:T(8,128)(2,1)S(1)} collective-permute-done((bf16[256,1024]{1,0:T(8,128)(2,1)S(1)}, bf16[256,1024]{1,0:T(8,128)(2,1)S(1)}, u32[]{:S(2)}, u32[]{:S(2)}) %collective-permute-start.14) | collective-permute-done | bytes 524320 | tf_op jit(solution)/shard_map/ppermute | solution.py:282
  70.1 0.6 add_add_fusion
  70.7 0.2 convert.4
  70.9 1.0 collective-permute-start.21
  71.9 0.1 collective-permute-start.24
  72.0 0.4 collective-permute-start.25
  72.4 0.1 collective-permute-start.22
  72.5 0.6 collective-permute-done.21
  73.1 1.2 collective-permute-start.23
  74.4 2.0 %shard_map.86 = (f32[128,1024]{1,0:T(8,128)S(1)}, f32[1,1024]{1,0:T(1,128)S(1)}, bf16[6,512,256]{2,1,0:T(8,128)(2,1)S(1)}) custom-call(s32[8]{0:T(128)S(1)} %copy-done, bf16[1024,128]{1,0:T(8,128)(2,1)S(1)} %bitcast.52, bf16[128,1024]{1,0:T(8,128)(2,1)S(1)} %maximum_select_fusion.2.plane, bf16[128,1024]{1,0:T(8,128)(2,1)S(1)} %collective-permute-done.17.r1, ...), custom_call_target="tpu_custom_call" | custom-call | flops 1 | bytes 6291456 | tf_op jit(solution)/shard_map/pallas_call | solution.py:251
  76.4 4.3 %collective-permute-done.23.o2 = bf16[128,1024]{1,0:T(8,128)(2,1)S(1)} collective-permute-done((bf16[128,1024]{1,0:T(8,128)(2,1)S(1)}, bf16[128,1024]{1,0:T(8,128)(2,1)S(1)}, u32[]{:S(2)}, u32[]{:S(2)}) %collective-permute-start.23) | collective-permute-done | bytes 262176 | tf_op jit(solution)/shard_map/ppermute | solution.py:271
  80.7 1.1 shard_map.87
  81.8 1.3 %collective-permute-start.26 = (bf16[512,256]{1,0:T(8,128)(2,1)S(1)}, bf16[512,256]{1,0:T(8,128)(2,1)S(1)}, u32[]{:S(2)}, u32[]{:S(2)}) collective-permute-start(bf16[512,256]{1,0:T(8,128)(2,1)S(1)} %get-tuple-element.33), channel_id=1, source_target_pairs={{0,8},{8,0},{1,9},{9,1},{2,10},{10,2},{3,11},{11,3},{4,12},{12,4},... | collective-permute-start | bytes 786440 | tf_op jit(solution)/shard_map/ppermute | solution.py:271
  83.1 1.2 %collective-permute-done.26 = bf16[512,256]{1,0:T(8,128)(2,1)S(1)} collective-permute-done((bf16[512,256]{1,0:T(8,128)(2,1)S(1)}, bf16[512,256]{1,0:T(8,128)(2,1)S(1)}, u32[]{:S(2)}, u32[]{:S(2)}) %collective-permute-start.26) | collective-permute-done | bytes 262176 | tf_op jit(solution)/shard_map/ppermute | solution.py:271
  84.3 0.1 collective-permute-start.27
  84.4 2.4 %shard_map.88 = (bf16[128,1024]{1,0:T(8,128)(2,1)S(1)}, bf16[512,256]{1,0:T(8,128)(2,1)S(1)}, bf16[512,256]{1,0:T(8,128)(2,1)S(1)}, bf16[512,256]{1,0:T(8,128)(2,1)S(1)}, bf16[512,256]{1,0:T(8,128)(2,1)S(1)}) custom-call(s32[8]{0:T(128)S(1)} %copy-done, bf16[1024,128]{1,0:T(8,128)(2,1)S(1)} %bitcast.54, bf16[1024,128]{1,0:T(8,128)(2,1)S(1)} %get-tuple-element.35.do, ...), custom_call_target="tpu_custom_call" | custom-call | flops 1677721600 | bytes 6291456 | tf_op jit(solution)/shard_map/pallas_call | solution.py:251
  86.8 3.3 %collective-permute-start.28 = (bf16[512,256]{1,0:T(8,128)(2,1)S(1)}, bf16[512,256]{1,0:T(8,128)(2,1)S(1)}, u32[]{:S(2)}, u32[]{:S(2)}) collective-permute-start(bf16[512,256]{1,0:T(8,128)(2,1)S(1)} %get-tuple-element.42), channel_id=1, source_target_pairs={{0,8},{8,0},{1,9},{9,1},{2,10},{10,2},{3,11},{11,3},{4,12},{12,4},... | collective-permute-start | bytes 786440 | tf_op jit(solution)/shard_map/ppermute | solution.py:271
  90.2 0.1 collective-permute-start.30
  90.3 0.6 collective-permute-done.27
  90.8 0.5 collective-permute-done.28
  91.3 0.1 add_convert_fusion
  91.4 4.3 %collective-permute-start.29 = (bf16[512,256]{1,0:T(8,128)(2,1)S(1)}, bf16[512,256]{1,0:T(8,128)(2,1)S(1)}, u32[]{:S(2)}, u32[]{:S(2)}) collective-permute-start(bf16[512,256]{1,0:T(8,128)(2,1)S(1)} %add_convert_fusion), channel_id=1, source_target_pairs={{0,224},{32,0},{64,32},{96,64},{128,96},{160,128},{192,160},{224,1... | collective-permute-start | bytes 786440 | tf_op jit(solution)/shard_map/ppermute | solution.py:282
  95.7 6.5 %collective-permute-done.29 = bf16[512,256]{1,0:T(8,128)(2,1)S(1)} collective-permute-done((bf16[512,256]{1,0:T(8,128)(2,1)S(1)}, bf16[512,256]{1,0:T(8,128)(2,1)S(1)}, u32[]{:S(2)}, u32[]{:S(2)}) %collective-permute-start.29) | collective-permute-done | bytes 262176 | tf_op jit(solution)/shard_map/ppermute | solution.py:282
  102.2 0.1 fusion
  102.3 2.1 %collective-permute-start.31 = (bf16[512,256]{1,0:T(8,128)(2,1)S(1)}, bf16[512,256]{1,0:T(8,128)(2,1)S(1)}, u32[]{:S(2)}, u32[]{:S(2)}) collective-permute-start(bf16[512,256]{1,0:T(8,128)(2,1)S(1)} %fusion), channel_id=1, source_target_pairs={{0,224},{32,0},{64,32},{96,64},{128,96},{160,128},{192,160},{224,1... | collective-permute-start | bytes 786440 | tf_op jit(solution)/shard_map/ppermute | solution.py:282
  104.4 5.7 %collective-permute-done.31 = bf16[512,256]{1,0:T(8,128)(2,1)S(1)} collective-permute-done((bf16[512,256]{1,0:T(8,128)(2,1)S(1)}, bf16[512,256]{1,0:T(8,128)(2,1)S(1)}, u32[]{:S(2)}, u32[]{:S(2)}) %collective-permute-start.31) | collective-permute-done | bytes 262176 | tf_op jit(solution)/shard_map/ppermute | solution.py:282
  110.1 0.1 add_select_fusion
  110.3 0.1 collective-permute-start.32
  110.4 1.3 %collective-permute-done.32 = bf16[256,256]{1,0:T(8,128)(2,1)S(1)} collective-permute-done((bf16[256,256]{1,0:T(8,128)(2,1)S(1)}, bf16[256,256]{1,0:T(8,128)(2,1)S(1)}, u32[]{:S(2)}, u32[]{:S(2)}) %collective-permute-start.32) | collective-permute-done | bytes 131104 | tf_op jit(solution)/shard_map/ppermute | solution.py:271
  111.8 1.4 %collective-permute-start.33 = (bf16[128,256]{1,0:T(8,128)(2,1)S(1)}, bf16[128,256]{1,0:T(8,128)(2,1)S(1)}, u32[]{:S(2)}, u32[]{:S(2)}) collective-permute-start(bf16[128,256]{1,0:T(8,128)(2,1)S(1)} %select_convert_fusion.1), channel_id=1, source_target_pairs={{0,16},{16,0},{1,17},{17,1},{2,18},{18,2},{3,19},{19,3},{4,20},{20... | collective-permute-start | bytes 196616 | tf_op jit(solution)/shard_map/ppermute | solution.py:271
  113.2 0.8 copy.15
  113.9 1.5 %collective-permute-done.33 = bf16[128,256]{1,0:T(8,128)(2,1)S(1)} collective-permute-done((bf16[128,256]{1,0:T(8,128)(2,1)S(1)}, bf16[128,256]{1,0:T(8,128)(2,1)S(1)}, u32[]{:S(2)}, u32[]{:S(2)}) %collective-permute-start.33) | collective-permute-done | bytes 65568 | tf_op jit(solution)/shard_map/ppermute | solution.py:271
  115.4 0.6 slice_bitcast_fusion.4
  (61 shorter events, 0.8 us)
Async XLA Ops:
  0.6 4.7 %copy-start.1 = (bf16[256,1024]{1,0:T(8,128)(2,1)S(1)}, bf16[256,1024]{1,0:T(8,128)(2,1)}, u32[]{:S(2)}) copy-start(bf16[256,1024]{1,0:T(8,128)(2,1)} %w0.1) | copy-start | bytes 1572868
  0.6 16.0 %copy-start.4 = (bf16[128,1,128]{2,0,1:T(8,128)(2,1)S(1)}, bf16[128,1,128]{2,0,1:T(8,128)(2,1)}, u32[]{:S(2)}) copy-start(bf16[128,1,128]{2,0,1:T(8,128)(2,1)} %param.7) | copy-start | bytes 98308
  0.7 16.0 %copy-start.3 = (bf16[128,1,128]{2,0,1:T(8,128)(2,1)S(1)}, bf16[128,1,128]{2,0,1:T(8,128)(2,1)}, u32[]{:S(2)}) copy-start(bf16[128,1,128]{2,0,1:T(8,128)(2,1)} %param.8) | copy-start | bytes 98308
  2.0 7.3 %collective-permute-start = (bf16[32,2048]{1,0:T(8,128)(2,1)S(1)}, bf16[32,2048]{1,0:T(8,128)(2,1)S(1)}, u32[]{:S(2)}, u32[]{:S(2)}) collective-permute-start(bf16[32,2048]{1,0:T(8,128)(2,1)S(1)} %bitcast.63), channel_id=1, source_target_pairs={{0,8},{8,0},{1,9},{9,1},{2,10},{10,2},{3,11},{11,3},{4,12},{12,4},... | collective-permute-start | bytes 393224 | tf_op jit(solution)/shard_map/ppermute | solution.py:271
  5.4 11.7 %collective-permute-start.8 = (bf16[256,1024]{1,0:T(8,128)(2,1)S(1)}, bf16[256,1024]{1,0:T(8,128)(2,1)S(1)}, u32[]{:S(2)}, u32[]{:S(2)}) collective-permute-start(bf16[256,1024]{1,0:T(8,128)(2,1)S(1)} %copy-done.1), channel_id=1, source_target_pairs={{0,8},{8,0},{1,9},{9,1},{2,10},{10,2},{3,11},{11,3},{4,12},{12,4},... | collective-permute-start | bytes 1572872 | tf_op jit(solution)/shard_map/ppermute | solution.py:271
  5.5 13.1 %collective-permute-start.7 = (bf16[256,1024]{1,0:T(8,128)(2,1)S(1)}, bf16[256,1024]{1,0:T(8,128)(2,1)S(1)}, u32[]{:S(2)}, u32[]{:S(2)}) collective-permute-start(bf16[256,1024]{1,0:T(8,128)(2,1)S(1)} %copy-done.1), channel_id=1, source_target_pairs={{0,32},{32,64},{64,96},{96,128},{128,160},{160,192},{192,224},{224... | collective-permute-start | bytes 1572872 | tf_op jit(solution)/shard_map/ppermute | solution.py:282
  9.4 4.2 %collective-permute-start.1 = (bf16[2,16,2048]{2,1,0:T(8,128)(2,1)S(1)}, bf16[2,16,2048]{2,1,0:T(8,128)(2,1)S(1)}, u32[]{:S(2)}, u32[]{:S(2)}) collective-permute-start(bf16[2,16,2048]{2,1,0:T(8,128)(2,1)S(1)} %fusion.12), channel_id=1, source_target_pairs={{0,16},{16,0},{1,17},{17,1},{2,18},{18,2},{3,19},{19,3},{4,20},{20... | collective-permute-start | bytes 393224 | tf_op jit(solution)/shard_map/ppermute | solution.py:271
  13.6 9.0 %collective-permute-start.2 = (bf16[64,2048]{1,0:T(8,128)(2,1)S(1)}, bf16[64,2048]{1,0:T(8,128)(2,1)S(1)}, u32[]{:S(2)}, u32[]{:S(2)}) collective-permute-start(bf16[64,2048]{1,0:T(8,128)(2,1)S(1)} %bitcast.59), channel_id=1, source_target_pairs={{0,1},{1,0},{2,3},{3,2},{4,5},{5,4},{6,7},{7,6},{8,9},{9,8},{10,11... | collective-permute-start | bytes 786440 | tf_op jit(solution)/shard_map/ppermute | solution.py:271
  16.6 8.8 %collective-permute-start.15 = (bf16[128,256]{1,0:T(8,128)(2,1)S(1)}, bf16[128,256]{1,0:T(8,128)(2,1)S(1)}, u32[]{:S(2)}, u32[]{:S(2)}) collective-permute-start(bf16[128,256]{1,0:T(8,128)(2,1)S(1)} %pad_maximum_fusion.2), channel_id=1, source_target_pairs={{0,16},{16,0},{1,17},{17,1},{2,18},{18,2},{3,19},{19,3},{4,20},{20... | collective-permute-start | bytes 196616 | tf_op jit(solution)/shard_map/ppermute | solution.py:271
  17.1 14.3 %collective-permute-start.9 = (bf16[256,1024]{1,0:T(8,128)(2,1)S(1)}, bf16[256,1024]{1,0:T(8,128)(2,1)S(1)}, u32[]{:S(2)}, u32[]{:S(2)}) collective-permute-start(bf16[256,1024]{1,0:T(8,128)(2,1)S(1)} %collective-permute-done.8), channel_id=1, source_target_pairs={{0,32},{32,64},{64,96},{96,128},{128,160},{160,192},{192,224},{224... | collective-permute-start | bytes 1572872 | tf_op jit(solution)/shard_map/ppermute | solution.py:282
  18.6 13.6 %collective-permute-start.10 = (bf16[256,1024]{1,0:T(8,128)(2,1)S(1)}, bf16[256,1024]{1,0:T(8,128)(2,1)S(1)}, u32[]{:S(2)}, u32[]{:S(2)}) collective-permute-start(bf16[256,1024]{1,0:T(8,128)(2,1)S(1)} %collective-permute-done.7.w1), channel_id=1, source_target_pairs={{0,32},{32,64},{64,96},{96,128},{128,160},{160,192},{192,224},{224... | collective-permute-start | bytes 1572872 | tf_op jit(solution)/shard_map/ppermute | solution.py:282
  22.7 20.0 %collective-permute-start.3 = (bf16[128,2048]{1,0:T(8,128)(2,1)S(1)}, bf16[128,2048]{1,0:T(8,128)(2,1)S(1)}, u32[]{:S(2)}, u32[]{:S(2)}) collective-permute-start(bf16[128,2048]{1,0:T(8,128)(2,1)S(1)} %pad_maximum_fusion.gh), channel_id=1, source_target_pairs={{0,2},{2,4},{4,6},{6,0},{1,3},{3,5},{5,7},{7,1},{8,10},{10,12},{12... | collective-permute-start | bytes 1572872 | tf_op jit(solution)/shard_map/ppermute | solution.py:275
  23.4 19.4 %collective-permute-start.4 = (bf16[128,2048]{1,0:T(8,128)(2,1)S(1)}, bf16[128,2048]{1,0:T(8,128)(2,1)S(1)}, u32[]{:S(2)}, u32[]{:S(2)}) collective-permute-start(bf16[128,2048]{1,0:T(8,128)(2,1)S(1)} %pad_maximum_fusion.gh), channel_id=1, source_target_pairs={{0,6},{2,0},{4,2},{6,4},{1,7},{3,1},{5,3},{7,5},{8,14},{10,8},{12,... | collective-permute-start | bytes 1572872 | tf_op jit(solution)/shard_map/ppermute | solution.py:275
  25.5 1.4 %collective-permute-start.16 = (bf16[128,512]{1,0:T(8,128)(2,1)S(1)}, bf16[128,512]{1,0:T(8,128)(2,1)S(1)}, u32[]{:S(2)}, u32[]{:S(2)}) collective-permute-start(bf16[128,512]{1,0:T(8,128)(2,1)S(1)} %maximum_select_fusion.3), channel_id=1, source_target_pairs={{0,8},{8,0},{1,9},{9,1},{2,10},{10,2},{3,11},{11,3},{4,12},{12,4},... | collective-permute-start | bytes 393224 | tf_op jit(solution)/shard_map/ppermute | solution.py:271
  27.0 13.4 %collective-permute-start.17 = (bf16[128,1024]{1,0:T(8,128)(2,1)S(1)}, bf16[128,1024]{1,0:T(8,128)(2,1)S(1)}, u32[]{:S(2)}, u32[]{:S(2)}) collective-permute-start(bf16[128,1024]{1,0:T(8,128)(2,1)S(1)} %maximum_select_fusion.2.plane), channel_id=1, source_target_pairs={{0,32},{32,64},{64,96},{96,128},{128,160},{160,192},{192,224},{224... | collective-permute-start | bytes 786440 | tf_op jit(solution)/shard_map/ppermute | solution.py:282
  31.4 23.7 %collective-permute-start.11 = (bf16[256,1024]{1,0:T(8,128)(2,1)S(1)}, bf16[256,1024]{1,0:T(8,128)(2,1)S(1)}, u32[]{:S(2)}, u32[]{:S(2)}) collective-permute-start(bf16[256,1024]{1,0:T(8,128)(2,1)S(1)} %collective-permute-done.9.w2), channel_id=1, source_target_pairs={{0,32},{32,64},{64,96},{96,128},{128,160},{160,192},{192,224},{224... | collective-permute-start | bytes 1572872 | tf_op jit(solution)/shard_map/ppermute | solution.py:282
  32.2 26.2 %collective-permute-start.12 = (bf16[256,1024]{1,0:T(8,128)(2,1)S(1)}, bf16[256,1024]{1,0:T(8,128)(2,1)S(1)}, u32[]{:S(2)}, u32[]{:S(2)}) collective-permute-start(bf16[256,1024]{1,0:T(8,128)(2,1)S(1)} %collective-permute-done.10.w3), channel_id=1, source_target_pairs={{0,32},{32,64},{64,96},{96,128},{128,160},{160,192},{192,224},{224... | collective-permute-start | bytes 1572872 | tf_op jit(solution)/shard_map/ppermute | solution.py:282
  40.4 14.0 %collective-permute-start.18 = (bf16[128,1024]{1,0:T(8,128)(2,1)S(1)}, bf16[128,1024]{1,0:T(8,128)(2,1)S(1)}, u32[]{:S(2)}, u32[]{:S(2)}) collective-permute-start(bf16[128,1024]{1,0:T(8,128)(2,1)S(1)} %collective-permute-done.17.r1), channel_id=1, source_target_pairs={{0,32},{32,64},{64,96},{96,128},{128,160},{160,192},{192,224},{224... | collective-permute-start | bytes 786440 | tf_op jit(solution)/shard_map/ppermute | solution.py:282
  42.7 15.8 %collective-permute-start.5 = (bf16[64,2048]{1,0:T(8,128)(2,1)S(1)}, bf16[64,2048]{1,0:T(8,128)(2,1)S(1)}, u32[]{:S(2)}, u32[]{:S(2)}) collective-permute-start(bf16[64,2048]{1,0:T(8,128)(2,1)S(1)} %slice.290), channel_id=1, source_target_pairs={{0,2},{2,4},{4,6},{6,0},{1,3},{3,5},{5,7},{7,1},{8,10},{10,12},{12... | collective-permute-start | bytes 786440 | tf_op jit(solution)/shard_map/ppermute | solution.py:275
  42.8 15.6 %collective-permute-start.6 = (bf16[64,2048]{1,0:T(8,128)(2,1)S(1)}, bf16[64,2048]{1,0:T(8,128)(2,1)S(1)}, u32[]{:S(2)}, u32[]{:S(2)}) collective-permute-start(bf16[64,2048]{1,0:T(8,128)(2,1)S(1)} %slice.291), channel_id=1, source_target_pairs={{0,6},{2,0},{4,2},{6,4},{1,7},{3,1},{5,3},{7,5},{8,14},{10,8},{12,... | collective-permute-start | bytes 786440 | tf_op jit(solution)/shard_map/ppermute | solution.py:275
  54.5 6.1 %collective-permute-start.19 = (bf16[128,1024]{1,0:T(8,128)(2,1)S(1)}, bf16[128,1024]{1,0:T(8,128)(2,1)S(1)}, u32[]{:S(2)}, u32[]{:S(2)}) collective-permute-start(bf16[128,1024]{1,0:T(8,128)(2,1)S(1)} %collective-permute-done.18.r2), channel_id=1, source_target_pairs={{0,32},{32,64},{64,96},{96,128},{128,160},{160,192},{192,224},{224... | collective-permute-start | bytes 786440 | tf_op jit(solution)/shard_map/ppermute | solution.py:282
  55.1 9.3 %collective-permute-start.13 = (bf16[256,1024]{1,0:T(8,128)(2,1)S(1)}, bf16[256,1024]{1,0:T(8,128)(2,1)S(1)}, u32[]{:S(2)}, u32[]{:S(2)}) collective-permute-start(bf16[256,1024]{1,0:T(8,128)(2,1)S(1)} %collective-permute-done.11.w4), channel_id=1, source_target_pairs={{0,32},{32,64},{64,96},{96,128},{128,160},{160,192},{192,224},{224... | collective-permute-start | bytes 1572872 | tf_op jit(solution)/shard_map/ppermute | solution.py:282
  58.3 11.7 %collective-permute-start.14 = (bf16[256,1024]{1,0:T(8,128)(2,1)S(1)}, bf16[256,1024]{1,0:T(8,128)(2,1)S(1)}, u32[]{:S(2)}, u32[]{:S(2)}) collective-permute-start(bf16[256,1024]{1,0:T(8,128)(2,1)S(1)} %collective-permute-done.12), channel_id=1, source_target_pairs={{0,32},{32,64},{64,96},{96,128},{128,160},{160,192},{192,224},{224... | collective-permute-start | bytes 1572872 | tf_op jit(solution)/shard_map/ppermute | solution.py:282
  60.5 10.3 %collective-permute-start.20 = (bf16[128,1024]{1,0:T(8,128)(2,1)S(1)}, bf16[128,1024]{1,0:T(8,128)(2,1)S(1)}, u32[]{:S(2)}, u32[]{:S(2)}) collective-permute-start(bf16[128,1024]{1,0:T(8,128)(2,1)S(1)} %collective-permute-done.19.r3), channel_id=1, source_target_pairs={{0,8},{8,0},{1,9},{9,1},{2,10},{10,2},{3,11},{11,3},{4,12},{12,4},... | collective-permute-start | bytes 786440 | tf_op jit(solution)/shard_map/ppermute | solution.py:271
  70.6 3.6 %copy-start.2 = (bf16[128,8,128]{2,1,0:T(8,128)(2,1)S(1)}, bf16[128,8,128]{2,1,0:T(8,128)(2,1)}, u32[]{:S(2)}) copy-start(bf16[128,8,128]{2,1,0:T(8,128)(2,1)} %param.6) | copy-start | bytes 786436
  70.8 3.5 %copy-start = (s32[8]{0:T(128)S(1)}, s32[8]{0:T(128)}, u32[]{:S(2)}) copy-start(s32[8]{0:T(128)} %lengths.5) | copy-start | bytes 100
  70.9 2.1 %collective-permute-start.21 = (bf16[128,1024]{1,0:T(8,128)(2,1)S(1)}, bf16[128,1024]{1,0:T(8,128)(2,1)S(1)}, u32[]{:S(2)}, u32[]{:S(2)}) collective-permute-start(bf16[128,1024]{1,0:T(8,128)(2,1)S(1)} %get-tuple-element.27), channel_id=1, source_target_pairs={{0,8},{8,0},{1,9},{9,1},{2,10},{10,2},{3,11},{11,3},{4,12},{12,4},... | collective-permute-start | bytes 786440 | tf_op jit(solution)/shard_map/ppermute | solution.py:271
  71.9 2.5 %collective-permute-start.24 = (bf16[128,1024]{1,0:T(8,128)(2,1)S(1)}, bf16[128,1024]{1,0:T(8,128)(2,1)S(1)}, u32[]{:S(2)}, u32[]{:S(2)}) collective-permute-start(bf16[128,1024]{1,0:T(8,128)(2,1)S(1)} %collective-permute-done.17.r1), channel_id=1, source_target_pairs={{0,8},{8,0},{1,9},{9,1},{2,10},{10,2},{3,11},{11,3},{4,12},{12,4},... | collective-permute-start | bytes 786440 | tf_op jit(solution)/shard_map/ppermute | solution.py:271
  72.0 2.4 %collective-permute-start.25 = (bf16[128,1024]{1,0:T(8,128)(2,1)S(1)}, bf16[128,1024]{1,0:T(8,128)(2,1)S(1)}, u32[]{:S(2)}, u32[]{:S(2)}) collective-permute-start(bf16[128,1024]{1,0:T(8,128)(2,1)S(1)} %collective-permute-done.18.r2), channel_id=1, source_target_pairs={{0,8},{8,0},{1,9},{9,1},{2,10},{10,2},{3,11},{11,3},{4,12},{12,4},... | collective-permute-start | bytes 786440 | tf_op jit(solution)/shard_map/ppermute | solution.py:271
  72.4 4.0 %collective-permute-start.22 = (bf16[128,1024]{1,0:T(8,128)(2,1)S(1)}, bf16[128,1024]{1,0:T(8,128)(2,1)S(1)}, u32[]{:S(2)}, u32[]{:S(2)}) collective-permute-start(bf16[128,1024]{1,0:T(8,128)(2,1)S(1)} %get-tuple-element.45), channel_id=1, source_target_pairs={{0,8},{8,0},{1,9},{9,1},{2,10},{10,2},{3,11},{11,3},{4,12},{12,4},... | collective-permute-start | bytes 786440 | tf_op jit(solution)/shard_map/ppermute | solution.py:271
  73.1 7.6 %collective-permute-start.23 = (bf16[128,1024]{1,0:T(8,128)(2,1)S(1)}, bf16[128,1024]{1,0:T(8,128)(2,1)S(1)}, u32[]{:S(2)}, u32[]{:S(2)}) collective-permute-start(bf16[128,1024]{1,0:T(8,128)(2,1)S(1)} %fusion.2), channel_id=1, source_target_pairs={{0,16},{16,0},{1,17},{17,1},{2,18},{18,2},{3,19},{19,3},{4,20},{20... | collective-permute-start | bytes 786440 | tf_op jit(solution)/shard_map/ppermute | solution.py:271
  81.8 2.5 %collective-permute-start.26 = (bf16[512,256]{1,0:T(8,128)(2,1)S(1)}, bf16[512,256]{1,0:T(8,128)(2,1)S(1)}, u32[]{:S(2)}, u32[]{:S(2)}) collective-permute-start(bf16[512,256]{1,0:T(8,128)(2,1)S(1)} %get-tuple-element.33), channel_id=1, source_target_pairs={{0,8},{8,0},{1,9},{9,1},{2,10},{10,2},{3,11},{11,3},{4,12},{12,4},... | collective-permute-start | bytes 786440 | tf_op jit(solution)/shard_map/ppermute | solution.py:271
  84.3 6.5 %collective-permute-start.27 = (bf16[512,256]{1,0:T(8,128)(2,1)S(1)}, bf16[512,256]{1,0:T(8,128)(2,1)S(1)}, u32[]{:S(2)}, u32[]{:S(2)}) collective-permute-start(bf16[512,256]{1,0:T(8,128)(2,1)S(1)} %add_convert_fusion.1), channel_id=1, source_target_pairs={{0,224},{32,0},{64,32},{96,64},{128,96},{160,128},{192,160},{224,1... | collective-permute-start | bytes 786440 | tf_op jit(solution)/shard_map/ppermute | solution.py:282
  86.8 4.5 %collective-permute-start.28 = (bf16[512,256]{1,0:T(8,128)(2,1)S(1)}, bf16[512,256]{1,0:T(8,128)(2,1)S(1)}, u32[]{:S(2)}, u32[]{:S(2)}) collective-permute-start(bf16[512,256]{1,0:T(8,128)(2,1)S(1)} %get-tuple-element.42), channel_id=1, source_target_pairs={{0,8},{8,0},{1,9},{9,1},{2,10},{10,2},{3,11},{11,3},{4,12},{12,4},... | collective-permute-start | bytes 786440 | tf_op jit(solution)/shard_map/ppermute | solution.py:271
  90.2 5.5 %collective-permute-start.30 = (bf16[512,256]{1,0:T(8,128)(2,1)S(1)}, bf16[512,256]{1,0:T(8,128)(2,1)S(1)}, u32[]{:S(2)}, u32[]{:S(2)}) collective-permute-start(bf16[512,256]{1,0:T(8,128)(2,1)S(1)} %get-tuple-element.44), channel_id=1, source_target_pairs={{0,8},{8,0},{1,9},{9,1},{2,10},{10,2},{3,11},{11,3},{4,12},{12,4},... | collective-permute-start | bytes 786440 | tf_op jit(solution)/shard_map/ppermute | solution.py:271
  91.4 10.8 %collective-permute-start.29 = (bf16[512,256]{1,0:T(8,128)(2,1)S(1)}, bf16[512,256]{1,0:T(8,128)(2,1)S(1)}, u32[]{:S(2)}, u32[]{:S(2)}) collective-permute-start(bf16[512,256]{1,0:T(8,128)(2,1)S(1)} %add_convert_fusion), channel_id=1, source_target_pairs={{0,224},{32,0},{64,32},{96,64},{128,96},{160,128},{192,160},{224,1... | collective-permute-start | bytes 786440 | tf_op jit(solution)/shard_map/ppermute | solution.py:282
  102.3 7.8 %collective-permute-start.31 = (bf16[512,256]{1,0:T(8,128)(2,1)S(1)}, bf16[512,256]{1,0:T(8,128)(2,1)S(1)}, u32[]{:S(2)}, u32[]{:S(2)}) collective-permute-start(bf16[512,256]{1,0:T(8,128)(2,1)S(1)} %fusion), channel_id=1, source_target_pairs={{0,224},{32,0},{64,32},{96,64},{128,96},{160,128},{192,160},{224,1... | collective-permute-start | bytes 786440 | tf_op jit(solution)/shard_map/ppermute | solution.py:282
  110.3 1.4 %collective-permute-start.32 = (bf16[256,256]{1,0:T(8,128)(2,1)S(1)}, bf16[256,256]{1,0:T(8,128)(2,1)S(1)}, u32[]{:S(2)}, u32[]{:S(2)}) collective-permute-start(bf16[256,256]{1,0:T(8,128)(2,1)S(1)} %select_convert_fusion), channel_id=1, source_target_pairs={{0,8},{8,0},{1,9},{9,1},{2,10},{10,2},{3,11},{11,3},{4,12},{12,4},... | collective-permute-start | bytes 393224 | tf_op jit(solution)/shard_map/ppermute | solution.py:271
  111.8 3.6 %collective-permute-start.33 = (bf16[128,256]{1,0:T(8,128)(2,1)S(1)}, bf16[128,256]{1,0:T(8,128)(2,1)S(1)}, u32[]{:S(2)}, u32[]{:S(2)}) collective-permute-start(bf16[128,256]{1,0:T(8,128)(2,1)S(1)} %select_convert_fusion.1), channel_id=1, source_target_pairs={{0,16},{16,0},{1,17},{17,1},{2,18},{18,2},{3,19},{19,3},{4,20},{20... | collective-permute-start | bytes 196616 | tf_op jit(solution)/shard_map/ppermute | solution.py:271

commit v3 on v2

--- a/solution.py
+++ b/solution.py
@@ -18,7 +18,7 @@
 ROWS = 1024
 MIB = 1024 * 1024
 P_MIB, F_MIB, B_MIB = 16, 20, 24
-HINT = 8
+HINT = 0
 
 NT = (((1,), (1,)), ((), ()))
 NN = (((1,), (0,)), ((), ()))
@@ -309,6 +309,8 @@
     t = swap(jnp.where(first, sent[1::2], sent[0::2]).reshape(32, 2048), "c")
     own = jnp.where(first, sent[0::2], sent[1::2]).reshape(32, 2048)
     both = jnp.where(first, jnp.stack([own, t]), jnp.stack([t, own])).reshape(2, 2, 16, 2048)
+    q0 = swap(out_weight, "c")
+    both, q0 = tie(both, q0)
     away = swap(jnp.where(yl == 0, both[:, 1], both[:, 0]), "yl")
     here = jnp.where(yl == 0, both[:, 0], both[:, 1])
     got = jnp.where(yl == 0, jnp.stack([here, away]), jnp.stack([away, here])).reshape(64, 2048)
@@ -317,7 +319,6 @@
     gu2, gd2 = turn(gu[:64], 1), turn(gd[64:], 3)
 
     p1 = along_z(out_weight, 1, 7)
-    q0 = swap(out_weight, "c")
     kv = jnp.concatenate([key_states.reshape(128, HD), value_vectors.reshape(128, HD)], axis=1)
     other = swap(kv, "yl")
     half = jnp.where(

time: 116 us -> 109 us (0.940)
  waiting for transfers between devices: 54.2 us -> 42.8 us
  starting transfers between devices: 48.4 us -> 51.9 us
    ppermute x13, waiting for transfers between devices: 37.2 us -> 30.1 us  [along_z(): return lax.ppermute(x, ('z', 'c'), pairs)]
    ppermute x13, starting transfers between devices: 25.2 us -> 29.8 us  [along_z(): return lax.ppermute(x, ('z', 'c'), pairs)]
    ppermute x17, waiting for transfers between devices: 17 us -> 12.7 us  [swap(): return lax.ppermute(x, axis, [(0, 1), (1, 0)])]
  transfers between devices with their start and end apart: 34 -> 34, of which waited for: 16 -> 14; matrix products, arithmetic and copies ran while one was open for 2% -> 4% of each run, Pallas kernels for 5% -> 6%
where the time goes in v3:
time: 109 us; the launch traced here: 108 us
  starting transfers between devices  51.9 us (48%)
  waiting for transfers between devices  42.8 us (39%)
  Pallas kernels  7.18 us (7%)
  other arithmetic  2.16 us (2%)
  local copies, waits for them, and re-layouts  1.61 us (1%)
  matrix products  1.43 us (1%)
  between operations  1.1 us (1%)
    ppermute x13, waiting for transfers between devices, along_z(): return lax.ppermute(x, ('z', 'c'), pairs)  30.1 us
    ppermute x13, starting transfers between devices, along_z(): return lax.ppermute(x, ('z', 'c'), pairs)  29.8 us
    ppermute x17, starting transfers between devices, swap(): return lax.ppermute(x, axis, [(0, 1), (1, 0)])  16.3 us
    ppermute x17, waiting for transfers between devices, swap(): return lax.ppermute(x, axis, [(0, 1), (1, 0)])  12.7 us
    pallas_call x4, Pallas kernels, call(): pl.pallas_call(kernel, out_shape=outs, in_specs=first + [vmem] * len(args...  7.18 us
    ppermute x4, starting transfers between devices, turn(): return lax.ppermute(x, 'x', [(i, (i + step) % 4) for i in range(4)])  5.77 us
  transfers between devices with their start and end apart: 34, of which 14 were waited for; matrix products, arithmetic and copies ran while one was open for 4% of the time, Pallas kernels for 6%

profile of v3, /device:TPU:1, one launch (start us, length us, event | category | flops | bytes accessed | tf_op | source)
XLA Modules:
  0.0 108.2 jit_solution(17977146189713761487)
XLA Ops:
  0.7 3.3 %collective-permute-start.1 = (bf16[256,1024]{1,0:T(8,128)(2,1)}, bf16[256,1024]{1,0:T(8,128)(2,1)S(1)}, u32[]{:S(2)}, u32[]{:S(2)}) collective-permute-start(bf16[256,1024]{1,0:T(8,128)(2,1)} %w0.1), channel_id=1, source_target_pairs={{0,8},{8,0},{1,9},{9,1},{2,10},{10,2},{3,11},{11,3},{4,12},{12,4},... | collective-permute-start | bytes 1572872 | tf_op jit(solution)/shard_map/ppermute | solution.py:271
  4.0 1.1 %fusion.3 = bf16[16,8192]{1,0:T(8,128)(2,1)S(1)} fusion(s32[]{:T(128)S(6)} %select_n.115, bf16[16,8192]{1,0:T(8,128)(2,1)} %param.9), kind=kLoop, calls=%fused_computation.14 | loop fusion | flops 524288 | bytes 524292 | tf_op jit(solution)/shard_map/concatenate | solution.py:294
  5.3 0.2 collective-permute-start
  5.5 3.9 %collective-permute-start.8 = (bf16[256,1024]{1,0:T(8,128)(2,1)S(1)}, bf16[256,1024]{1,0:T(8,128)(2,1)S(1)}, u32[]{:S(2)}, u32[]{:S(2)}) collective-permute-start(bf16[256,1024]{1,0:T(8,128)(2,1)S(1)} %copy-done), channel_id=1, source_target_pairs={{0,32},{32,64},{64,96},{96,128},{128,160},{160,192},{192,224},{224... | collective-permute-start | bytes 1572872 | tf_op jit(solution)/shard_map/ppermute | solution.py:282
  9.4 1.4 %collective-permute-start.15 = (bf16[128,256]{1,0:T(8,128)(2,1)S(1)}, bf16[128,256]{1,0:T(8,128)(2,1)S(1)}, u32[]{:S(2)}, u32[]{:S(2)}) collective-permute-start(bf16[128,256]{1,0:T(8,128)(2,1)S(1)} %pad_maximum_fusion.2), channel_id=1, source_target_pairs={{0,16},{16,0},{1,17},{17,1},{2,18},{18,2},{3,19},{19,3},{4,20},{20... | collective-permute-start | bytes 196616 | tf_op jit(solution)/shard_map/ppermute | solution.py:271
  10.8 0.3 collective-permute-start.2
  11.1 1.0 collective-permute-start.9
  12.2 2.9 %collective-permute-done.2 = bf16[2,16,2048]{2,1,0:T(8,128)(2,1)S(1)} collective-permute-done((bf16[2,16,2048]{2,1,0:T(8,128)(2,1)S(1)}, bf16[2,16,2048]{2,1,0:T(8,128)(2,1)S(1)}, u32[]{:S(2)}, u32[]{:S(2)}) %collective-permute-start.2) | collective-permute-done | bytes 131104 | tf_op jit(solution)/shard_map/ppermute | solution.py:271
  15.1 2.7 %collective-permute-start.3 = (bf16[64,2048]{1,0:T(8,128)(2,1)S(1)}, bf16[64,2048]{1,0:T(8,128)(2,1)S(1)}, u32[]{:S(2)}, u32[]{:S(2)}) collective-permute-start(bf16[64,2048]{1,0:T(8,128)(2,1)S(1)} %bitcast.57), channel_id=1, source_target_pairs={{0,1},{1,0},{2,3},{3,2},{4,5},{5,4},{6,7},{7,6},{8,9},{9,8},{10,11... | collective-permute-start | bytes 786440 | tf_op jit(solution)/shard_map/ppermute | solution.py:271
  17.8 0.1 collective-permute-start.16
  17.9 3.0 %collective-permute-start.10 = (bf16[256,1024]{1,0:T(8,128)(2,1)S(1)}, bf16[256,1024]{1,0:T(8,128)(2,1)S(1)}, u32[]{:S(2)}, u32[]{:S(2)}) collective-permute-start(bf16[256,1024]{1,0:T(8,128)(2,1)S(1)} %collective-permute-done.8.w1), channel_id=1, source_target_pairs={{0,32},{32,64},{64,96},{96,128},{128,160},{160,192},{192,224},{224... | collective-permute-start | bytes 1572872 | tf_op jit(solution)/shard_map/ppermute | solution.py:282
  20.9 0.1 maximum_select_fusion.2.plane
  21.0 2.4 %collective-permute-start.17 = (bf16[128,1024]{1,0:T(8,128)(2,1)S(1)}, bf16[128,1024]{1,0:T(8,128)(2,1)S(1)}, u32[]{:S(2)}, u32[]{:S(2)}) collective-permute-start(bf16[128,1024]{1,0:T(8,128)(2,1)S(1)} %maximum_select_fusion.2.plane), channel_id=1, source_target_pairs={{0,32},{32,64},{64,96},{96,128},{128,160},{160,192},{192,224},{224... | collective-permute-start | bytes 786440 | tf_op jit(solution)/shard_map/ppermute | solution.py:282
  23.5 1.3 %collective-permute-start.4 = (bf16[128,2048]{1,0:T(8,128)(2,1)S(1)}, bf16[128,2048]{1,0:T(8,128)(2,1)S(1)}, u32[]{:S(2)}, u32[]{:S(2)}) collective-permute-start(bf16[128,2048]{1,0:T(8,128)(2,1)S(1)} %pad_maximum_fusion.gh), channel_id=1, source_target_pairs={{0,2},{2,4},{4,6},{6,0},{1,3},{3,5},{5,7},{7,1},{8,10},{10,12},{12... | collective-permute-start | bytes 1572872 | tf_op jit(solution)/shard_map/ppermute | solution.py:275
  24.8 1.5 %collective-permute-start.5 = (bf16[128,2048]{1,0:T(8,128)(2,1)S(1)}, bf16[128,2048]{1,0:T(8,128)(2,1)S(1)}, u32[]{:S(2)}, u32[]{:S(2)}) collective-permute-start(bf16[128,2048]{1,0:T(8,128)(2,1)S(1)} %pad_maximum_fusion.gh), channel_id=1, source_target_pairs={{0,6},{2,0},{4,2},{6,4},{1,7},{3,1},{5,3},{7,5},{8,14},{10,8},{12,... | collective-permute-start | bytes 1572872 | tf_op jit(solution)/shard_map/ppermute | solution.py:275
  26.3 2.1 %collective-permute-start.11 = (bf16[256,1024]{1,0:T(8,128)(2,1)S(1)}, bf16[256,1024]{1,0:T(8,128)(2,1)S(1)}, u32[]{:S(2)}, u32[]{:S(2)}) collective-permute-start(bf16[256,1024]{1,0:T(8,128)(2,1)S(1)} %collective-permute-done.9.w2), channel_id=1, source_target_pairs={{0,32},{32,64},{64,96},{96,128},{128,160},{160,192},{192,224},{224... | collective-permute-start | bytes 1572872 | tf_op jit(solution)/shard_map/ppermute | solution.py:282
  28.3 7.2 %collective-permute-done.17.r1 = bf16[128,1024]{1,0:T(8,128)(2,1)S(1)} collective-permute-done((bf16[128,1024]{1,0:T(8,128)(2,1)S(1)}, bf16[128,1024]{1,0:T(8,128)(2,1)S(1)}, u32[]{:S(2)}, u32[]{:S(2)}) %collective-permute-start.17) | collective-permute-done | bytes 262176 | tf_op jit(solution)/shard_map/ppermute | solution.py:282
  35.5 2.7 %collective-permute-start.12 = (bf16[256,1024]{1,0:T(8,128)(2,1)S(1)}, bf16[256,1024]{1,0:T(8,128)(2,1)S(1)}, u32[]{:S(2)}, u32[]{:S(2)}) collective-permute-start(bf16[256,1024]{1,0:T(8,128)(2,1)S(1)} %collective-permute-done.10.w3), channel_id=1, source_target_pairs={{0,32},{32,64},{64,96},{96,128},{128,160},{160,192},{192,224},{224... | collective-permute-start | bytes 1572872 | tf_op jit(solution)/shard_map/ppermute | solution.py:282
  38.2 6.3 %collective-permute-done.18.r2 = bf16[128,1024]{1,0:T(8,128)(2,1)S(1)} collective-permute-done((bf16[128,1024]{1,0:T(8,128)(2,1)S(1)}, bf16[128,1024]{1,0:T(8,128)(2,1)S(1)}, u32[]{:S(2)}, u32[]{:S(2)}) %collective-permute-start.18) | collective-permute-done | bytes 262176 | tf_op jit(solution)/shard_map/ppermute | solution.py:282
  44.4 0.7 collective-permute-start.19
  45.2 1.2 %collective-permute-start.6 = (bf16[64,2048]{1,0:T(8,128)(2,1)S(1)}, bf16[64,2048]{1,0:T(8,128)(2,1)S(1)}, u32[]{:S(2)}, u32[]{:S(2)}) collective-permute-start(bf16[64,2048]{1,0:T(8,128)(2,1)S(1)} %slice.289), channel_id=1, source_target_pairs={{0,2},{2,4},{4,6},{6,0},{1,3},{3,5},{5,7},{7,1},{8,10},{10,12},{12... | collective-permute-start | bytes 786440 | tf_op jit(solution)/shard_map/ppermute | solution.py:275
  46.4 1.8 %collective-permute-start.7 = (bf16[64,2048]{1,0:T(8,128)(2,1)S(1)}, bf16[64,2048]{1,0:T(8,128)(2,1)S(1)}, u32[]{:S(2)}, u32[]{:S(2)}) collective-permute-start(bf16[64,2048]{1,0:T(8,128)(2,1)S(1)} %slice.290), channel_id=1, source_target_pairs={{0,6},{2,0},{4,2},{6,4},{1,7},{3,1},{5,3},{7,5},{8,14},{10,8},{12,... | collective-permute-start | bytes 786440 | tf_op jit(solution)/shard_map/ppermute | solution.py:275
  48.2 2.6 %collective-permute-start.13 = (bf16[256,1024]{1,0:T(8,128)(2,1)S(1)}, bf16[256,1024]{1,0:T(8,128)(2,1)S(1)}, u32[]{:S(2)}, u32[]{:S(2)}) collective-permute-start(bf16[256,1024]{1,0:T(8,128)(2,1)S(1)} %collective-permute-done.11.w4), channel_id=1, source_target_pairs={{0,32},{32,64},{64,96},{96,128},{128,160},{160,192},{192,224},{224... | collective-permute-start | bytes 1572872 | tf_op jit(solution)/shard_map/ppermute | solution.py:282
  50.8 2.2 %collective-permute-start.14 = (bf16[256,1024]{1,0:T(8,128)(2,1)S(1)}, bf16[256,1024]{1,0:T(8,128)(2,1)S(1)}, u32[]{:S(2)}, u32[]{:S(2)}) collective-permute-start(bf16[256,1024]{1,0:T(8,128)(2,1)S(1)} %collective-permute-done.12), channel_id=1, source_target_pairs={{0,32},{32,64},{64,96},{96,128},{128,160},{160,192},{192,224},{224... | collective-permute-start | bytes 1572872 | tf_op jit(solution)/shard_map/ppermute | solution.py:282
  53.0 1.6 %shard_map.85 = (f32[512,1024]{1,0:T(8,128)S(1)}, bf16[512,768]{1,0:T(8,128)(2,1)S(1)}) custom-call(bf16[128,2048]{1,0:T(8,128)(2,1)S(1)} %pad_maximum_fusion.gh, bf16[128,2048]{1,0:T(8,128)(2,1)S(1)} %collective-permute-done.4.gu, bf16[128,2048]{1,0:T(8,128)(2,1)S(1)} %collective-permute-done.5.gd, bf16[64,2048]{1,0:T(8,128)(2,1)S(1)} %collective-permute-done.6.gu2, ...), custom_call_target="tpu_custom_call" | custom-call | bytes 6291456 | tf_op jit(solution)/shard_map/pallas_call | solution.py:251
  54.6 0.4 fusion.7
  55.1 1.9 %collective-permute-done.13 = bf16[256,1024]{1,0:T(8,128)(2,1)S(1)} collective-permute-done((bf16[256,1024]{1,0:T(8,128)(2,1)S(1)}, bf16[256,1024]{1,0:T(8,128)(2,1)S(1)}, u32[]{:S(2)}, u32[]{:S(2)}) %collective-permute-start.13) | collective-permute-done | bytes 524320 | tf_op jit(solution)/shard_map/ppermute | solution.py:282
  56.9 0.4 fusion.5
  57.4 5.2 %collective-permute-done.14 = bf16[256,1024]{1,0:T(8,128)(2,1)S(1)} collective-permute-done((bf16[256,1024]{1,0:T(8,128)(2,1)S(1)}, bf16[256,1024]{1,0:T(8,128)(2,1)S(1)}, u32[]{:S(2)}, u32[]{:S(2)}) %collective-permute-start.14) | collective-permute-done | bytes 524320 | tf_op jit(solution)/shard_map/ppermute | solution.py:282
  62.5 0.6 add_add_fusion
  63.1 0.0 copy-start.2
  63.1 0.2 convert.4
  63.3 0.1 collective-permute-start.21
  63.4 0.5 collective-permute-start.24
  63.9 0.1 collective-permute-start.25
  64.0 0.4 collective-permute-start.22
  64.4 0.5 collective-permute-done.21
  65.0 0.1 fusion.2
  65.0 1.1 collective-permute-start.23
  66.2 2.0 %shard_map.86 = (f32[128,1024]{1,0:T(8,128)S(1)}, f32[1,1024]{1,0:T(1,128)S(1)}, bf16[6,512,256]{2,1,0:T(8,128)(2,1)S(1)}) custom-call(s32[8]{0:T(128)S(1)} %copy-done.1, bf16[1024,128]{1,0:T(8,128)(2,1)S(1)} %bitcast.50, bf16[128,1024]{1,0:T(8,128)(2,1)S(1)} %maximum_select_fusion.2.plane, bf16[128,1024]{1,0:T(8,128)(2,1)S(1)} %collective-permute-done.17.r1, ...), custom_call_target="tpu_custom_call" | custom-call | flops 1 | bytes 6291456 | tf_op jit(solution)/shard_map/pallas_call | solution.py:251
  68.3 4.6 %collective-permute-done.23.o2 = bf16[128,1024]{1,0:T(8,128)(2,1)S(1)} collective-permute-done((bf16[128,1024]{1,0:T(8,128)(2,1)S(1)}, bf16[128,1024]{1,0:T(8,128)(2,1)S(1)}, u32[]{:S(2)}, u32[]{:S(2)}) %collective-permute-start.23) | collective-permute-done | bytes 262176 | tf_op jit(solution)/shard_map/ppermute | solution.py:271
  72.9 1.1 shard_map.87
  74.0 1.0 collective-permute-start.26
  75.0 1.2 %collective-permute-done.26 = bf16[512,256]{1,0:T(8,128)(2,1)S(1)} collective-permute-done((bf16[512,256]{1,0:T(8,128)(2,1)S(1)}, bf16[512,256]{1,0:T(8,128)(2,1)S(1)}, u32[]{:S(2)}, u32[]{:S(2)}) %collective-permute-start.26) | collective-permute-done | bytes 262176 | tf_op jit(solution)/shard_map/ppermute | solution.py:271
  76.2 0.1 add_convert_fusion.1
  76.2 0.9 collective-permute-start.27
  77.1 2.4 %shard_map.88 = (bf16[128,1024]{1,0:T(8,128)(2,1)S(1)}, bf16[512,256]{1,0:T(8,128)(2,1)S(1)}, bf16[512,256]{1,0:T(8,128)(2,1)S(1)}, bf16[512,256]{1,0:T(8,128)(2,1)S(1)}, bf16[512,256]{1,0:T(8,128)(2,1)S(1)}) custom-call(s32[8]{0:T(128)S(1)} %copy-done.1, bf16[1024,128]{1,0:T(8,128)(2,1)S(1)} %bitcast.52, bf16[1024,128]{1,0:T(8,128)(2,1)S(1)} %get-tuple-element.39.do, ...), custom_call_target="tpu_custom_call" | custom-call | flops 1677721600 | bytes 6291456 | tf_op jit(solution)/shard_map/pallas_call | solution.py:251
  79.5 3.1 %collective-permute-start.28 = (bf16[512,256]{1,0:T(8,128)(2,1)S(1)}, bf16[512,256]{1,0:T(8,128)(2,1)S(1)}, u32[]{:S(2)}, u32[]{:S(2)}) collective-permute-start(bf16[512,256]{1,0:T(8,128)(2,1)S(1)} %get-tuple-element.46), channel_id=1, source_target_pairs={{0,8},{8,0},{1,9},{9,1},{2,10},{10,2},{3,11},{11,3},{4,12},{12,4},... | collective-permute-start | bytes 786440 | tf_op jit(solution)/shard_map/ppermute | solution.py:271
  82.6 0.1 collective-permute-start.30
  82.7 0.5 collective-permute-done.27
  83.2 0.6 collective-permute-done.28
  83.8 0.1 add_convert_fusion
  83.9 6.2 %collective-permute-start.29 = (bf16[512,256]{1,0:T(8,128)(2,1)S(1)}, bf16[512,256]{1,0:T(8,128)(2,1)S(1)}, u32[]{:S(2)}, u32[]{:S(2)}) collective-permute-start(bf16[512,256]{1,0:T(8,128)(2,1)S(1)} %add_convert_fusion), channel_id=1, source_target_pairs={{0,224},{32,0},{64,32},{96,64},{128,96},{160,128},{192,160},{224,1... | collective-permute-start | bytes 786440 | tf_op jit(solution)/shard_map/ppermute | solution.py:282
  90.1 4.9 %collective-permute-done.29 = bf16[512,256]{1,0:T(8,128)(2,1)S(1)} collective-permute-done((bf16[512,256]{1,0:T(8,128)(2,1)S(1)}, bf16[512,256]{1,0:T(8,128)(2,1)S(1)}, u32[]{:S(2)}, u32[]{:S(2)}) %collective-permute-start.29) | collective-permute-done | bytes 262176 | tf_op jit(solution)/shard_map/ppermute | solution.py:282
  94.9 0.1 fusion
  95.1 2.2 %collective-permute-start.31 = (bf16[512,256]{1,0:T(8,128)(2,1)S(1)}, bf16[512,256]{1,0:T(8,128)(2,1)S(1)}, u32[]{:S(2)}, u32[]{:S(2)}) collective-permute-start(bf16[512,256]{1,0:T(8,128)(2,1)S(1)} %fusion), channel_id=1, source_target_pairs={{0,224},{32,0},{64,32},{96,64},{128,96},{160,128},{192,160},{224,1... | collective-permute-start | bytes 786440 | tf_op jit(solution)/shard_map/ppermute | solution.py:282
  97.3 4.3 %collective-permute-done.31 = bf16[512,256]{1,0:T(8,128)(2,1)S(1)} collective-permute-done((bf16[512,256]{1,0:T(8,128)(2,1)S(1)}, bf16[512,256]{1,0:T(8,128)(2,1)S(1)}, u32[]{:S(2)}, u32[]{:S(2)}) %collective-permute-start.31) | collective-permute-done | bytes 262176 | tf_op jit(solution)/shard_map/ppermute | solution.py:282
  101.6 0.1 add_select_fusion
  101.7 0.1 collective-permute-start.32
  101.8 1.3 %collective-permute-done.32 = bf16[256,256]{1,0:T(8,128)(2,1)S(1)} collective-permute-done((bf16[256,256]{1,0:T(8,128)(2,1)S(1)}, bf16[256,256]{1,0:T(8,128)(2,1)S(1)}, u32[]{:S(2)}, u32[]{:S(2)}) %collective-permute-start.32) | collective-permute-done | bytes 131104 | tf_op jit(solution)/shard_map/ppermute | solution.py:271
  103.2 2.0 %collective-permute-start.33 = (bf16[128,256]{1,0:T(8,128)(2,1)S(1)}, bf16[128,256]{1,0:T(8,128)(2,1)S(1)}, u32[]{:S(2)}, u32[]{:S(2)}) collective-permute-start(bf16[128,256]{1,0:T(8,128)(2,1)S(1)} %select_convert_fusion.1), channel_id=1, source_target_pairs={{0,16},{16,0},{1,17},{17,1},{2,18},{18,2},{3,19},{19,3},{4,20},{20... | collective-permute-start | bytes 196616 | tf_op jit(solution)/shard_map/ppermute | solution.py:271
  105.2 0.8 copy.14
  105.9 1.6 %collective-permute-done.33 = bf16[128,256]{1,0:T(8,128)(2,1)S(1)} collective-permute-done((bf16[128,256]{1,0:T(8,128)(2,1)S(1)}, bf16[128,256]{1,0:T(8,128)(2,1)S(1)}, u32[]{:S(2)}, u32[]{:S(2)}) %collective-permute-start.33) | collective-permute-done | bytes 65568 | tf_op jit(solution)/shard_map/ppermute | solution.py:271
  107.5 0.6 slice_bitcast_fusion.4
  (61 shorter events, 0.6 us)
Async XLA Ops:
  0.6 4.8 %copy-start = (bf16[256,1024]{1,0:T(8,128)(2,1)S(1)}, bf16[256,1024]{1,0:T(8,128)(2,1)}, u32[]{:S(2)}) copy-start(bf16[256,1024]{1,0:T(8,128)(2,1)} %w0.1) | copy-start | bytes 1572868
  0.6 8.7 %copy-start.4 = (bf16[128,1,128]{2,0,1:T(8,128)(2,1)S(1)}, bf16[128,1,128]{2,0,1:T(8,128)(2,1)}, u32[]{:S(2)}) copy-start(bf16[128,1,128]{2,0,1:T(8,128)(2,1)} %param.7) | copy-start | bytes 98308
  0.7 8.7 %copy-start.3 = (bf16[128,1,128]{2,0,1:T(8,128)(2,1)S(1)}, bf16[128,1,128]{2,0,1:T(8,128)(2,1)}, u32[]{:S(2)}) copy-start(bf16[128,1,128]{2,0,1:T(8,128)(2,1)} %param.8) | copy-start | bytes 98308
  0.7 10.1 %collective-permute-start.1 = (bf16[256,1024]{1,0:T(8,128)(2,1)}, bf16[256,1024]{1,0:T(8,128)(2,1)S(1)}, u32[]{:S(2)}, u32[]{:S(2)}) collective-permute-start(bf16[256,1024]{1,0:T(8,128)(2,1)} %w0.1), channel_id=1, source_target_pairs={{0,8},{8,0},{1,9},{9,1},{2,10},{10,2},{3,11},{11,3},{4,12},{12,4},... | collective-permute-start | bytes 1572872 | tf_op jit(solution)/shard_map/ppermute | solution.py:271
  5.3 5.4 %collective-permute-start = (bf16[32,2048]{1,0:T(8,128)(2,1)S(1)}, bf16[32,2048]{1,0:T(8,128)(2,1)S(1)}, u32[]{:S(2)}, u32[]{:S(2)}) collective-permute-start(bf16[32,2048]{1,0:T(8,128)(2,1)S(1)} %bitcast.61), channel_id=1, source_target_pairs={{0,8},{8,0},{1,9},{9,1},{2,10},{10,2},{3,11},{11,3},{4,12},{12,4},... | collective-permute-start | bytes 393224 | tf_op jit(solution)/shard_map/ppermute | solution.py:271
  5.5 12.4 %collective-permute-start.8 = (bf16[256,1024]{1,0:T(8,128)(2,1)S(1)}, bf16[256,1024]{1,0:T(8,128)(2,1)S(1)}, u32[]{:S(2)}, u32[]{:S(2)}) collective-permute-start(bf16[256,1024]{1,0:T(8,128)(2,1)S(1)} %copy-done), channel_id=1, source_target_pairs={{0,32},{32,64},{64,96},{96,128},{128,160},{160,192},{192,224},{224... | collective-permute-start | bytes 1572872 | tf_op jit(solution)/shard_map/ppermute | solution.py:282
  9.4 8.4 %collective-permute-start.15 = (bf16[128,256]{1,0:T(8,128)(2,1)S(1)}, bf16[128,256]{1,0:T(8,128)(2,1)S(1)}, u32[]{:S(2)}, u32[]{:S(2)}) collective-permute-start(bf16[128,256]{1,0:T(8,128)(2,1)S(1)} %pad_maximum_fusion.2), channel_id=1, source_target_pairs={{0,16},{16,0},{1,17},{17,1},{2,18},{18,2},{3,19},{19,3},{4,20},{20... | collective-permute-start | bytes 196616 | tf_op jit(solution)/shard_map/ppermute | solution.py:271
  10.8 4.2 %collective-permute-start.2 = (bf16[2,16,2048]{2,1,0:T(8,128)(2,1)S(1)}, bf16[2,16,2048]{2,1,0:T(8,128)(2,1)S(1)}, u32[]{:S(2)}, u32[]{:S(2)}) collective-permute-start(bf16[2,16,2048]{2,1,0:T(8,128)(2,1)S(1)} %fusion.9), channel_id=1, source_target_pairs={{0,16},{16,0},{1,17},{17,1},{2,18},{18,2},{3,19},{19,3},{4,20},{20... | collective-permute-start | bytes 393224 | tf_op jit(solution)/shard_map/ppermute | solution.py:271
  11.1 15.1 %collective-permute-start.9 = (bf16[256,1024]{1,0:T(8,128)(2,1)S(1)}, bf16[256,1024]{1,0:T(8,128)(2,1)S(1)}, u32[]{:S(2)}, u32[]{:S(2)}) collective-permute-start(bf16[256,1024]{1,0:T(8,128)(2,1)S(1)} %collective-permute-done.1), channel_id=1, source_target_pairs={{0,32},{32,64},{64,96},{96,128},{128,160},{160,192},{192,224},{224... | collective-permute-start | bytes 1572872 | tf_op jit(solution)/shard_map/ppermute | solution.py:282
  15.1 8.4 %collective-permute-start.3 = (bf16[64,2048]{1,0:T(8,128)(2,1)S(1)}, bf16[64,2048]{1,0:T(8,128)(2,1)S(1)}, u32[]{:S(2)}, u32[]{:S(2)}) collective-permute-start(bf16[64,2048]{1,0:T(8,128)(2,1)S(1)} %bitcast.57), channel_id=1, source_target_pairs={{0,1},{1,0},{2,3},{3,2},{4,5},{5,4},{6,7},{7,6},{8,9},{9,8},{10,11... | collective-permute-start | bytes 786440 | tf_op jit(solution)/shard_map/ppermute | solution.py:271
  17.8 3.1 %collective-permute-start.16 = (bf16[128,512]{1,0:T(8,128)(2,1)S(1)}, bf16[128,512]{1,0:T(8,128)(2,1)S(1)}, u32[]{:S(2)}, u32[]{:S(2)}) collective-permute-start(bf16[128,512]{1,0:T(8,128)(2,1)S(1)} %maximum_select_fusion.3), channel_id=1, source_target_pairs={{0,8},{8,0},{1,9},{9,1},{2,10},{10,2},{3,11},{11,3},{4,12},{12,4},... | collective-permute-start | bytes 393224 | tf_op jit(solution)/shard_map/ppermute | solution.py:271
  17.9 17.6 %collective-permute-start.10 = (bf16[256,1024]{1,0:T(8,128)(2,1)S(1)}, bf16[256,1024]{1,0:T(8,128)(2,1)S(1)}, u32[]{:S(2)}, u32[]{:S(2)}) collective-permute-start(bf16[256,1024]{1,0:T(8,128)(2,1)S(1)} %collective-permute-done.8.w1), channel_id=1, source_target_pairs={{0,32},{32,64},{64,96},{96,128},{128,160},{160,192},{192,224},{224... | collective-permute-start | bytes 1572872 | tf_op jit(solution)/shard_map/ppermute | solution.py:282
  21.0 14.5 %collective-permute-start.17 = (bf16[128,1024]{1,0:T(8,128)(2,1)S(1)}, bf16[128,1024]{1,0:T(8,128)(2,1)S(1)}, u32[]{:S(2)}, u32[]{:S(2)}) collective-permute-start(bf16[128,1024]{1,0:T(8,128)(2,1)S(1)} %maximum_select_fusion.2.plane), channel_id=1, source_target_pairs={{0,32},{32,64},{64,96},{96,128},{128,160},{160,192},{192,224},{224... | collective-permute-start | bytes 786440 | tf_op jit(solution)/shard_map/ppermute | solution.py:282
  23.5 21.6 %collective-permute-start.4 = (bf16[128,2048]{1,0:T(8,128)(2,1)S(1)}, bf16[128,2048]{1,0:T(8,128)(2,1)S(1)}, u32[]{:S(2)}, u32[]{:S(2)}) collective-permute-start(bf16[128,2048]{1,0:T(8,128)(2,1)S(1)} %pad_maximum_fusion.gh), channel_id=1, source_target_pairs={{0,2},{2,4},{4,6},{6,0},{1,3},{3,5},{5,7},{7,1},{8,10},{10,12},{12... | collective-permute-start | bytes 1572872 | tf_op jit(solution)/shard_map/ppermute | solution.py:275
  24.8 21.6 %collective-permute-start.5 = (bf16[128,2048]{1,0:T(8,128)(2,1)S(1)}, bf16[128,2048]{1,0:T(8,128)(2,1)S(1)}, u32[]{:S(2)}, u32[]{:S(2)}) collective-permute-start(bf16[128,2048]{1,0:T(8,128)(2,1)S(1)} %pad_maximum_fusion.gh), channel_id=1, source_target_pairs={{0,6},{2,0},{4,2},{6,4},{1,7},{3,1},{5,3},{7,5},{8,14},{10,8},{12,... | collective-permute-start | bytes 1572872 | tf_op jit(solution)/shard_map/ppermute | solution.py:275
  26.3 21.9 %collective-permute-start.11 = (bf16[256,1024]{1,0:T(8,128)(2,1)S(1)}, bf16[256,1024]{1,0:T(8,128)(2,1)S(1)}, u32[]{:S(2)}, u32[]{:S(2)}) collective-permute-start(bf16[256,1024]{1,0:T(8,128)(2,1)S(1)} %collective-permute-done.9.w2), channel_id=1, source_target_pairs={{0,32},{32,64},{64,96},{96,128},{128,160},{160,192},{192,224},{224... | collective-permute-start | bytes 1572872 | tf_op jit(solution)/shard_map/ppermute | solution.py:282
  35.5 9.0 %collective-permute-start.18 = (bf16[128,1024]{1,0:T(8,128)(2,1)S(1)}, bf16[128,1024]{1,0:T(8,128)(2,1)S(1)}, u32[]{:S(2)}, u32[]{:S(2)}) collective-permute-start(bf16[128,1024]{1,0:T(8,128)(2,1)S(1)} %collective-permute-done.17.r1), channel_id=1, source_target_pairs={{0,32},{32,64},{64,96},{96,128},{128,160},{160,192},{192,224},{224... | collective-permute-start | bytes 786440 | tf_op jit(solution)/shard_map/ppermute | solution.py:282
  35.5 15.3 %collective-permute-start.12 = (bf16[256,1024]{1,0:T(8,128)(2,1)S(1)}, bf16[256,1024]{1,0:T(8,128)(2,1)S(1)}, u32[]{:S(2)}, u32[]{:S(2)}) collective-permute-start(bf16[256,1024]{1,0:T(8,128)(2,1)S(1)} %collective-permute-done.10.w3), channel_id=1, source_target_pairs={{0,32},{32,64},{64,96},{96,128},{128,160},{160,192},{192,224},{224... | collective-permute-start | bytes 1572872 | tf_op jit(solution)/shard_map/ppermute | solution.py:282
  44.4 8.5 %collective-permute-start.19 = (bf16[128,1024]{1,0:T(8,128)(2,1)S(1)}, bf16[128,1024]{1,0:T(8,128)(2,1)S(1)}, u32[]{:S(2)}, u32[]{:S(2)}) collective-permute-start(bf16[128,1024]{1,0:T(8,128)(2,1)S(1)} %collective-permute-done.18.r2), channel_id=1, source_target_pairs={{0,32},{32,64},{64,96},{96,128},{128,160},{160,192},{192,224},{224... | collective-permute-start | bytes 786440 | tf_op jit(solution)/shard_map/ppermute | solution.py:282
  45.2 7.8 %collective-permute-start.6 = (bf16[64,2048]{1,0:T(8,128)(2,1)S(1)}, bf16[64,2048]{1,0:T(8,128)(2,1)S(1)}, u32[]{:S(2)}, u32[]{:S(2)}) collective-permute-start(bf16[64,2048]{1,0:T(8,128)(2,1)S(1)} %slice.289), channel_id=1, source_target_pairs={{0,2},{2,4},{4,6},{6,0},{1,3},{3,5},{5,7},{7,1},{8,10},{10,12},{12... | collective-permute-start | bytes 786440 | tf_op jit(solution)/shard_map/ppermute | solution.py:275
  46.4 6.6 %collective-permute-start.7 = (bf16[64,2048]{1,0:T(8,128)(2,1)S(1)}, bf16[64,2048]{1,0:T(8,128)(2,1)S(1)}, u32[]{:S(2)}, u32[]{:S(2)}) collective-permute-start(bf16[64,2048]{1,0:T(8,128)(2,1)S(1)} %slice.290), channel_id=1, source_target_pairs={{0,6},{2,0},{4,2},{6,4},{1,7},{3,1},{5,3},{7,5},{8,14},{10,8},{12,... | collective-permute-start | bytes 786440 | tf_op jit(solution)/shard_map/ppermute | solution.py:275
  48.2 8.7 %collective-permute-start.13 = (bf16[256,1024]{1,0:T(8,128)(2,1)S(1)}, bf16[256,1024]{1,0:T(8,128)(2,1)S(1)}, u32[]{:S(2)}, u32[]{:S(2)}) collective-permute-start(bf16[256,1024]{1,0:T(8,128)(2,1)S(1)} %collective-permute-done.11.w4), channel_id=1, source_target_pairs={{0,32},{32,64},{64,96},{96,128},{128,160},{160,192},{192,224},{224... | collective-permute-start | bytes 1572872 | tf_op jit(solution)/shard_map/ppermute | solution.py:282
  50.8 11.7 %collective-permute-start.14 = (bf16[256,1024]{1,0:T(8,128)(2,1)S(1)}, bf16[256,1024]{1,0:T(8,128)(2,1)S(1)}, u32[]{:S(2)}, u32[]{:S(2)}) collective-permute-start(bf16[256,1024]{1,0:T(8,128)(2,1)S(1)} %collective-permute-done.12), channel_id=1, source_target_pairs={{0,32},{32,64},{64,96},{96,128},{128,160},{160,192},{192,224},{224... | collective-permute-start | bytes 1572872 | tf_op jit(solution)/shard_map/ppermute | solution.py:282
  52.9 10.4 %collective-permute-start.20 = (bf16[128,1024]{1,0:T(8,128)(2,1)S(1)}, bf16[128,1024]{1,0:T(8,128)(2,1)S(1)}, u32[]{:S(2)}, u32[]{:S(2)}) collective-permute-start(bf16[128,1024]{1,0:T(8,128)(2,1)S(1)} %collective-permute-done.19.r3), channel_id=1, source_target_pairs={{0,8},{8,0},{1,9},{9,1},{2,10},{10,2},{3,11},{11,3},{4,12},{12,4},... | collective-permute-start | bytes 786440 | tf_op jit(solution)/shard_map/ppermute | solution.py:271
  63.1 3.0 %copy-start.2 = (bf16[128,8,128]{2,1,0:T(8,128)(2,1)S(1)}, bf16[128,8,128]{2,1,0:T(8,128)(2,1)}, u32[]{:S(2)}) copy-start(bf16[128,8,128]{2,1,0:T(8,128)(2,1)} %param.6) | copy-start | bytes 786436
  63.3 2.9 %copy-start.1 = (s32[8]{0:T(128)S(1)}, s32[8]{0:T(128)}, u32[]{:S(2)}) copy-start(s32[8]{0:T(128)} %lengths.5) | copy-start | bytes 100
  63.3 1.6 %collective-permute-start.21 = (bf16[128,1024]{1,0:T(8,128)(2,1)S(1)}, bf16[128,1024]{1,0:T(8,128)(2,1)S(1)}, u32[]{:S(2)}, u32[]{:S(2)}) collective-permute-start(bf16[128,1024]{1,0:T(8,128)(2,1)S(1)} %get-tuple-element.31), channel_id=1, source_target_pairs={{0,8},{8,0},{1,9},{9,1},{2,10},{10,2},{3,11},{11,3},{4,12},{12,4},... | collective-permute-start | bytes 786440 | tf_op jit(solution)/shard_map/ppermute | solution.py:271
  63.4 2.7 %collective-permute-start.24 = (bf16[128,1024]{1,0:T(8,128)(2,1)S(1)}, bf16[128,1024]{1,0:T(8,128)(2,1)S(1)}, u32[]{:S(2)}, u32[]{:S(2)}) collective-permute-start(bf16[128,1024]{1,0:T(8,128)(2,1)S(1)} %collective-permute-done.17.r1), channel_id=1, source_target_pairs={{0,8},{8,0},{1,9},{9,1},{2,10},{10,2},{3,11},{11,3},{4,12},{12,4},... | collective-permute-start | bytes 786440 | tf_op jit(solution)/shard_map/ppermute | solution.py:271
  63.9 2.3 %collective-permute-start.25 = (bf16[128,1024]{1,0:T(8,128)(2,1)S(1)}, bf16[128,1024]{1,0:T(8,128)(2,1)S(1)}, u32[]{:S(2)}, u32[]{:S(2)}) collective-permute-start(bf16[128,1024]{1,0:T(8,128)(2,1)S(1)} %collective-permute-done.18.r2), channel_id=1, source_target_pairs={{0,8},{8,0},{1,9},{9,1},{2,10},{10,2},{3,11},{11,3},{4,12},{12,4},... | collective-permute-start | bytes 786440 | tf_op jit(solution)/shard_map/ppermute | solution.py:271
  64.0 4.2 %collective-permute-start.22 = (bf16[128,1024]{1,0:T(8,128)(2,1)S(1)}, bf16[128,1024]{1,0:T(8,128)(2,1)S(1)}, u32[]{:S(2)}, u32[]{:S(2)}) collective-permute-start(bf16[128,1024]{1,0:T(8,128)(2,1)S(1)} %get-tuple-element.49), channel_id=1, source_target_pairs={{0,8},{8,0},{1,9},{9,1},{2,10},{10,2},{3,11},{11,3},{4,12},{12,4},... | collective-permute-start | bytes 786440 | tf_op jit(solution)/shard_map/ppermute | solution.py:271
  65.0 7.9 %collective-permute-start.23 = (bf16[128,1024]{1,0:T(8,128)(2,1)S(1)}, bf16[128,1024]{1,0:T(8,128)(2,1)S(1)}, u32[]{:S(2)}, u32[]{:S(2)}) collective-permute-start(bf16[128,1024]{1,0:T(8,128)(2,1)S(1)} %fusion.2), channel_id=1, source_target_pairs={{0,16},{16,0},{1,17},{17,1},{2,18},{18,2},{3,19},{19,3},{4,20},{20... | collective-permute-start | bytes 786440 | tf_op jit(solution)/shard_map/ppermute | solution.py:271
  74.0 2.2 %collective-permute-start.26 = (bf16[512,256]{1,0:T(8,128)(2,1)S(1)}, bf16[512,256]{1,0:T(8,128)(2,1)S(1)}, u32[]{:S(2)}, u32[]{:S(2)}) collective-permute-start(bf16[512,256]{1,0:T(8,128)(2,1)S(1)} %get-tuple-element.37), channel_id=1, source_target_pairs={{0,8},{8,0},{1,9},{9,1},{2,10},{10,2},{3,11},{11,3},{4,12},{12,4},... | collective-permute-start | bytes 786440 | tf_op jit(solution)/shard_map/ppermute | solution.py:271
  76.2 7.0 %collective-permute-start.27 = (bf16[512,256]{1,0:T(8,128)(2,1)S(1)}, bf16[512,256]{1,0:T(8,128)(2,1)S(1)}, u32[]{:S(2)}, u32[]{:S(2)}) collective-permute-start(bf16[512,256]{1,0:T(8,128)(2,1)S(1)} %add_convert_fusion.1), channel_id=1, source_target_pairs={{0,224},{32,0},{64,32},{96,64},{128,96},{160,128},{192,160},{224,1... | collective-permute-start | bytes 786440 | tf_op jit(solution)/shard_map/ppermute | solution.py:282
  79.5 4.2 %collective-permute-start.28 = (bf16[512,256]{1,0:T(8,128)(2,1)S(1)}, bf16[512,256]{1,0:T(8,128)(2,1)S(1)}, u32[]{:S(2)}, u32[]{:S(2)}) collective-permute-start(bf16[512,256]{1,0:T(8,128)(2,1)S(1)} %get-tuple-element.46), channel_id=1, source_target_pairs={{0,8},{8,0},{1,9},{9,1},{2,10},{10,2},{3,11},{11,3},{4,12},{12,4},... | collective-permute-start | bytes 786440 | tf_op jit(solution)/shard_map/ppermute | solution.py:271
  82.6 7.5 %collective-permute-start.30 = (bf16[512,256]{1,0:T(8,128)(2,1)S(1)}, bf16[512,256]{1,0:T(8,128)(2,1)S(1)}, u32[]{:S(2)}, u32[]{:S(2)}) collective-permute-start(bf16[512,256]{1,0:T(8,128)(2,1)S(1)} %get-tuple-element.48), channel_id=1, source_target_pairs={{0,8},{8,0},{1,9},{9,1},{2,10},{10,2},{3,11},{11,3},{4,12},{12,4},... | collective-permute-start | bytes 786440 | tf_op jit(solution)/shard_map/ppermute | solution.py:271
  83.9 11.1 %collective-permute-start.29 = (bf16[512,256]{1,0:T(8,128)(2,1)S(1)}, bf16[512,256]{1,0:T(8,128)(2,1)S(1)}, u32[]{:S(2)}, u32[]{:S(2)}) collective-permute-start(bf16[512,256]{1,0:T(8,128)(2,1)S(1)} %add_convert_fusion), channel_id=1, source_target_pairs={{0,224},{32,0},{64,32},{96,64},{128,96},{160,128},{192,160},{224,1... | collective-permute-start | bytes 786440 | tf_op jit(solution)/shard_map/ppermute | solution.py:282
  95.1 6.5 %collective-permute-start.31 = (bf16[512,256]{1,0:T(8,128)(2,1)S(1)}, bf16[512,256]{1,0:T(8,128)(2,1)S(1)}, u32[]{:S(2)}, u32[]{:S(2)}) collective-permute-start(bf16[512,256]{1,0:T(8,128)(2,1)S(1)} %fusion), channel_id=1, source_target_pairs={{0,224},{32,0},{64,32},{96,64},{128,96},{160,128},{192,160},{224,1... | collective-permute-start | bytes 786440 | tf_op jit(solution)/shard_map/ppermute | solution.py:282
  101.7 1.4 %collective-permute-start.32 = (bf16[256,256]{1,0:T(8,128)(2,1)S(1)}, bf16[256,256]{1,0:T(8,128)(2,1)S(1)}, u32[]{:S(2)}, u32[]{:S(2)}) collective-permute-start(bf16[256,256]{1,0:T(8,128)(2,1)S(1)} %select_convert_fusion), channel_id=1, source_target_pairs={{0,8},{8,0},{1,9},{9,1},{2,10},{10,2},{3,11},{11,3},{4,12},{12,4},... | collective-permute-start | bytes 393224 | tf_op jit(solution)/shard_map/ppermute | solution.py:271
  103.2 4.3 %collective-permute-start.33 = (bf16[128,256]{1,0:T(8,128)(2,1)S(1)}, bf16[128,256]{1,0:T(8,128)(2,1)S(1)}, u32[]{:S(2)}, u32[]{:S(2)}) collective-permute-start(bf16[128,256]{1,0:T(8,128)(2,1)S(1)} %select_convert_fusion.1), channel_id=1, source_target_pairs={{0,16},{16,0},{1,17},{17,1},{2,18},{18,2},{3,19},{19,3},{4,20},{20... | collective-permute-start | bytes 196616 | tf_op jit(solution)/shard_map/ppermute | solution.py:271

commit v4 on v3

--- a/solution.py
+++ b/solution.py
@@ -78,33 +78,9 @@
     total[...] = out
 
 
-def forward_kernel(
-    lengths, q, plane, r1, r2, r3, t1, t2, t3, att, lse, kv, m_scr, l_scr
-):
+def forward_planes(lengths, q, kv, probs, tops, att, m_row, l_row):
     z, c, pos0 = where_am_i()
     row_pos, start, low, high = documents(lengths, pos0)
-
-    def place(d, ref):
-        for b in range(4):
-            kv[d, b * 128 : b * 128 + 128, :] = ref[:, b * 256 : b * 256 + 256]
-
-    def place_all(near, far):
-        for d, ref in ((1, near[0]), (2, near[1]), (3, near[2]), (4, far[1]), (5, far[0])):
-            place(d, ref)
-
-    place(0, plane)
-
-    @pl.when(c == 0)
-    def _():
-        place_all((r1, r2, r3), (t1, t2))
-
-    @pl.when(c != 0)
-    def _():
-        place_all((t1, t2, t3), (r1, r2))
-
-    m_scr[...] = jnp.full((1, ROWS), NEG, F32)
-    l_scr[...] = jnp.zeros((1, ROWS), F32)
-    att[...] = jnp.zeros((HD, ROWS), F32)
 
     def work(d, masked):
         k = kv[d, :, 0:HD]
@@ -112,17 +88,49 @@
         s = dot(k, q[...], NT)
         if masked:
             s = jnp.where(allowed(z, d, row_pos, start), s, NEG)
-        old = m_scr[...]
+        old = m_row[...]
         new = jnp.maximum(old, jnp.max(s, axis=0, keepdims=True) * C2)
         shrink = jnp.exp2(old - new)
         p = jnp.exp2(s * C2 - new)
-        l_scr[...] = l_scr[...] * shrink + jnp.sum(p, axis=0, keepdims=True)
-        m_scr[...] = new
-        att[...] = att[...] * shrink + dot(v_t, p.astype(BF), NN)
+        l_row[...] = l_row[...] * shrink + jnp.sum(p, axis=0, keepdims=True)
+        m_row[...] = new
+        tops[d] = new
+        p = p.astype(BF)
+        probs[d] = p
+        att[...] = att[...] * shrink + dot(v_t, p, NN)
 
     each_plane(work, z, 0, z - low // PLANE + 1, high)
-    lse[...] = m_scr[...] + jnp.log2(l_scr[...])
-    att[...] = att[...] / l_scr[...]
+
+
+def place(kv, i, ref):
+    for b in range(4):
+        kv[i, b * 128 : b * 128 + 128, :] = ref[:, b * 256 : b * 256 + 256]
+
+
+def forward_kernel(
+    lengths, q, plane, r1, r2, r3, t1, t2, t3, att, kv, probs, factors, m_row, l_row
+):
+    place(kv, 0, plane)
+
+    @pl.when(lax.axis_index("c") == 0)
+    def _():
+        for i, ref in enumerate((r1, r2, r3, t2, t1)):
+            place(kv, i + 1, ref)
+
+    @pl.when(lax.axis_index("c") != 0)
+    def _():
+        for i, ref in enumerate((t1, t2, t3, r2, r1)):
+            place(kv, i + 1, ref)
+
+    m_row[...] = jnp.full((1, ROWS), NEG, F32)
+    l_row[...] = jnp.zeros((1, ROWS), F32)
+    att[...] = jnp.zeros((HD, ROWS), F32)
+    factors[...] = jnp.zeros((PLANES, 1, ROWS), F32)
+    forward_planes(lengths, q, kv, probs, factors, att, m_row, l_row)
+    lse = m_row[...] + jnp.log2(l_row[...])
+    for i in range(PLANES):
+        factors[i] = jnp.exp2(jnp.minimum(factors[i] - lse, 0.0))
+    att[...] = att[...] / l_row[...]
 
 
 def allowed(z, d, row_pos, start):
@@ -147,38 +155,35 @@
     lax.fori_loop(begin, end, plane, 0)
 
 
-def gradients(lengths, q, do, kv, lse, delta, dq_t, begin, end, store):
+def gradients(lengths, q, do, kv, probs, factors, delta, dq_t, begin, store):
     z, c, pos0 = where_am_i()
     row_pos, start, low, high = documents(lengths, pos0)
-    count = z - low // PLANE + 1
-
-    def work(d, masked):
+
+    def plane(d, carry):
         k = kv[d, :, 0:HD]
         v = kv[d, :, HD : 2 * HD]
         k_t = k.astype(F32).T.astype(BF)
-        s = dot(k, q[...], NT)
+        p = probs[d].astype(F32) * factors[d]
+        dv = dot(p.astype(BF), do[...], NN)
         dp = dot(v, do[...], NT)
-        p = jnp.exp2(s * C2 - lse[...])
-        if masked:
-            p = jnp.where(allowed(z, d, row_pos, start), p, 0.0)
-        dv = dot(p.astype(BF), do[...], NN)
         ds = (p * (dp - delta[...])).astype(BF)
         dk = dot(ds, q[...], NN) * SCALE
         dq_t[...] += dot(k_t, ds, NN)
         store(d, jnp.concatenate([dk, dv], axis=1).astype(BF))
-
-    stop = jnp.clip(count, begin, end)
-    each_plane(work, z, begin, stop, high)
+        return carry
+
+    stop = jnp.clip(z - low // PLANE + 1, begin, begin + 3)
+    lax.fori_loop(begin, stop, plane, 0)
 
     def blank(d, carry):
         store(d, jnp.zeros((PLANE, 2 * HD), BF))
         return carry
 
-    lax.fori_loop(stop, end, blank, 0)
+    lax.fori_loop(stop, begin + 3, blank, 0)
 
 
 def far_kernel(
-    lengths, q, o0, o1, o2, att, lse, kv, keep, send, fifth, do, delta, dq_t
+    lengths, q, o0, o1, o2, att, kv, probs, factors, keep, send, fifth, do, delta, dq_t
 ):
     c = lax.axis_index("c")
     o = (o0[...] + o1[...].astype(F32) + o2[...].astype(F32)).astype(BF)
@@ -203,11 +208,11 @@
         def _():
             fifth[...] = value
 
-    gradients(lengths, q, do, kv, lse, delta, dq_t, 3, 6, store)
+    gradients(lengths, q, do, kv, probs, factors, delta, dq_t, 3, store)
 
 
 def near_kernel(
-    lengths, q, do, lse, delta, kv, dq_far, fifth, dq, keep2, keep1, send2, send1, dq_t
+    lengths, q, do, delta, kv, probs, factors, dq_far, fifth, dq, keep2, keep1, send2, send1, dq_t
 ):
     c = lax.axis_index("c")
     dq_t[...] = dq_far[...]
@@ -239,7 +244,7 @@
         def _():
             send1[...] = value
 
-    gradients(lengths, q, do, kv, lse, delta, dq_t, 0, 3, store)
+    gradients(lengths, q, do, kv, probs, factors, delta, dq_t, 0, store)
     for h in range(8):
         cols = slice(h * 128, h * 128 + 128)
         dq[:, cols] = (dq_t[:, cols] * SCALE).T.astype(BF)
@@ -359,13 +364,15 @@
 
     q = queries.transpose(1, 0, 2).reshape(ROWS, HD)
     q, from_both = tie(q, from_both)
-    att, lse, planes = call(
+    row_shape, dq_shape = shape((1, ROWS), F32), shape((HD, ROWS), F32)
+    att, kv, probs, factors = call(
         forward_kernel,
         [q, plane, r1, r2, r3, t1, t2, t3],
         [
-            shape((HD, ROWS), F32),
-            shape((1, ROWS), F32),
+            dq_shape,
             shape((PLANES, PLANE, 2 * HD), BF),
+            shape((PLANES, PLANE, ROWS), BF),
+            shape((PLANES, 1, ROWS), F32),
         ],
         [pltpu.VMEM((1, ROWS), F32)] * 2,
         1,
@@ -376,8 +383,8 @@
     block = shape((PLANE, 2 * HD), BF)
     keep, send, fifth, do, delta, dq_far = call(
         far_kernel,
-        [q, keep0, from_core, from_y, att, lse, planes],
-        [block, block, block, shape((ROWS, HD), BF), shape((1, ROWS), F32), shape((HD, ROWS), F32)],
+        [q, keep0, from_core, from_y, att, kv, probs, factors],
+        [block, block, block, shape((ROWS, HD), BF), row_shape, dq_shape],
         [],
         5 * 1024 * 2560 * 128,
         B_MIB,
@@ -389,7 +396,7 @@
     q, got = tie(q, got)
     dq, keep2, keep1, send2, send1 = call(
         near_kernel,
-        [q, do, lse, delta, planes, dq_far, fifth],
+        [q, do, delta, kv, probs, factors, dq_far, fifth],
         [shape((128, 1024), BF), block, block, block, block],
         [pltpu.VMEM((HD, ROWS), F32)],
         5 * 1024 * 2560 * 128,
@@ -397,6 +404,7 @@
         doc_lengths,
     )
     middle = add(keep2, swap(send2, "c"))
+    send1, run = tie(send1, run)
     final = add(keep1, swap(send1, "c"))
     run = along_z((run.astype(F32) + middle).astype(BF), 7, 2)
     run = jnp.where(first, run.astype(F32) + final, run.astype(F32)).astype(BF)

time: 109 us -> 111 us (1.018)
  waiting for transfers between devices: 42.8 us -> 45.2 us
    ppermute x17, starting transfers between devices: 16.3 us -> 24.8 us  [swap(): return lax.ppermute(x, axis, [(0, 1), (1, 0)])]
    ppermute x13, starting transfers between devices: 29.8 us -> 21.7 us  [along_z(): return lax.ppermute(x, ('z', 'c'), pairs)]
    ppermute x4, waiting for transfers between devices: 0.01 us -> 3.18 us  [turn(): return lax.ppermute(x, 'x', [(i, (i + step) % 4) for i in range(4)])]
  transfers between devices with their start and end apart: 34 -> 34, of which waited for: 14 -> 14; matrix products, arithmetic and copies ran while one was open for 4% -> 4% of each run, Pallas kernels for 6% -> 5%
where the time goes in v4:
time: 111 us; the launch traced here: 110 us
  starting transfers between devices  51.8 us (47%)
  waiting for transfers between devices  45.2 us (41%)
  Pallas kernels  6.63 us (6%)
  other arithmetic  2.16 us (2%)
  local copies, waits for them, and re-layouts  1.61 us (1%)
  matrix products  1.46 us (1%)
  between operations  1.12 us (1%)
    ppermute x13, waiting for transfers between devices, along_z(): return lax.ppermute(x, ('z', 'c'), pairs)  29.4 us
    ppermute x17, starting transfers between devices, swap(): return lax.ppermute(x, axis, [(0, 1), (1, 0)])  24.8 us
    ppermute x13, starting transfers between devices, along_z(): return lax.ppermute(x, ('z', 'c'), pairs)  21.7 us
    ppermute x17, waiting for transfers between devices, swap(): return lax.ppermute(x, axis, [(0, 1), (1, 0)])  12.6 us
    pallas_call x4, Pallas kernels, call(): pl.pallas_call(kernel, out_shape=outs, in_specs=first + [vmem] * len(args...  6.63 us
    ppermute x4, starting transfers between devices, turn(): return lax.ppermute(x, 'x', [(i, (i + step) % 4) for i in range(4)])  5.38 us
    ppermute x4, waiting for transfers between devices, turn(): return lax.ppermute(x, 'x', [(i, (i + step) % 4) for i in range(4)])  3.18 us
  transfers between devices with their start and end apart: 34, of which 14 were waited for; matrix products, arithmetic and copies ran while one was open for 4% of the time, Pallas kernels for 5%

profile of v4, /device:TPU:1, one launch (start us, length us, event | category | flops | bytes accessed | tf_op | source)
XLA Modules:
  0.0 110.0 jit_solution(194055752174200506)
XLA Ops:
  0.7 3.3 %collective-permute-start.1 = (bf16[256,1024]{1,0:T(8,128)(2,1)}, bf16[256,1024]{1,0:T(8,128)(2,1)S(1)}, u32[]{:S(2)}, u32[]{:S(2)}) collective-permute-start(bf16[256,1024]{1,0:T(8,128)(2,1)} %w0.1), channel_id=1, source_target_pairs={{0,8},{8,0},{1,9},{9,1},{2,10},{10,2},{3,11},{11,3},{4,12},{12,4},... | collective-permute-start | bytes 1572872 | tf_op jit(solution)/shard_map/ppermute | solution.py:276
  4.0 1.1 fusion.3
  5.3 0.2 collective-permute-start
  5.5 3.9 %collective-permute-start.8 = (bf16[256,1024]{1,0:T(8,128)(2,1)S(1)}, bf16[256,1024]{1,0:T(8,128)(2,1)S(1)}, u32[]{:S(2)}, u32[]{:S(2)}) collective-permute-start(bf16[256,1024]{1,0:T(8,128)(2,1)S(1)} %copy-done), channel_id=1, source_target_pairs={{0,32},{32,64},{64,96},{96,128},{128,160},{160,192},{192,224},{224... | collective-permute-start | bytes 1572872 | tf_op jit(solution)/shard_map/ppermute | solution.py:287
  9.4 1.4 %collective-permute-start.15 = (bf16[128,256]{1,0:T(8,128)(2,1)S(1)}, bf16[128,256]{1,0:T(8,128)(2,1)S(1)}, u32[]{:S(2)}, u32[]{:S(2)}) collective-permute-start(bf16[128,256]{1,0:T(8,128)(2,1)S(1)} %pad_maximum_fusion.2), channel_id=1, source_target_pairs={{0,16},{16,0},{1,17},{17,1},{2,18},{18,2},{3,19},{19,3},{4,20},{20... | collective-permute-start | bytes 196616 | tf_op jit(solution)/shard_map/ppermute | solution.py:276
  10.8 0.3 collective-permute-start.2
  11.1 1.0 collective-permute-start.9
  12.2 2.9 %collective-permute-done.2 = bf16[2,16,2048]{2,1,0:T(8,128)(2,1)S(1)} collective-permute-done((bf16[2,16,2048]{2,1,0:T(8,128)(2,1)S(1)}, bf16[2,16,2048]{2,1,0:T(8,128)(2,1)S(1)}, u32[]{:S(2)}, u32[]{:S(2)}) %collective-permute-start.2) | collective-permute-done | bytes 131104 | tf_op jit(solution)/shard_map/ppermute | solution.py:276
  15.1 2.7 %collective-permute-start.3 = (bf16[64,2048]{1,0:T(8,128)(2,1)S(1)}, bf16[64,2048]{1,0:T(8,128)(2,1)S(1)}, u32[]{:S(2)}, u32[]{:S(2)}) collective-permute-start(bf16[64,2048]{1,0:T(8,128)(2,1)S(1)} %bitcast.57), channel_id=1, source_target_pairs={{0,1},{1,0},{2,3},{3,2},{4,5},{5,4},{6,7},{7,6},{8,9},{9,8},{10,11... | collective-permute-start | bytes 786440 | tf_op jit(solution)/shard_map/ppermute | solution.py:276
  17.8 0.1 collective-permute-start.16
  17.9 3.0 %collective-permute-start.10 = (bf16[256,1024]{1,0:T(8,128)(2,1)S(1)}, bf16[256,1024]{1,0:T(8,128)(2,1)S(1)}, u32[]{:S(2)}, u32[]{:S(2)}) collective-permute-start(bf16[256,1024]{1,0:T(8,128)(2,1)S(1)} %collective-permute-done.8.w1), channel_id=1, source_target_pairs={{0,32},{32,64},{64,96},{96,128},{128,160},{160,192},{192,224},{224... | collective-permute-start | bytes 1572872 | tf_op jit(solution)/shard_map/ppermute | solution.py:287
  20.9 0.1 maximum_select_fusion.2.plane
  21.0 2.4 %collective-permute-start.17 = (bf16[128,1024]{1,0:T(8,128)(2,1)S(1)}, bf16[128,1024]{1,0:T(8,128)(2,1)S(1)}, u32[]{:S(2)}, u32[]{:S(2)}) collective-permute-start(bf16[128,1024]{1,0:T(8,128)(2,1)S(1)} %maximum_select_fusion.2.plane), channel_id=1, source_target_pairs={{0,32},{32,64},{64,96},{96,128},{128,160},{160,192},{192,224},{224... | collective-permute-start | bytes 786440 | tf_op jit(solution)/shard_map/ppermute | solution.py:287
  23.5 2.6 %collective-permute-start.5 = (bf16[128,2048]{1,0:T(8,128)(2,1)S(1)}, bf16[128,2048]{1,0:T(8,128)(2,1)S(1)}, u32[]{:S(2)}, u32[]{:S(2)}) collective-permute-start(bf16[128,2048]{1,0:T(8,128)(2,1)S(1)} %pad_maximum_fusion.gh), channel_id=1, source_target_pairs={{0,6},{2,0},{4,2},{6,4},{1,7},{3,1},{5,3},{7,5},{8,14},{10,8},{12,... | collective-permute-start | bytes 1572872 | tf_op jit(solution)/shard_map/ppermute | solution.py:280
  26.0 2.1 %collective-permute-start.11 = (bf16[256,1024]{1,0:T(8,128)(2,1)S(1)}, bf16[256,1024]{1,0:T(8,128)(2,1)S(1)}, u32[]{:S(2)}, u32[]{:S(2)}) collective-permute-start(bf16[256,1024]{1,0:T(8,128)(2,1)S(1)} %collective-permute-done.9.w2), channel_id=1, source_target_pairs={{0,32},{32,64},{64,96},{96,128},{128,160},{160,192},{192,224},{224... | collective-permute-start | bytes 1572872 | tf_op jit(solution)/shard_map/ppermute | solution.py:287
  28.1 7.4 %collective-permute-done.17.r1 = bf16[128,1024]{1,0:T(8,128)(2,1)S(1)} collective-permute-done((bf16[128,1024]{1,0:T(8,128)(2,1)S(1)}, bf16[128,1024]{1,0:T(8,128)(2,1)S(1)}, u32[]{:S(2)}, u32[]{:S(2)}) %collective-permute-start.17) | collective-permute-done | bytes 262176 | tf_op jit(solution)/shard_map/ppermute | solution.py:287
  35.5 2.7 %collective-permute-start.12 = (bf16[256,1024]{1,0:T(8,128)(2,1)S(1)}, bf16[256,1024]{1,0:T(8,128)(2,1)S(1)}, u32[]{:S(2)}, u32[]{:S(2)}) collective-permute-start(bf16[256,1024]{1,0:T(8,128)(2,1)S(1)} %collective-permute-done.10.w3), channel_id=1, source_target_pairs={{0,32},{32,64},{64,96},{96,128},{128,160},{160,192},{192,224},{224... | collective-permute-start | bytes 1572872 | tf_op jit(solution)/shard_map/ppermute | solution.py:287
  38.2 6.3 %collective-permute-done.18.r2 = bf16[128,1024]{1,0:T(8,128)(2,1)S(1)} collective-permute-done((bf16[128,1024]{1,0:T(8,128)(2,1)S(1)}, bf16[128,1024]{1,0:T(8,128)(2,1)S(1)}, u32[]{:S(2)}, u32[]{:S(2)}) %collective-permute-start.18) | collective-permute-done | bytes 262176 | tf_op jit(solution)/shard_map/ppermute | solution.py:287
  44.4 0.7 collective-permute-start.19
  45.2 2.6 %collective-permute-start.7 = (bf16[64,2048]{1,0:T(8,128)(2,1)S(1)}, bf16[64,2048]{1,0:T(8,128)(2,1)S(1)}, u32[]{:S(2)}, u32[]{:S(2)}) collective-permute-start(bf16[64,2048]{1,0:T(8,128)(2,1)S(1)} %slice.290), channel_id=1, source_target_pairs={{0,6},{2,0},{4,2},{6,4},{1,7},{3,1},{5,3},{7,5},{8,14},{10,8},{12,... | collective-permute-start | bytes 786440 | tf_op jit(solution)/shard_map/ppermute | solution.py:280
  47.7 0.3 collective-permute-start.6
  48.0 2.7 %collective-permute-start.13 = (bf16[256,1024]{1,0:T(8,128)(2,1)S(1)}, bf16[256,1024]{1,0:T(8,128)(2,1)S(1)}, u32[]{:S(2)}, u32[]{:S(2)}) collective-permute-start(bf16[256,1024]{1,0:T(8,128)(2,1)S(1)} %collective-permute-done.11.w4), channel_id=1, source_target_pairs={{0,32},{32,64},{64,96},{96,128},{128,160},{160,192},{192,224},{224... | collective-permute-start | bytes 1572872 | tf_op jit(solution)/shard_map/ppermute | solution.py:287
  50.7 2.0 %collective-permute-start.14 = (bf16[256,1024]{1,0:T(8,128)(2,1)S(1)}, bf16[256,1024]{1,0:T(8,128)(2,1)S(1)}, u32[]{:S(2)}, u32[]{:S(2)}) collective-permute-start(bf16[256,1024]{1,0:T(8,128)(2,1)S(1)} %collective-permute-done.12), channel_id=1, source_target_pairs={{0,32},{32,64},{64,96},{96,128},{128,160},{160,192},{192,224},{224... | collective-permute-start | bytes 1572872 | tf_op jit(solution)/shard_map/ppermute | solution.py:287
  52.7 3.2 %collective-permute-done.6.gu2 = bf16[64,2048]{1,0:T(8,128)(2,1)S(1)} collective-permute-done((bf16[64,2048]{1,0:T(8,128)(2,1)S(1)}, bf16[64,2048]{1,0:T(8,128)(2,1)S(1)}, u32[]{:S(2)}, u32[]{:S(2)}) %collective-permute-start.6) | collective-permute-done | bytes 262176 | tf_op jit(solution)/shard_map/ppermute | solution.py:280
  55.8 1.6 %shard_map.85 = (f32[512,1024]{1,0:T(8,128)S(1)}, bf16[512,768]{1,0:T(8,128)(2,1)S(1)}) custom-call(bf16[128,2048]{1,0:T(8,128)(2,1)S(1)} %pad_maximum_fusion.gh, bf16[128,2048]{1,0:T(8,128)(2,1)S(1)} %collective-permute-done.4.gu, bf16[128,2048]{1,0:T(8,128)(2,1)S(1)} %collective-permute-done.5.gd, bf16[64,2048]{1,0:T(8,128)(2,1)S(1)} %collective-permute-done.6.gu2, ...), custom_call_target="tpu_custom_call" | custom-call | bytes 6291456 | tf_op jit(solution)/shard_map/pallas_call | solution.py:256
  57.5 0.4 fusion.7
  57.9 0.4 fusion.5
  58.4 4.0 %collective-permute-done.14 = bf16[256,1024]{1,0:T(8,128)(2,1)S(1)} collective-permute-done((bf16[256,1024]{1,0:T(8,128)(2,1)S(1)}, bf16[256,1024]{1,0:T(8,128)(2,1)S(1)}, u32[]{:S(2)}, u32[]{:S(2)}) %collective-permute-start.14) | collective-permute-done | bytes 524320 | tf_op jit(solution)/shard_map/ppermute | solution.py:287
  62.4 0.6 add_add_fusion
  63.0 0.0 copy-start.2
  63.0 0.2 convert.4
  63.2 0.0 copy-start.1
  63.3 0.1 collective-permute-start.21
  63.4 0.5 collective-permute-start.24
  63.8 0.1 collective-permute-start.25
  63.9 0.4 collective-permute-start.22
  64.4 0.5 collective-permute-done.21
  64.9 0.1 fusion.2
  64.9 1.1 collective-permute-start.23
  66.1 2.1 %shard_map.86 = (f32[128,1024]{1,0:T(8,128)S(1)}, bf16[6,512,256]{2,1,0:T(8,128)(2,1)S(1)}, bf16[6,512,1024]{2,1,0:T(8,128)(2,1)S(1)}, f32[6,1,1024]{2,1,0:T(1,128)S(1)}) custom-call(s32[8]{0:T(128)S(1)} %copy-done.1, bf16[1024,128]{1,0:T(8,128)(2,1)S(1)} %bitcast.50, bf16[128,1024]{1,0:T(8,128)(2,1)S(1)} %maximum_select_fusion.2.plane, ...), custom_call_target="tpu_custom_call" | custom-call | flops 1 | bytes 6291456 | tf_op jit(solution)/shard_map/pallas_call | solution.py:256
  68.3 4.5 %collective-permute-done.23.o2 = bf16[128,1024]{1,0:T(8,128)(2,1)S(1)} collective-permute-done((bf16[128,1024]{1,0:T(8,128)(2,1)S(1)}, bf16[128,1024]{1,0:T(8,128)(2,1)S(1)}, u32[]{:S(2)}, u32[]{:S(2)}) %collective-permute-start.23) | collective-permute-done | bytes 262176 | tf_op jit(solution)/shard_map/ppermute | solution.py:276
  72.8 0.8 shard_map.87
  73.6 1.0 collective-permute-start.26
  74.7 1.2 %collective-permute-done.26 = bf16[512,256]{1,0:T(8,128)(2,1)S(1)} collective-permute-done((bf16[512,256]{1,0:T(8,128)(2,1)S(1)}, bf16[512,256]{1,0:T(8,128)(2,1)S(1)}, u32[]{:S(2)}, u32[]{:S(2)}) %collective-permute-start.26) | collective-permute-done | bytes 262176 | tf_op jit(solution)/shard_map/ppermute | solution.py:276
  75.8 0.1 add_convert_fusion.1
  75.9 1.1 collective-permute-start.27
  77.0 2.0 %shard_map.88 = (bf16[128,1024]{1,0:T(8,128)(2,1)S(1)}, bf16[512,256]{1,0:T(8,128)(2,1)S(1)}, bf16[512,256]{1,0:T(8,128)(2,1)S(1)}, bf16[512,256]{1,0:T(8,128)(2,1)S(1)}, bf16[512,256]{1,0:T(8,128)(2,1)S(1)}) custom-call(s32[8]{0:T(128)S(1)} %copy-done.1, bf16[1024,128]{1,0:T(8,128)(2,1)S(1)} %bitcast.52, bf16[1024,128]{1,0:T(8,128)(2,1)S(1)} %get-tuple-element.43.do, ...), custom_call_target="tpu_custom_call" | custom-call | flops 1677721600 | bytes 6291456 | tf_op jit(solution)/shard_map/pallas_call | solution.py:256
  79.0 8.5 %collective-permute-start.28 = (bf16[512,256]{1,0:T(8,128)(2,1)S(1)}, bf16[512,256]{1,0:T(8,128)(2,1)S(1)}, u32[]{:S(2)}, u32[]{:S(2)}) collective-permute-start(bf16[512,256]{1,0:T(8,128)(2,1)S(1)} %get-tuple-element.52), channel_id=1, source_target_pairs={{0,8},{8,0},{1,9},{9,1},{2,10},{10,2},{3,11},{11,3},{4,12},{12,4},... | collective-permute-start | bytes 786440 | tf_op jit(solution)/shard_map/ppermute | solution.py:276
  87.5 1.0 collective-permute-done.27
  88.5 0.2 collective-permute-done.28
  88.7 0.1 add_convert_fusion
  88.8 0.1 collective-permute-start.29
  88.9 4.3 %collective-permute-start.30 = (bf16[512,256]{1,0:T(8,128)(2,1)S(1)}, bf16[512,256]{1,0:T(8,128)(2,1)S(1)}, u32[]{:S(2)}, u32[]{:S(2)}) collective-permute-start(bf16[512,256]{1,0:T(8,128)(2,1)S(1)} %get-tuple-element.54), channel_id=1, source_target_pairs={{0,8},{8,0},{1,9},{9,1},{2,10},{10,2},{3,11},{11,3},{4,12},{12,4},... | collective-permute-start | bytes 786440 | tf_op jit(solution)/shard_map/ppermute | solution.py:276
  93.2 4.3 %collective-permute-done.29 = bf16[512,256]{1,0:T(8,128)(2,1)S(1)} collective-permute-done((bf16[512,256]{1,0:T(8,128)(2,1)S(1)}, bf16[512,256]{1,0:T(8,128)(2,1)S(1)}, u32[]{:S(2)}, u32[]{:S(2)}) %collective-permute-start.29) | collective-permute-done | bytes 262176 | tf_op jit(solution)/shard_map/ppermute | solution.py:287
  97.5 0.1 fusion
  97.7 0.1 collective-permute-start.31
  97.8 6.4 %collective-permute-done.31 = bf16[512,256]{1,0:T(8,128)(2,1)S(1)} collective-permute-done((bf16[512,256]{1,0:T(8,128)(2,1)S(1)}, bf16[512,256]{1,0:T(8,128)(2,1)S(1)}, u32[]{:S(2)}, u32[]{:S(2)}) %collective-permute-start.31) | collective-permute-done | bytes 262176 | tf_op jit(solution)/shard_map/ppermute | solution.py:287
  104.2 0.1 add_select_fusion
  104.3 0.8 collective-permute-start.32
  105.1 1.0 collective-permute-done.32
  106.2 0.1 collective-permute-start.33
  106.3 0.8 copy.14
  107.0 2.4 %collective-permute-done.33 = bf16[128,256]{1,0:T(8,128)(2,1)S(1)} collective-permute-done((bf16[128,256]{1,0:T(8,128)(2,1)S(1)}, bf16[128,256]{1,0:T(8,128)(2,1)S(1)}, u32[]{:S(2)}, u32[]{:S(2)}) %collective-permute-start.33) | collective-permute-done | bytes 65568 | tf_op jit(solution)/shard_map/ppermute | solution.py:276
  109.4 0.6 slice_bitcast_fusion.4
  (61 shorter events, 0.6 us)
Async XLA Ops:
  0.6 4.8 %copy-start = (bf16[256,1024]{1,0:T(8,128)(2,1)S(1)}, bf16[256,1024]{1,0:T(8,128)(2,1)}, u32[]{:S(2)}) copy-start(bf16[256,1024]{1,0:T(8,128)(2,1)} %w0.1) | copy-start | bytes 1572868
  0.6 8.7 %copy-start.3 = (bf16[128,1,128]{2,0,1:T(8,128)(2,1)S(1)}, bf16[128,1,128]{2,0,1:T(8,128)(2,1)}, u32[]{:S(2)}) copy-start(bf16[128,1,128]{2,0,1:T(8,128)(2,1)} %param.8) | copy-start | bytes 98308
  0.7 8.7 %copy-start.4 = (bf16[128,1,128]{2,0,1:T(8,128)(2,1)S(1)}, bf16[128,1,128]{2,0,1:T(8,128)(2,1)}, u32[]{:S(2)}) copy-start(bf16[128,1,128]{2,0,1:T(8,128)(2,1)} %param.7) | copy-start | bytes 98308
  0.7 10.1 %collective-permute-start.1 = (bf16[256,1024]{1,0:T(8,128)(2,1)}, bf16[256,1024]{1,0:T(8,128)(2,1)S(1)}, u32[]{:S(2)}, u32[]{:S(2)}) collective-permute-start(bf16[256,1024]{1,0:T(8,128)(2,1)} %w0.1), channel_id=1, source_target_pairs={{0,8},{8,0},{1,9},{9,1},{2,10},{10,2},{3,11},{11,3},{4,12},{12,4},... | collective-permute-start | bytes 1572872 | tf_op jit(solution)/shard_map/ppermute | solution.py:276
  5.3 5.4 %collective-permute-start = (bf16[32,2048]{1,0:T(8,128)(2,1)S(1)}, bf16[32,2048]{1,0:T(8,128)(2,1)S(1)}, u32[]{:S(2)}, u32[]{:S(2)}) collective-permute-start(bf16[32,2048]{1,0:T(8,128)(2,1)S(1)} %bitcast.61), channel_id=1, source_target_pairs={{0,8},{8,0},{1,9},{9,1},{2,10},{10,2},{3,11},{11,3},{4,12},{12,4},... | collective-permute-start | bytes 393224 | tf_op jit(solution)/shard_map/ppermute | solution.py:276
  5.5 12.4 %collective-permute-start.8 = (bf16[256,1024]{1,0:T(8,128)(2,1)S(1)}, bf16[256,1024]{1,0:T(8,128)(2,1)S(1)}, u32[]{:S(2)}, u32[]{:S(2)}) collective-permute-start(bf16[256,1024]{1,0:T(8,128)(2,1)S(1)} %copy-done), channel_id=1, source_target_pairs={{0,32},{32,64},{64,96},{96,128},{128,160},{160,192},{192,224},{224... | collective-permute-start | bytes 1572872 | tf_op jit(solution)/shard_map/ppermute | solution.py:287
  9.4 8.4 %collective-permute-start.15 = (bf16[128,256]{1,0:T(8,128)(2,1)S(1)}, bf16[128,256]{1,0:T(8,128)(2,1)S(1)}, u32[]{:S(2)}, u32[]{:S(2)}) collective-permute-start(bf16[128,256]{1,0:T(8,128)(2,1)S(1)} %pad_maximum_fusion.2), channel_id=1, source_target_pairs={{0,16},{16,0},{1,17},{17,1},{2,18},{18,2},{3,19},{19,3},{4,20},{20... | collective-permute-start | bytes 196616 | tf_op jit(solution)/shard_map/ppermute | solution.py:276
  10.8 4.2 %collective-permute-start.2 = (bf16[2,16,2048]{2,1,0:T(8,128)(2,1)S(1)}, bf16[2,16,2048]{2,1,0:T(8,128)(2,1)S(1)}, u32[]{:S(2)}, u32[]{:S(2)}) collective-permute-start(bf16[2,16,2048]{2,1,0:T(8,128)(2,1)S(1)} %fusion.9), channel_id=1, source_target_pairs={{0,16},{16,0},{1,17},{17,1},{2,18},{18,2},{3,19},{19,3},{4,20},{20... | collective-permute-start | bytes 393224 | tf_op jit(solution)/shard_map/ppermute | solution.py:276
  11.1 14.9 %collective-permute-start.9 = (bf16[256,1024]{1,0:T(8,128)(2,1)S(1)}, bf16[256,1024]{1,0:T(8,128)(2,1)S(1)}, u32[]{:S(2)}, u32[]{:S(2)}) collective-permute-start(bf16[256,1024]{1,0:T(8,128)(2,1)S(1)} %collective-permute-done.1), channel_id=1, source_target_pairs={{0,32},{32,64},{64,96},{96,128},{128,160},{160,192},{192,224},{224... | collective-permute-start | bytes 1572872 | tf_op jit(solution)/shard_map/ppermute | solution.py:287
  15.1 8.4 %collective-permute-start.3 = (bf16[64,2048]{1,0:T(8,128)(2,1)S(1)}, bf16[64,2048]{1,0:T(8,128)(2,1)S(1)}, u32[]{:S(2)}, u32[]{:S(2)}) collective-permute-start(bf16[64,2048]{1,0:T(8,128)(2,1)S(1)} %bitcast.57), channel_id=1, source_target_pairs={{0,1},{1,0},{2,3},{3,2},{4,5},{5,4},{6,7},{7,6},{8,9},{9,8},{10,11... | collective-permute-start | bytes 786440 | tf_op jit(solution)/shard_map/ppermute | solution.py:276
  17.8 3.1 %collective-permute-start.16 = (bf16[128,512]{1,0:T(8,128)(2,1)S(1)}, bf16[128,512]{1,0:T(8,128)(2,1)S(1)}, u32[]{:S(2)}, u32[]{:S(2)}) collective-permute-start(bf16[128,512]{1,0:T(8,128)(2,1)S(1)} %maximum_select_fusion.3), channel_id=1, source_target_pairs={{0,8},{8,0},{1,9},{9,1},{2,10},{10,2},{3,11},{11,3},{4,12},{12,4},... | collective-permute-start | bytes 393224 | tf_op jit(solution)/shard_map/ppermute | solution.py:276
  17.9 17.6 %collective-permute-start.10 = (bf16[256,1024]{1,0:T(8,128)(2,1)S(1)}, bf16[256,1024]{1,0:T(8,128)(2,1)S(1)}, u32[]{:S(2)}, u32[]{:S(2)}) collective-permute-start(bf16[256,1024]{1,0:T(8,128)(2,1)S(1)} %collective-permute-done.8.w1), channel_id=1, source_target_pairs={{0,32},{32,64},{64,96},{96,128},{128,160},{160,192},{192,224},{224... | collective-permute-start | bytes 1572872 | tf_op jit(solution)/shard_map/ppermute | solution.py:287
  21.0 14.5 %collective-permute-start.17 = (bf16[128,1024]{1,0:T(8,128)(2,1)S(1)}, bf16[128,1024]{1,0:T(8,128)(2,1)S(1)}, u32[]{:S(2)}, u32[]{:S(2)}) collective-permute-start(bf16[128,1024]{1,0:T(8,128)(2,1)S(1)} %maximum_select_fusion.2.plane), channel_id=1, source_target_pairs={{0,32},{32,64},{64,96},{96,128},{128,160},{160,192},{192,224},{224... | collective-permute-start | bytes 786440 | tf_op jit(solution)/shard_map/ppermute | solution.py:287
  23.5 21.6 %collective-permute-start.5 = (bf16[128,2048]{1,0:T(8,128)(2,1)S(1)}, bf16[128,2048]{1,0:T(8,128)(2,1)S(1)}, u32[]{:S(2)}, u32[]{:S(2)}) collective-permute-start(bf16[128,2048]{1,0:T(8,128)(2,1)S(1)} %pad_maximum_fusion.gh), channel_id=1, source_target_pairs={{0,6},{2,0},{4,2},{6,4},{1,7},{3,1},{5,3},{7,5},{8,14},{10,8},{12,... | collective-permute-start | bytes 1572872 | tf_op jit(solution)/shard_map/ppermute | solution.py:280
  26.0 21.7 %collective-permute-start.4 = (bf16[128,2048]{1,0:T(8,128)(2,1)S(1)}, bf16[128,2048]{1,0:T(8,128)(2,1)S(1)}, u32[]{:S(2)}, u32[]{:S(2)}) collective-permute-start(bf16[128,2048]{1,0:T(8,128)(2,1)S(1)} %pad_maximum_fusion.gh), channel_id=1, source_target_pairs={{0,2},{2,4},{4,6},{6,0},{1,3},{3,5},{5,7},{7,1},{8,10},{10,12},{12... | collective-permute-start | bytes 1572872 | tf_op jit(solution)/shard_map/ppermute | solution.py:280
  26.0 22.0 %collective-permute-start.11 = (bf16[256,1024]{1,0:T(8,128)(2,1)S(1)}, bf16[256,1024]{1,0:T(8,128)(2,1)S(1)}, u32[]{:S(2)}, u32[]{:S(2)}) collective-permute-start(bf16[256,1024]{1,0:T(8,128)(2,1)S(1)} %collective-permute-done.9.w2), channel_id=1, source_target_pairs={{0,32},{32,64},{64,96},{96,128},{128,160},{160,192},{192,224},{224... | collective-permute-start | bytes 1572872 | tf_op jit(solution)/shard_map/ppermute | solution.py:287
  35.5 9.0 %collective-permute-start.18 = (bf16[128,1024]{1,0:T(8,128)(2,1)S(1)}, bf16[128,1024]{1,0:T(8,128)(2,1)S(1)}, u32[]{:S(2)}, u32[]{:S(2)}) collective-permute-start(bf16[128,1024]{1,0:T(8,128)(2,1)S(1)} %collective-permute-done.17.r1), channel_id=1, source_target_pairs={{0,32},{32,64},{64,96},{96,128},{128,160},{160,192},{192,224},{224... | collective-permute-start | bytes 786440 | tf_op jit(solution)/shard_map/ppermute | solution.py:287
  35.5 15.2 %collective-permute-start.12 = (bf16[256,1024]{1,0:T(8,128)(2,1)S(1)}, bf16[256,1024]{1,0:T(8,128)(2,1)S(1)}, u32[]{:S(2)}, u32[]{:S(2)}) collective-permute-start(bf16[256,1024]{1,0:T(8,128)(2,1)S(1)} %collective-permute-done.10.w3), channel_id=1, source_target_pairs={{0,32},{32,64},{64,96},{96,128},{128,160},{160,192},{192,224},{224... | collective-permute-start | bytes 1572872 | tf_op jit(solution)/shard_map/ppermute | solution.py:287
  44.4 8.2 %collective-permute-start.19 = (bf16[128,1024]{1,0:T(8,128)(2,1)S(1)}, bf16[128,1024]{1,0:T(8,128)(2,1)S(1)}, u32[]{:S(2)}, u32[]{:S(2)}) collective-permute-start(bf16[128,1024]{1,0:T(8,128)(2,1)S(1)} %collective-permute-done.18.r2), channel_id=1, source_target_pairs={{0,32},{32,64},{64,96},{96,128},{128,160},{160,192},{192,224},{224... | collective-permute-start | bytes 786440 | tf_op jit(solution)/shard_map/ppermute | solution.py:287
  45.2 7.5 %collective-permute-start.7 = (bf16[64,2048]{1,0:T(8,128)(2,1)S(1)}, bf16[64,2048]{1,0:T(8,128)(2,1)S(1)}, u32[]{:S(2)}, u32[]{:S(2)}) collective-permute-start(bf16[64,2048]{1,0:T(8,128)(2,1)S(1)} %slice.290), channel_id=1, source_target_pairs={{0,6},{2,0},{4,2},{6,4},{1,7},{3,1},{5,3},{7,5},{8,14},{10,8},{12,... | collective-permute-start | bytes 786440 | tf_op jit(solution)/shard_map/ppermute | solution.py:280
  47.7 8.1 %collective-permute-start.6 = (bf16[64,2048]{1,0:T(8,128)(2,1)S(1)}, bf16[64,2048]{1,0:T(8,128)(2,1)S(1)}, u32[]{:S(2)}, u32[]{:S(2)}) collective-permute-start(bf16[64,2048]{1,0:T(8,128)(2,1)S(1)} %slice.289), channel_id=1, source_target_pairs={{0,2},{2,4},{4,6},{6,0},{1,3},{3,5},{5,7},{7,1},{8,10},{10,12},{12... | collective-permute-start | bytes 786440 | tf_op jit(solution)/shard_map/ppermute | solution.py:280
  48.0 9.9 %collective-permute-start.13 = (bf16[256,1024]{1,0:T(8,128)(2,1)S(1)}, bf16[256,1024]{1,0:T(8,128)(2,1)S(1)}, u32[]{:S(2)}, u32[]{:S(2)}) collective-permute-start(bf16[256,1024]{1,0:T(8,128)(2,1)S(1)} %collective-permute-done.11.w4), channel_id=1, source_target_pairs={{0,32},{32,64},{64,96},{96,128},{128,160},{160,192},{192,224},{224... | collective-permute-start | bytes 1572872 | tf_op jit(solution)/shard_map/ppermute | solution.py:287
  50.7 11.7 %collective-permute-start.14 = (bf16[256,1024]{1,0:T(8,128)(2,1)S(1)}, bf16[256,1024]{1,0:T(8,128)(2,1)S(1)}, u32[]{:S(2)}, u32[]{:S(2)}) collective-permute-start(bf16[256,1024]{1,0:T(8,128)(2,1)S(1)} %collective-permute-done.12), channel_id=1, source_target_pairs={{0,32},{32,64},{64,96},{96,128},{128,160},{160,192},{192,224},{224... | collective-permute-start | bytes 1572872 | tf_op jit(solution)/shard_map/ppermute | solution.py:287
  52.6 10.6 %collective-permute-start.20 = (bf16[128,1024]{1,0:T(8,128)(2,1)S(1)}, bf16[128,1024]{1,0:T(8,128)(2,1)S(1)}, u32[]{:S(2)}, u32[]{:S(2)}) collective-permute-start(bf16[128,1024]{1,0:T(8,128)(2,1)S(1)} %collective-permute-done.19.r3), channel_id=1, source_target_pairs={{0,8},{8,0},{1,9},{9,1},{2,10},{10,2},{3,11},{11,3},{4,12},{12,4},... | collective-permute-start | bytes 786440 | tf_op jit(solution)/shard_map/ppermute | solution.py:276
  63.0 3.0 %copy-start.2 = (bf16[128,8,128]{2,1,0:T(8,128)(2,1)S(1)}, bf16[128,8,128]{2,1,0:T(8,128)(2,1)}, u32[]{:S(2)}) copy-start(bf16[128,8,128]{2,1,0:T(8,128)(2,1)} %param.6) | copy-start | bytes 786436
  63.2 2.9 %copy-start.1 = (s32[8]{0:T(128)S(1)}, s32[8]{0:T(128)}, u32[]{:S(2)}) copy-start(s32[8]{0:T(128)} %lengths.5) | copy-start | bytes 100
  63.3 1.6 %collective-permute-start.21 = (bf16[128,1024]{1,0:T(8,128)(2,1)S(1)}, bf16[128,1024]{1,0:T(8,128)(2,1)S(1)}, u32[]{:S(2)}, u32[]{:S(2)}) collective-permute-start(bf16[128,1024]{1,0:T(8,128)(2,1)S(1)} %get-tuple-element.34), channel_id=1, source_target_pairs={{0,8},{8,0},{1,9},{9,1},{2,10},{10,2},{3,11},{11,3},{4,12},{12,4},... | collective-permute-start | bytes 786440 | tf_op jit(solution)/shard_map/ppermute | solution.py:276
  63.4 2.7 %collective-permute-start.24 = (bf16[128,1024]{1,0:T(8,128)(2,1)S(1)}, bf16[128,1024]{1,0:T(8,128)(2,1)S(1)}, u32[]{:S(2)}, u32[]{:S(2)}) collective-permute-start(bf16[128,1024]{1,0:T(8,128)(2,1)S(1)} %collective-permute-done.17.r1), channel_id=1, source_target_pairs={{0,8},{8,0},{1,9},{9,1},{2,10},{10,2},{3,11},{11,3},{4,12},{12,4},... | collective-permute-start | bytes 786440 | tf_op jit(solution)/shard_map/ppermute | solution.py:276
  63.8 2.3 %collective-permute-start.25 = (bf16[128,1024]{1,0:T(8,128)(2,1)S(1)}, bf16[128,1024]{1,0:T(8,128)(2,1)S(1)}, u32[]{:S(2)}, u32[]{:S(2)}) collective-permute-start(bf16[128,1024]{1,0:T(8,128)(2,1)S(1)} %collective-permute-done.18.r2), channel_id=1, source_target_pairs={{0,8},{8,0},{1,9},{9,1},{2,10},{10,2},{3,11},{11,3},{4,12},{12,4},... | collective-permute-start | bytes 786440 | tf_op jit(solution)/shard_map/ppermute | solution.py:276
  63.9 4.3 %collective-permute-start.22 = (bf16[128,1024]{1,0:T(8,128)(2,1)S(1)}, bf16[128,1024]{1,0:T(8,128)(2,1)S(1)}, u32[]{:S(2)}, u32[]{:S(2)}) collective-permute-start(bf16[128,1024]{1,0:T(8,128)(2,1)S(1)} %get-tuple-element.55), channel_id=1, source_target_pairs={{0,8},{8,0},{1,9},{9,1},{2,10},{10,2},{3,11},{11,3},{4,12},{12,4},... | collective-permute-start | bytes 786440 | tf_op jit(solution)/shard_map/ppermute | solution.py:276
  64.9 7.9 %collective-permute-start.23 = (bf16[128,1024]{1,0:T(8,128)(2,1)S(1)}, bf16[128,1024]{1,0:T(8,128)(2,1)S(1)}, u32[]{:S(2)}, u32[]{:S(2)}) collective-permute-start(bf16[128,1024]{1,0:T(8,128)(2,1)S(1)} %fusion.2), channel_id=1, source_target_pairs={{0,16},{16,0},{1,17},{17,1},{2,18},{18,2},{3,19},{19,3},{4,20},{20... | collective-permute-start | bytes 786440 | tf_op jit(solution)/shard_map/ppermute | solution.py:276
  73.6 2.2 %collective-permute-start.26 = (bf16[512,256]{1,0:T(8,128)(2,1)S(1)}, bf16[512,256]{1,0:T(8,128)(2,1)S(1)}, u32[]{:S(2)}, u32[]{:S(2)}) collective-permute-start(bf16[512,256]{1,0:T(8,128)(2,1)S(1)} %get-tuple-element.41), channel_id=1, source_target_pairs={{0,8},{8,0},{1,9},{9,1},{2,10},{10,2},{3,11},{11,3},{4,12},{12,4},... | collective-permute-start | bytes 786440 | tf_op jit(solution)/shard_map/ppermute | solution.py:276
  75.9 12.6 %collective-permute-start.27 = (bf16[512,256]{1,0:T(8,128)(2,1)S(1)}, bf16[512,256]{1,0:T(8,128)(2,1)S(1)}, u32[]{:S(2)}, u32[]{:S(2)}) collective-permute-start(bf16[512,256]{1,0:T(8,128)(2,1)S(1)} %add_convert_fusion.1), channel_id=1, source_target_pairs={{0,224},{32,0},{64,32},{96,64},{128,96},{160,128},{192,160},{224,1... | collective-permute-start | bytes 786440 | tf_op jit(solution)/shard_map/ppermute | solution.py:287
  79.0 9.7 %collective-permute-start.28 = (bf16[512,256]{1,0:T(8,128)(2,1)S(1)}, bf16[512,256]{1,0:T(8,128)(2,1)S(1)}, u32[]{:S(2)}, u32[]{:S(2)}) collective-permute-start(bf16[512,256]{1,0:T(8,128)(2,1)S(1)} %get-tuple-element.52), channel_id=1, source_target_pairs={{0,8},{8,0},{1,9},{9,1},{2,10},{10,2},{3,11},{11,3},{4,12},{12,4},... | collective-permute-start | bytes 786440 | tf_op jit(solution)/shard_map/ppermute | solution.py:276
  88.8 8.7 %collective-permute-start.29 = (bf16[512,256]{1,0:T(8,128)(2,1)S(1)}, bf16[512,256]{1,0:T(8,128)(2,1)S(1)}, u32[]{:S(2)}, u32[]{:S(2)}) collective-permute-start(bf16[512,256]{1,0:T(8,128)(2,1)S(1)} %add_convert_fusion), channel_id=1, source_target_pairs={{0,224},{32,0},{64,32},{96,64},{128,96},{160,128},{192,160},{224,1... | collective-permute-start | bytes 786440 | tf_op jit(solution)/shard_map/ppermute | solution.py:287
  88.9 8.6 %collective-permute-start.30 = (bf16[512,256]{1,0:T(8,128)(2,1)S(1)}, bf16[512,256]{1,0:T(8,128)(2,1)S(1)}, u32[]{:S(2)}, u32[]{:S(2)}) collective-permute-start(bf16[512,256]{1,0:T(8,128)(2,1)S(1)} %get-tuple-element.54), channel_id=1, source_target_pairs={{0,8},{8,0},{1,9},{9,1},{2,10},{10,2},{3,11},{11,3},{4,12},{12,4},... | collective-permute-start | bytes 786440 | tf_op jit(solution)/shard_map/ppermute | solution.py:276
  97.7 6.5 %collective-permute-start.31 = (bf16[512,256]{1,0:T(8,128)(2,1)S(1)}, bf16[512,256]{1,0:T(8,128)(2,1)S(1)}, u32[]{:S(2)}, u32[]{:S(2)}) collective-permute-start(bf16[512,256]{1,0:T(8,128)(2,1)S(1)} %fusion), channel_id=1, source_target_pairs={{0,224},{32,0},{64,32},{96,64},{128,96},{160,128},{192,160},{224,1... | collective-permute-start | bytes 786440 | tf_op jit(solution)/shard_map/ppermute | solution.py:287
  104.3 1.8 %collective-permute-start.32 = (bf16[256,256]{1,0:T(8,128)(2,1)S(1)}, bf16[256,256]{1,0:T(8,128)(2,1)S(1)}, u32[]{:S(2)}, u32[]{:S(2)}) collective-permute-start(bf16[256,256]{1,0:T(8,128)(2,1)S(1)} %select_convert_fusion), channel_id=1, source_target_pairs={{0,8},{8,0},{1,9},{9,1},{2,10},{10,2},{3,11},{11,3},{4,12},{12,4},... | collective-permute-start | bytes 393224 | tf_op jit(solution)/shard_map/ppermute | solution.py:276
  106.2 3.2 %collective-permute-start.33 = (bf16[128,256]{1,0:T(8,128)(2,1)S(1)}, bf16[128,256]{1,0:T(8,128)(2,1)S(1)}, u32[]{:S(2)}, u32[]{:S(2)}) collective-permute-start(bf16[128,256]{1,0:T(8,128)(2,1)S(1)} %select_convert_fusion.1), channel_id=1, source_target_pairs={{0,16},{16,0},{1,17},{17,1},{2,18},{18,2},{3,19},{19,3},{4,20},{20... | collective-permute-start | bytes 196616 | tf_op jit(solution)/shard_map/ppermute | solution.py:276

commit v5 on v4

--- a/solution.py
+++ b/solution.py
@@ -84,7 +84,7 @@
 
     def work(d, masked):
         k = kv[d, :, 0:HD]
-        v_t = kv[d, :, HD : 2 * HD].astype(F32).T.astype(BF)
+        v_t = kv[d, :, HD : 2 * HD].T
         s = dot(k, q[...], NT)
         if masked:
             s = jnp.where(allowed(z, d, row_pos, start), s, NEG)
@@ -162,7 +162,7 @@
     def plane(d, carry):
         k = kv[d, :, 0:HD]
         v = kv[d, :, HD : 2 * HD]
-        k_t = k.astype(F32).T.astype(BF)
+        k_t = k.T
         p = probs[d].astype(F32) * factors[d]
         dv = dot(p.astype(BF), do[...], NN)
         dp = dot(v, do[...], NT)

time: 111 us -> 108 us (0.973)
  starting transfers between devices: 51.8 us -> 50.1 us
    ppermute x17, starting transfers between devices: 24.8 us -> 17.8 us  [swap(): return lax.ppermute(x, axis, [(0, 1), (1, 0)])]
    ppermute x13, starting transfers between devices: 21.7 us -> 26.9 us  [along_z(): return lax.ppermute(x, ('z', 'c'), pairs)]
    ppermute x13, waiting for transfers between devices: 29.4 us -> 27.8 us  [along_z(): return lax.ppermute(x, ('z', 'c'), pairs)]
where the time goes in v5:
time: 108 us; the launch traced here: 107 us
  starting transfers between devices  50.1 us (46%)
  waiting for transfers between devices  44.4 us (41%)
  Pallas kernels  6.62 us (6%)
  other arithmetic  2.16 us (2%)
  local copies, waits for them, and re-layouts  1.61 us (1%)
  matrix products  1.46 us (1%)
  between operations  1.11 us (1%)
    ppermute x13, waiting for transfers between devices, along_z(): return lax.ppermute(x, ('z', 'c'), pairs)  27.8 us
    ppermute x13, starting transfers between devices, along_z(): return lax.ppermute(x, ('z', 'c'), pairs)  26.9 us
    ppermute x17, starting transfers between devices, swap(): return lax.ppermute(x, axis, [(0, 1), (1, 0)])  17.8 us
    ppermute x17, waiting for transfers between devices, swap(): return lax.ppermute(x, axis, [(0, 1), (1, 0)])  13.4 us
    pallas_call x4, Pallas kernels, call(): pl.pallas_call(kernel, out_shape=outs, in_specs=first + [vmem] * len(args...  6.62 us
    ppermute x4, starting transfers between devices, turn(): return lax.ppermute(x, 'x', [(i, (i + step) % 4) for i in range(4)])  5.38 us
    ppermute x4, waiting for transfers between devices, turn(): return lax.ppermute(x, 'x', [(i, (i + step) % 4) for i in range(4)])  3.18 us
  transfers between devices with their start and end apart: 34, of which 14 were waited for; matrix products, arithmetic and copies ran while one was open for 4% of the time, Pallas kernels for 5%

profile of v5, /device:TPU:1, one launch (start us, length us, event | category | flops | bytes accessed | tf_op | source)
XLA Modules:
  0.0 107.5 jit_solution(1035819152641581741)
XLA Ops:
  0.7 3.3 %collective-permute-start.1 = (bf16[256,1024]{1,0:T(8,128)(2,1)}, bf16[256,1024]{1,0:T(8,128)(2,1)S(1)}, u32[]{:S(2)}, u32[]{:S(2)}) collective-permute-start(bf16[256,1024]{1,0:T(8,128)(2,1)} %w0.1), channel_id=1, source_target_pairs={{0,8},{8,0},{1,9},{9,1},{2,10},{10,2},{3,11},{11,3},{4,12},{12,4},... | collective-permute-start | bytes 1572872 | tf_op jit(solution)/shard_map/ppermute | solution.py:276
  4.0 1.1 %fusion.3 = bf16[16,8192]{1,0:T(8,128)(2,1)S(1)} fusion(s32[]{:T(128)S(6)} %select_n.115, bf16[16,8192]{1,0:T(8,128)(2,1)} %param.9), kind=kLoop, calls=%fused_computation.14 | loop fusion | flops 524288 | bytes 524292 | tf_op jit(solution)/shard_map/concatenate | solution.py:299
  5.3 0.2 collective-permute-start
  5.5 3.9 %collective-permute-start.8 = (bf16[256,1024]{1,0:T(8,128)(2,1)S(1)}, bf16[256,1024]{1,0:T(8,128)(2,1)S(1)}, u32[]{:S(2)}, u32[]{:S(2)}) collective-permute-start(bf16[256,1024]{1,0:T(8,128)(2,1)S(1)} %copy-done), channel_id=1, source_target_pairs={{0,32},{32,64},{64,96},{96,128},{128,160},{160,192},{192,224},{224... | collective-permute-start | bytes 1572872 | tf_op jit(solution)/shard_map/ppermute | solution.py:287
  9.4 1.4 %collective-permute-start.15 = (bf16[128,256]{1,0:T(8,128)(2,1)S(1)}, bf16[128,256]{1,0:T(8,128)(2,1)S(1)}, u32[]{:S(2)}, u32[]{:S(2)}) collective-permute-start(bf16[128,256]{1,0:T(8,128)(2,1)S(1)} %pad_maximum_fusion.2), channel_id=1, source_target_pairs={{0,16},{16,0},{1,17},{17,1},{2,18},{18,2},{3,19},{19,3},{4,20},{20... | collective-permute-start | bytes 196616 | tf_op jit(solution)/shard_map/ppermute | solution.py:276
  10.8 0.3 collective-permute-start.2
  11.1 1.0 collective-permute-start.9
  12.2 2.9 %collective-permute-done.2 = bf16[2,16,2048]{2,1,0:T(8,128)(2,1)S(1)} collective-permute-done((bf16[2,16,2048]{2,1,0:T(8,128)(2,1)S(1)}, bf16[2,16,2048]{2,1,0:T(8,128)(2,1)S(1)}, u32[]{:S(2)}, u32[]{:S(2)}) %collective-permute-start.2) | collective-permute-done | bytes 131104 | tf_op jit(solution)/shard_map/ppermute | solution.py:276
  15.1 2.7 %collective-permute-start.3 = (bf16[64,2048]{1,0:T(8,128)(2,1)S(1)}, bf16[64,2048]{1,0:T(8,128)(2,1)S(1)}, u32[]{:S(2)}, u32[]{:S(2)}) collective-permute-start(bf16[64,2048]{1,0:T(8,128)(2,1)S(1)} %bitcast.57), channel_id=1, source_target_pairs={{0,1},{1,0},{2,3},{3,2},{4,5},{5,4},{6,7},{7,6},{8,9},{9,8},{10,11... | collective-permute-start | bytes 786440 | tf_op jit(solution)/shard_map/ppermute | solution.py:276
  17.8 0.1 collective-permute-start.16
  17.9 3.0 %collective-permute-start.10 = (bf16[256,1024]{1,0:T(8,128)(2,1)S(1)}, bf16[256,1024]{1,0:T(8,128)(2,1)S(1)}, u32[]{:S(2)}, u32[]{:S(2)}) collective-permute-start(bf16[256,1024]{1,0:T(8,128)(2,1)S(1)} %collective-permute-done.8.w1), channel_id=1, source_target_pairs={{0,32},{32,64},{64,96},{96,128},{128,160},{160,192},{192,224},{224... | collective-permute-start | bytes 1572872 | tf_op jit(solution)/shard_map/ppermute | solution.py:287
  20.9 0.1 maximum_select_fusion.2.plane
  21.0 2.4 %collective-permute-start.17 = (bf16[128,1024]{1,0:T(8,128)(2,1)S(1)}, bf16[128,1024]{1,0:T(8,128)(2,1)S(1)}, u32[]{:S(2)}, u32[]{:S(2)}) collective-permute-start(bf16[128,1024]{1,0:T(8,128)(2,1)S(1)} %maximum_select_fusion.2.plane), channel_id=1, source_target_pairs={{0,32},{32,64},{64,96},{96,128},{128,160},{160,192},{192,224},{224... | collective-permute-start | bytes 786440 | tf_op jit(solution)/shard_map/ppermute | solution.py:287
  23.5 2.6 %collective-permute-start.5 = (bf16[128,2048]{1,0:T(8,128)(2,1)S(1)}, bf16[128,2048]{1,0:T(8,128)(2,1)S(1)}, u32[]{:S(2)}, u32[]{:S(2)}) collective-permute-start(bf16[128,2048]{1,0:T(8,128)(2,1)S(1)} %pad_maximum_fusion.gh), channel_id=1, source_target_pairs={{0,6},{2,0},{4,2},{6,4},{1,7},{3,1},{5,3},{7,5},{8,14},{10,8},{12,... | collective-permute-start | bytes 1572872 | tf_op jit(solution)/shard_map/ppermute | solution.py:280
  26.0 2.1 %collective-permute-start.11 = (bf16[256,1024]{1,0:T(8,128)(2,1)S(1)}, bf16[256,1024]{1,0:T(8,128)(2,1)S(1)}, u32[]{:S(2)}, u32[]{:S(2)}) collective-permute-start(bf16[256,1024]{1,0:T(8,128)(2,1)S(1)} %collective-permute-done.9.w2), channel_id=1, source_target_pairs={{0,32},{32,64},{64,96},{96,128},{128,160},{160,192},{192,224},{224... | collective-permute-start | bytes 1572872 | tf_op jit(solution)/shard_map/ppermute | solution.py:287
  28.1 7.4 %collective-permute-done.17.r1 = bf16[128,1024]{1,0:T(8,128)(2,1)S(1)} collective-permute-done((bf16[128,1024]{1,0:T(8,128)(2,1)S(1)}, bf16[128,1024]{1,0:T(8,128)(2,1)S(1)}, u32[]{:S(2)}, u32[]{:S(2)}) %collective-permute-start.17) | collective-permute-done | bytes 262176 | tf_op jit(solution)/shard_map/ppermute | solution.py:287
  35.5 2.7 %collective-permute-start.12 = (bf16[256,1024]{1,0:T(8,128)(2,1)S(1)}, bf16[256,1024]{1,0:T(8,128)(2,1)S(1)}, u32[]{:S(2)}, u32[]{:S(2)}) collective-permute-start(bf16[256,1024]{1,0:T(8,128)(2,1)S(1)} %collective-permute-done.10.w3), channel_id=1, source_target_pairs={{0,32},{32,64},{64,96},{96,128},{128,160},{160,192},{192,224},{224... | collective-permute-start | bytes 1572872 | tf_op jit(solution)/shard_map/ppermute | solution.py:287
  38.2 6.3 %collective-permute-done.18.r2 = bf16[128,1024]{1,0:T(8,128)(2,1)S(1)} collective-permute-done((bf16[128,1024]{1,0:T(8,128)(2,1)S(1)}, bf16[128,1024]{1,0:T(8,128)(2,1)S(1)}, u32[]{:S(2)}, u32[]{:S(2)}) %collective-permute-start.18) | collective-permute-done | bytes 262176 | tf_op jit(solution)/shard_map/ppermute | solution.py:287
  44.4 0.7 collective-permute-start.19
  45.2 2.6 %collective-permute-start.7 = (bf16[64,2048]{1,0:T(8,128)(2,1)S(1)}, bf16[64,2048]{1,0:T(8,128)(2,1)S(1)}, u32[]{:S(2)}, u32[]{:S(2)}) collective-permute-start(bf16[64,2048]{1,0:T(8,128)(2,1)S(1)} %slice.290), channel_id=1, source_target_pairs={{0,6},{2,0},{4,2},{6,4},{1,7},{3,1},{5,3},{7,5},{8,14},{10,8},{12,... | collective-permute-start | bytes 786440 | tf_op jit(solution)/shard_map/ppermute | solution.py:280
  47.7 0.3 collective-permute-start.6
  48.0 2.7 %collective-permute-start.13 = (bf16[256,1024]{1,0:T(8,128)(2,1)S(1)}, bf16[256,1024]{1,0:T(8,128)(2,1)S(1)}, u32[]{:S(2)}, u32[]{:S(2)}) collective-permute-start(bf16[256,1024]{1,0:T(8,128)(2,1)S(1)} %collective-permute-done.11.w4), channel_id=1, source_target_pairs={{0,32},{32,64},{64,96},{96,128},{128,160},{160,192},{192,224},{224... | collective-permute-start | bytes 1572872 | tf_op jit(solution)/shard_map/ppermute | solution.py:287
  50.7 2.0 %collective-permute-start.14 = (bf16[256,1024]{1,0:T(8,128)(2,1)S(1)}, bf16[256,1024]{1,0:T(8,128)(2,1)S(1)}, u32[]{:S(2)}, u32[]{:S(2)}) collective-permute-start(bf16[256,1024]{1,0:T(8,128)(2,1)S(1)} %collective-permute-done.12), channel_id=1, source_target_pairs={{0,32},{32,64},{64,96},{96,128},{128,160},{160,192},{192,224},{224... | collective-permute-start | bytes 1572872 | tf_op jit(solution)/shard_map/ppermute | solution.py:287
  52.7 3.2 %collective-permute-done.6.gu2 = bf16[64,2048]{1,0:T(8,128)(2,1)S(1)} collective-permute-done((bf16[64,2048]{1,0:T(8,128)(2,1)S(1)}, bf16[64,2048]{1,0:T(8,128)(2,1)S(1)}, u32[]{:S(2)}, u32[]{:S(2)}) %collective-permute-start.6) | collective-permute-done | bytes 262176 | tf_op jit(solution)/shard_map/ppermute | solution.py:280
  55.8 1.6 %shard_map.85 = (f32[512,1024]{1,0:T(8,128)S(1)}, bf16[512,768]{1,0:T(8,128)(2,1)S(1)}) custom-call(bf16[128,2048]{1,0:T(8,128)(2,1)S(1)} %pad_maximum_fusion.gh, bf16[128,2048]{1,0:T(8,128)(2,1)S(1)} %collective-permute-done.4.gu, bf16[128,2048]{1,0:T(8,128)(2,1)S(1)} %collective-permute-done.5.gd, bf16[64,2048]{1,0:T(8,128)(2,1)S(1)} %collective-permute-done.6.gu2, ...), custom_call_target="tpu_custom_call" | custom-call | bytes 6291456 | tf_op jit(solution)/shard_map/pallas_call | solution.py:256
  57.5 0.4 fusion.7
  57.9 0.4 fusion.5
  58.4 4.0 %collective-permute-done.14 = bf16[256,1024]{1,0:T(8,128)(2,1)S(1)} collective-permute-done((bf16[256,1024]{1,0:T(8,128)(2,1)S(1)}, bf16[256,1024]{1,0:T(8,128)(2,1)S(1)}, u32[]{:S(2)}, u32[]{:S(2)}) %collective-permute-start.14) | collective-permute-done | bytes 524320 | tf_op jit(solution)/shard_map/ppermute | solution.py:287
  62.4 0.6 add_add_fusion
  63.0 0.0 copy-start.2
  63.0 0.2 convert.4
  63.2 0.0 copy-start.1
  63.3 0.1 collective-permute-start.21
  63.4 0.5 collective-permute-start.24
  63.8 0.1 collective-permute-start.25
  63.9 0.4 collective-permute-start.22
  64.4 0.5 collective-permute-done.21
  64.9 0.1 fusion.2
  64.9 1.1 collective-permute-start.23
  66.1 2.1 %shard_map.86 = (f32[128,1024]{1,0:T(8,128)S(1)}, bf16[6,512,256]{2,1,0:T(8,128)(2,1)S(1)}, bf16[6,512,1024]{2,1,0:T(8,128)(2,1)S(1)}, f32[6,1,1024]{2,1,0:T(1,128)S(1)}) custom-call(s32[8]{0:T(128)S(1)} %copy-done.1, bf16[1024,128]{1,0:T(8,128)(2,1)S(1)} %bitcast.50, bf16[128,1024]{1,0:T(8,128)(2,1)S(1)} %maximum_select_fusion.2.plane, ...), custom_call_target="tpu_custom_call" | custom-call | flops 1 | bytes 6291456 | tf_op jit(solution)/shard_map/pallas_call | solution.py:256
  68.2 4.6 %collective-permute-done.23.o2 = bf16[128,1024]{1,0:T(8,128)(2,1)S(1)} collective-permute-done((bf16[128,1024]{1,0:T(8,128)(2,1)S(1)}, bf16[128,1024]{1,0:T(8,128)(2,1)S(1)}, u32[]{:S(2)}, u32[]{:S(2)}) %collective-permute-start.23) | collective-permute-done | bytes 262176 | tf_op jit(solution)/shard_map/ppermute | solution.py:276
  72.8 0.8 shard_map.87
  73.6 1.0 collective-permute-start.26
  74.7 1.2 %collective-permute-done.26 = bf16[512,256]{1,0:T(8,128)(2,1)S(1)} collective-permute-done((bf16[512,256]{1,0:T(8,128)(2,1)S(1)}, bf16[512,256]{1,0:T(8,128)(2,1)S(1)}, u32[]{:S(2)}, u32[]{:S(2)}) %collective-permute-start.26) | collective-permute-done | bytes 262176 | tf_op jit(solution)/shard_map/ppermute | solution.py:276
  75.8 0.1 add_convert_fusion.1
  75.9 1.1 %collective-permute-start.27 = (bf16[512,256]{1,0:T(8,128)(2,1)S(1)}, bf16[512,256]{1,0:T(8,128)(2,1)S(1)}, u32[]{:S(2)}, u32[]{:S(2)}) collective-permute-start(bf16[512,256]{1,0:T(8,128)(2,1)S(1)} %add_convert_fusion.1), channel_id=1, source_target_pairs={{0,224},{32,0},{64,32},{96,64},{128,96},{160,128},{192,160},{224,1... | collective-permute-start | bytes 786440 | tf_op jit(solution)/shard_map/ppermute | solution.py:287
  77.0 2.0 %shard_map.88 = (bf16[128,1024]{1,0:T(8,128)(2,1)S(1)}, bf16[512,256]{1,0:T(8,128)(2,1)S(1)}, bf16[512,256]{1,0:T(8,128)(2,1)S(1)}, bf16[512,256]{1,0:T(8,128)(2,1)S(1)}, bf16[512,256]{1,0:T(8,128)(2,1)S(1)}) custom-call(s32[8]{0:T(128)S(1)} %copy-done.1, bf16[1024,128]{1,0:T(8,128)(2,1)S(1)} %bitcast.52, bf16[1024,128]{1,0:T(8,128)(2,1)S(1)} %get-tuple-element.43.do, ...), custom_call_target="tpu_custom_call" | custom-call | flops 1677721600 | bytes 6291456 | tf_op jit(solution)/shard_map/pallas_call | solution.py:256
  79.1 3.1 %collective-permute-start.28 = (bf16[512,256]{1,0:T(8,128)(2,1)S(1)}, bf16[512,256]{1,0:T(8,128)(2,1)S(1)}, u32[]{:S(2)}, u32[]{:S(2)}) collective-permute-start(bf16[512,256]{1,0:T(8,128)(2,1)S(1)} %get-tuple-element.52), channel_id=1, source_target_pairs={{0,8},{8,0},{1,9},{9,1},{2,10},{10,2},{3,11},{11,3},{4,12},{12,4},... | collective-permute-start | bytes 786440 | tf_op jit(solution)/shard_map/ppermute | solution.py:276
  82.1 1.0 collective-permute-done.27
  83.1 0.2 collective-permute-done.28
  83.3 0.1 add_convert_fusion
  83.4 2.8 %collective-permute-start.29 = (bf16[512,256]{1,0:T(8,128)(2,1)S(1)}, bf16[512,256]{1,0:T(8,128)(2,1)S(1)}, u32[]{:S(2)}, u32[]{:S(2)}) collective-permute-start(bf16[512,256]{1,0:T(8,128)(2,1)S(1)} %add_convert_fusion), channel_id=1, source_target_pairs={{0,224},{32,0},{64,32},{96,64},{128,96},{160,128},{192,160},{224,1... | collective-permute-start | bytes 786440 | tf_op jit(solution)/shard_map/ppermute | solution.py:287
  86.2 3.4 %collective-permute-start.30 = (bf16[512,256]{1,0:T(8,128)(2,1)S(1)}, bf16[512,256]{1,0:T(8,128)(2,1)S(1)}, u32[]{:S(2)}, u32[]{:S(2)}) collective-permute-start(bf16[512,256]{1,0:T(8,128)(2,1)S(1)} %get-tuple-element.54), channel_id=1, source_target_pairs={{0,8},{8,0},{1,9},{9,1},{2,10},{10,2},{3,11},{11,3},{4,12},{12,4},... | collective-permute-start | bytes 786440 | tf_op jit(solution)/shard_map/ppermute | solution.py:276
  89.6 4.5 %collective-permute-done.29 = bf16[512,256]{1,0:T(8,128)(2,1)S(1)} collective-permute-done((bf16[512,256]{1,0:T(8,128)(2,1)S(1)}, bf16[512,256]{1,0:T(8,128)(2,1)S(1)}, u32[]{:S(2)}, u32[]{:S(2)}) %collective-permute-start.29) | collective-permute-done | bytes 262176 | tf_op jit(solution)/shard_map/ppermute | solution.py:287
  94.2 0.1 fusion
  94.3 2.6 %collective-permute-start.31 = (bf16[512,256]{1,0:T(8,128)(2,1)S(1)}, bf16[512,256]{1,0:T(8,128)(2,1)S(1)}, u32[]{:S(2)}, u32[]{:S(2)}) collective-permute-start(bf16[512,256]{1,0:T(8,128)(2,1)S(1)} %fusion), channel_id=1, source_target_pairs={{0,224},{32,0},{64,32},{96,64},{128,96},{160,128},{192,160},{224,1... | collective-permute-start | bytes 786440 | tf_op jit(solution)/shard_map/ppermute | solution.py:287
  96.9 4.6 %collective-permute-done.31 = bf16[512,256]{1,0:T(8,128)(2,1)S(1)} collective-permute-done((bf16[512,256]{1,0:T(8,128)(2,1)S(1)}, bf16[512,256]{1,0:T(8,128)(2,1)S(1)}, u32[]{:S(2)}, u32[]{:S(2)}) %collective-permute-start.31) | collective-permute-done | bytes 262176 | tf_op jit(solution)/shard_map/ppermute | solution.py:287
  101.5 0.1 add_select_fusion
  101.7 0.1 collective-permute-start.32
  101.8 1.3 %collective-permute-done.32 = bf16[256,256]{1,0:T(8,128)(2,1)S(1)} collective-permute-done((bf16[256,256]{1,0:T(8,128)(2,1)S(1)}, bf16[256,256]{1,0:T(8,128)(2,1)S(1)}, u32[]{:S(2)}, u32[]{:S(2)}) %collective-permute-start.32) | collective-permute-done | bytes 131104 | tf_op jit(solution)/shard_map/ppermute | solution.py:276
  103.2 0.1 collective-permute-start.33
  103.3 0.8 copy.14
  104.0 2.8 %collective-permute-done.33 = bf16[128,256]{1,0:T(8,128)(2,1)S(1)} collective-permute-done((bf16[128,256]{1,0:T(8,128)(2,1)S(1)}, bf16[128,256]{1,0:T(8,128)(2,1)S(1)}, u32[]{:S(2)}, u32[]{:S(2)}) %collective-permute-start.33) | collective-permute-done | bytes 65568 | tf_op jit(solution)/shard_map/ppermute | solution.py:276
  106.9 0.6 slice_bitcast_fusion.4
  (61 shorter events, 0.6 us)
Async XLA Ops:
  0.6 4.8 %copy-start = (bf16[256,1024]{1,0:T(8,128)(2,1)S(1)}, bf16[256,1024]{1,0:T(8,128)(2,1)}, u32[]{:S(2)}) copy-start(bf16[256,1024]{1,0:T(8,128)(2,1)} %w0.1) | copy-start | bytes 1572868
  0.6 8.7 %copy-start.3 = (bf16[128,1,128]{2,0,1:T(8,128)(2,1)S(1)}, bf16[128,1,128]{2,0,1:T(8,128)(2,1)}, u32[]{:S(2)}) copy-start(bf16[128,1,128]{2,0,1:T(8,128)(2,1)} %param.8) | copy-start | bytes 98308
  0.7 8.7 %copy-start.4 = (bf16[128,1,128]{2,0,1:T(8,128)(2,1)S(1)}, bf16[128,1,128]{2,0,1:T(8,128)(2,1)}, u32[]{:S(2)}) copy-start(bf16[128,1,128]{2,0,1:T(8,128)(2,1)} %param.7) | copy-start | bytes 98308
  0.7 10.1 %collective-permute-start.1 = (bf16[256,1024]{1,0:T(8,128)(2,1)}, bf16[256,1024]{1,0:T(8,128)(2,1)S(1)}, u32[]{:S(2)}, u32[]{:S(2)}) collective-permute-start(bf16[256,1024]{1,0:T(8,128)(2,1)} %w0.1), channel_id=1, source_target_pairs={{0,8},{8,0},{1,9},{9,1},{2,10},{10,2},{3,11},{11,3},{4,12},{12,4},... | collective-permute-start | bytes 1572872 | tf_op jit(solution)/shard_map/ppermute | solution.py:276
  5.3 5.4 %collective-permute-start = (bf16[32,2048]{1,0:T(8,128)(2,1)S(1)}, bf16[32,2048]{1,0:T(8,128)(2,1)S(1)}, u32[]{:S(2)}, u32[]{:S(2)}) collective-permute-start(bf16[32,2048]{1,0:T(8,128)(2,1)S(1)} %bitcast.61), channel_id=1, source_target_pairs={{0,8},{8,0},{1,9},{9,1},{2,10},{10,2},{3,11},{11,3},{4,12},{12,4},... | collective-permute-start | bytes 393224 | tf_op jit(solution)/shard_map/ppermute | solution.py:276
  5.5 12.4 %collective-permute-start.8 = (bf16[256,1024]{1,0:T(8,128)(2,1)S(1)}, bf16[256,1024]{1,0:T(8,128)(2,1)S(1)}, u32[]{:S(2)}, u32[]{:S(2)}) collective-permute-start(bf16[256,1024]{1,0:T(8,128)(2,1)S(1)} %copy-done), channel_id=1, source_target_pairs={{0,32},{32,64},{64,96},{96,128},{128,160},{160,192},{192,224},{224... | collective-permute-start | bytes 1572872 | tf_op jit(solution)/shard_map/ppermute | solution.py:287
  9.4 8.4 %collective-permute-start.15 = (bf16[128,256]{1,0:T(8,128)(2,1)S(1)}, bf16[128,256]{1,0:T(8,128)(2,1)S(1)}, u32[]{:S(2)}, u32[]{:S(2)}) collective-permute-start(bf16[128,256]{1,0:T(8,128)(2,1)S(1)} %pad_maximum_fusion.2), channel_id=1, source_target_pairs={{0,16},{16,0},{1,17},{17,1},{2,18},{18,2},{3,19},{19,3},{4,20},{20... | collective-permute-start | bytes 196616 | tf_op jit(solution)/shard_map/ppermute | solution.py:276
  10.8 4.2 %collective-permute-start.2 = (bf16[2,16,2048]{2,1,0:T(8,128)(2,1)S(1)}, bf16[2,16,2048]{2,1,0:T(8,128)(2,1)S(1)}, u32[]{:S(2)}, u32[]{:S(2)}) collective-permute-start(bf16[2,16,2048]{2,1,0:T(8,128)(2,1)S(1)} %fusion.9), channel_id=1, source_target_pairs={{0,16},{16,0},{1,17},{17,1},{2,18},{18,2},{3,19},{19,3},{4,20},{20... | collective-permute-start | bytes 393224 | tf_op jit(solution)/shard_map/ppermute | solution.py:276
  11.1 14.9 %collective-permute-start.9 = (bf16[256,1024]{1,0:T(8,128)(2,1)S(1)}, bf16[256,1024]{1,0:T(8,128)(2,1)S(1)}, u32[]{:S(2)}, u32[]{:S(2)}) collective-permute-start(bf16[256,1024]{1,0:T(8,128)(2,1)S(1)} %collective-permute-done.1), channel_id=1, source_target_pairs={{0,32},{32,64},{64,96},{96,128},{128,160},{160,192},{192,224},{224... | collective-permute-start | bytes 1572872 | tf_op jit(solution)/shard_map/ppermute | solution.py:287
  15.1 8.4 %collective-permute-start.3 = (bf16[64,2048]{1,0:T(8,128)(2,1)S(1)}, bf16[64,2048]{1,0:T(8,128)(2,1)S(1)}, u32[]{:S(2)}, u32[]{:S(2)}) collective-permute-start(bf16[64,2048]{1,0:T(8,128)(2,1)S(1)} %bitcast.57), channel_id=1, source_target_pairs={{0,1},{1,0},{2,3},{3,2},{4,5},{5,4},{6,7},{7,6},{8,9},{9,8},{10,11... | collective-permute-start | bytes 786440 | tf_op jit(solution)/shard_map/ppermute | solution.py:276
  17.8 3.1 %collective-permute-start.16 = (bf16[128,512]{1,0:T(8,128)(2,1)S(1)}, bf16[128,512]{1,0:T(8,128)(2,1)S(1)}, u32[]{:S(2)}, u32[]{:S(2)}) collective-permute-start(bf16[128,512]{1,0:T(8,128)(2,1)S(1)} %maximum_select_fusion.3), channel_id=1, source_target_pairs={{0,8},{8,0},{1,9},{9,1},{2,10},{10,2},{3,11},{11,3},{4,12},{12,4},... | collective-permute-start | bytes 393224 | tf_op jit(solution)/shard_map/ppermute | solution.py:276
  17.9 17.6 %collective-permute-start.10 = (bf16[256,1024]{1,0:T(8,128)(2,1)S(1)}, bf16[256,1024]{1,0:T(8,128)(2,1)S(1)}, u32[]{:S(2)}, u32[]{:S(2)}) collective-permute-start(bf16[256,1024]{1,0:T(8,128)(2,1)S(1)} %collective-permute-done.8.w1), channel_id=1, source_target_pairs={{0,32},{32,64},{64,96},{96,128},{128,160},{160,192},{192,224},{224... | collective-permute-start | bytes 1572872 | tf_op jit(solution)/shard_map/ppermute | solution.py:287
  21.0 14.5 %collective-permute-start.17 = (bf16[128,1024]{1,0:T(8,128)(2,1)S(1)}, bf16[128,1024]{1,0:T(8,128)(2,1)S(1)}, u32[]{:S(2)}, u32[]{:S(2)}) collective-permute-start(bf16[128,1024]{1,0:T(8,128)(2,1)S(1)} %maximum_select_fusion.2.plane), channel_id=1, source_target_pairs={{0,32},{32,64},{64,96},{96,128},{128,160},{160,192},{192,224},{224... | collective-permute-start | bytes 786440 | tf_op jit(solution)/shard_map/ppermute | solution.py:287
  23.5 21.6 %collective-permute-start.5 = (bf16[128,2048]{1,0:T(8,128)(2,1)S(1)}, bf16[128,2048]{1,0:T(8,128)(2,1)S(1)}, u32[]{:S(2)}, u32[]{:S(2)}) collective-permute-start(bf16[128,2048]{1,0:T(8,128)(2,1)S(1)} %pad_maximum_fusion.gh), channel_id=1, source_target_pairs={{0,6},{2,0},{4,2},{6,4},{1,7},{3,1},{5,3},{7,5},{8,14},{10,8},{12,... | collective-permute-start | bytes 1572872 | tf_op jit(solution)/shard_map/ppermute | solution.py:280
  26.0 21.7 %collective-permute-start.4 = (bf16[128,2048]{1,0:T(8,128)(2,1)S(1)}, bf16[128,2048]{1,0:T(8,128)(2,1)S(1)}, u32[]{:S(2)}, u32[]{:S(2)}) collective-permute-start(bf16[128,2048]{1,0:T(8,128)(2,1)S(1)} %pad_maximum_fusion.gh), channel_id=1, source_target_pairs={{0,2},{2,4},{4,6},{6,0},{1,3},{3,5},{5,7},{7,1},{8,10},{10,12},{12... | collective-permute-start | bytes 1572872 | tf_op jit(solution)/shard_map/ppermute | solution.py:280
  26.0 22.0 %collective-permute-start.11 = (bf16[256,1024]{1,0:T(8,128)(2,1)S(1)}, bf16[256,1024]{1,0:T(8,128)(2,1)S(1)}, u32[]{:S(2)}, u32[]{:S(2)}) collective-permute-start(bf16[256,1024]{1,0:T(8,128)(2,1)S(1)} %collective-permute-done.9.w2), channel_id=1, source_target_pairs={{0,32},{32,64},{64,96},{96,128},{128,160},{160,192},{192,224},{224... | collective-permute-start | bytes 1572872 | tf_op jit(solution)/shard_map/ppermute | solution.py:287
  35.5 9.0 %collective-permute-start.18 = (bf16[128,1024]{1,0:T(8,128)(2,1)S(1)}, bf16[128,1024]{1,0:T(8,128)(2,1)S(1)}, u32[]{:S(2)}, u32[]{:S(2)}) collective-permute-start(bf16[128,1024]{1,0:T(8,128)(2,1)S(1)} %collective-permute-done.17.r1), channel_id=1, source_target_pairs={{0,32},{32,64},{64,96},{96,128},{128,160},{160,192},{192,224},{224... | collective-permute-start | bytes 786440 | tf_op jit(solution)/shard_map/ppermute | solution.py:287
  35.5 15.2 %collective-permute-start.12 = (bf16[256,1024]{1,0:T(8,128)(2,1)S(1)}, bf16[256,1024]{1,0:T(8,128)(2,1)S(1)}, u32[]{:S(2)}, u32[]{:S(2)}) collective-permute-start(bf16[256,1024]{1,0:T(8,128)(2,1)S(1)} %collective-permute-done.10.w3), channel_id=1, source_target_pairs={{0,32},{32,64},{64,96},{96,128},{128,160},{160,192},{192,224},{224... | collective-permute-start | bytes 1572872 | tf_op jit(solution)/shard_map/ppermute | solution.py:287
  44.4 8.2 %collective-permute-start.19 = (bf16[128,1024]{1,0:T(8,128)(2,1)S(1)}, bf16[128,1024]{1,0:T(8,128)(2,1)S(1)}, u32[]{:S(2)}, u32[]{:S(2)}) collective-permute-start(bf16[128,1024]{1,0:T(8,128)(2,1)S(1)} %collective-permute-done.18.r2), channel_id=1, source_target_pairs={{0,32},{32,64},{64,96},{96,128},{128,160},{160,192},{192,224},{224... | collective-permute-start | bytes 786440 | tf_op jit(solution)/shard_map/ppermute | solution.py:287
  45.2 7.5 %collective-permute-start.7 = (bf16[64,2048]{1,0:T(8,128)(2,1)S(1)}, bf16[64,2048]{1,0:T(8,128)(2,1)S(1)}, u32[]{:S(2)}, u32[]{:S(2)}) collective-permute-start(bf16[64,2048]{1,0:T(8,128)(2,1)S(1)} %slice.290), channel_id=1, source_target_pairs={{0,6},{2,0},{4,2},{6,4},{1,7},{3,1},{5,3},{7,5},{8,14},{10,8},{12,... | collective-permute-start | bytes 786440 | tf_op jit(solution)/shard_map/ppermute | solution.py:280
  47.7 8.1 %collective-permute-start.6 = (bf16[64,2048]{1,0:T(8,128)(2,1)S(1)}, bf16[64,2048]{1,0:T(8,128)(2,1)S(1)}, u32[]{:S(2)}, u32[]{:S(2)}) collective-permute-start(bf16[64,2048]{1,0:T(8,128)(2,1)S(1)} %slice.289), channel_id=1, source_target_pairs={{0,2},{2,4},{4,6},{6,0},{1,3},{3,5},{5,7},{7,1},{8,10},{10,12},{12... | collective-permute-start | bytes 786440 | tf_op jit(solution)/shard_map/ppermute | solution.py:280
  48.0 9.9 %collective-permute-start.13 = (bf16[256,1024]{1,0:T(8,128)(2,1)S(1)}, bf16[256,1024]{1,0:T(8,128)(2,1)S(1)}, u32[]{:S(2)}, u32[]{:S(2)}) collective-permute-start(bf16[256,1024]{1,0:T(8,128)(2,1)S(1)} %collective-permute-done.11.w4), channel_id=1, source_target_pairs={{0,32},{32,64},{64,96},{96,128},{128,160},{160,192},{192,224},{224... | collective-permute-start | bytes 1572872 | tf_op jit(solution)/shard_map/ppermute | solution.py:287
  50.7 11.7 %collective-permute-start.14 = (bf16[256,1024]{1,0:T(8,128)(2,1)S(1)}, bf16[256,1024]{1,0:T(8,128)(2,1)S(1)}, u32[]{:S(2)}, u32[]{:S(2)}) collective-permute-start(bf16[256,1024]{1,0:T(8,128)(2,1)S(1)} %collective-permute-done.12), channel_id=1, source_target_pairs={{0,32},{32,64},{64,96},{96,128},{128,160},{160,192},{192,224},{224... | collective-permute-start | bytes 1572872 | tf_op jit(solution)/shard_map/ppermute | solution.py:287
  52.6 10.6 %collective-permute-start.20 = (bf16[128,1024]{1,0:T(8,128)(2,1)S(1)}, bf16[128,1024]{1,0:T(8,128)(2,1)S(1)}, u32[]{:S(2)}, u32[]{:S(2)}) collective-permute-start(bf16[128,1024]{1,0:T(8,128)(2,1)S(1)} %collective-permute-done.19.r3), channel_id=1, source_target_pairs={{0,8},{8,0},{1,9},{9,1},{2,10},{10,2},{3,11},{11,3},{4,12},{12,4},... | collective-permute-start | bytes 786440 | tf_op jit(solution)/shard_map/ppermute | solution.py:276
  63.0 3.0 %copy-start.2 = (bf16[128,8,128]{2,1,0:T(8,128)(2,1)S(1)}, bf16[128,8,128]{2,1,0:T(8,128)(2,1)}, u32[]{:S(2)}) copy-start(bf16[128,8,128]{2,1,0:T(8,128)(2,1)} %param.6) | copy-start | bytes 786436
  63.2 2.9 %copy-start.1 = (s32[8]{0:T(128)S(1)}, s32[8]{0:T(128)}, u32[]{:S(2)}) copy-start(s32[8]{0:T(128)} %lengths.5) | copy-start | bytes 100
  63.3 1.6 %collective-permute-start.21 = (bf16[128,1024]{1,0:T(8,128)(2,1)S(1)}, bf16[128,1024]{1,0:T(8,128)(2,1)S(1)}, u32[]{:S(2)}, u32[]{:S(2)}) collective-permute-start(bf16[128,1024]{1,0:T(8,128)(2,1)S(1)} %get-tuple-element.34), channel_id=1, source_target_pairs={{0,8},{8,0},{1,9},{9,1},{2,10},{10,2},{3,11},{11,3},{4,12},{12,4},... | collective-permute-start | bytes 786440 | tf_op jit(solution)/shard_map/ppermute | solution.py:276
  63.4 2.7 %collective-permute-start.24 = (bf16[128,1024]{1,0:T(8,128)(2,1)S(1)}, bf16[128,1024]{1,0:T(8,128)(2,1)S(1)}, u32[]{:S(2)}, u32[]{:S(2)}) collective-permute-start(bf16[128,1024]{1,0:T(8,128)(2,1)S(1)} %collective-permute-done.17.r1), channel_id=1, source_target_pairs={{0,8},{8,0},{1,9},{9,1},{2,10},{10,2},{3,11},{11,3},{4,12},{12,4},... | collective-permute-start | bytes 786440 | tf_op jit(solution)/shard_map/ppermute | solution.py:276
  63.8 2.3 %collective-permute-start.25 = (bf16[128,1024]{1,0:T(8,128)(2,1)S(1)}, bf16[128,1024]{1,0:T(8,128)(2,1)S(1)}, u32[]{:S(2)}, u32[]{:S(2)}) collective-permute-start(bf16[128,1024]{1,0:T(8,128)(2,1)S(1)} %collective-permute-done.18.r2), channel_id=1, source_target_pairs={{0,8},{8,0},{1,9},{9,1},{2,10},{10,2},{3,11},{11,3},{4,12},{12,4},... | collective-permute-start | bytes 786440 | tf_op jit(solution)/shard_map/ppermute | solution.py:276
  63.9 4.3 %collective-permute-start.22 = (bf16[128,1024]{1,0:T(8,128)(2,1)S(1)}, bf16[128,1024]{1,0:T(8,128)(2,1)S(1)}, u32[]{:S(2)}, u32[]{:S(2)}) collective-permute-start(bf16[128,1024]{1,0:T(8,128)(2,1)S(1)} %get-tuple-element.55), channel_id=1, source_target_pairs={{0,8},{8,0},{1,9},{9,1},{2,10},{10,2},{3,11},{11,3},{4,12},{12,4},... | collective-permute-start | bytes 786440 | tf_op jit(solution)/shard_map/ppermute | solution.py:276
  64.9 7.9 %collective-permute-start.23 = (bf16[128,1024]{1,0:T(8,128)(2,1)S(1)}, bf16[128,1024]{1,0:T(8,128)(2,1)S(1)}, u32[]{:S(2)}, u32[]{:S(2)}) collective-permute-start(bf16[128,1024]{1,0:T(8,128)(2,1)S(1)} %fusion.2), channel_id=1, source_target_pairs={{0,16},{16,0},{1,17},{17,1},{2,18},{18,2},{3,19},{19,3},{4,20},{20... | collective-permute-start | bytes 786440 | tf_op jit(solution)/shard_map/ppermute | solution.py:276
  73.6 2.2 %collective-permute-start.26 = (bf16[512,256]{1,0:T(8,128)(2,1)S(1)}, bf16[512,256]{1,0:T(8,128)(2,1)S(1)}, u32[]{:S(2)}, u32[]{:S(2)}) collective-permute-start(bf16[512,256]{1,0:T(8,128)(2,1)S(1)} %get-tuple-element.41), channel_id=1, source_target_pairs={{0,8},{8,0},{1,9},{9,1},{2,10},{10,2},{3,11},{11,3},{4,12},{12,4},... | collective-permute-start | bytes 786440 | tf_op jit(solution)/shard_map/ppermute | solution.py:276
  75.9 7.2 %collective-permute-start.27 = (bf16[512,256]{1,0:T(8,128)(2,1)S(1)}, bf16[512,256]{1,0:T(8,128)(2,1)S(1)}, u32[]{:S(2)}, u32[]{:S(2)}) collective-permute-start(bf16[512,256]{1,0:T(8,128)(2,1)S(1)} %add_convert_fusion.1), channel_id=1, source_target_pairs={{0,224},{32,0},{64,32},{96,64},{128,96},{160,128},{192,160},{224,1... | collective-permute-start | bytes 786440 | tf_op jit(solution)/shard_map/ppermute | solution.py:287
  79.1 4.2 %collective-permute-start.28 = (bf16[512,256]{1,0:T(8,128)(2,1)S(1)}, bf16[512,256]{1,0:T(8,128)(2,1)S(1)}, u32[]{:S(2)}, u32[]{:S(2)}) collective-permute-start(bf16[512,256]{1,0:T(8,128)(2,1)S(1)} %get-tuple-element.52), channel_id=1, source_target_pairs={{0,8},{8,0},{1,9},{9,1},{2,10},{10,2},{3,11},{11,3},{4,12},{12,4},... | collective-permute-start | bytes 786440 | tf_op jit(solution)/shard_map/ppermute | solution.py:276
  83.4 10.8 %collective-permute-start.29 = (bf16[512,256]{1,0:T(8,128)(2,1)S(1)}, bf16[512,256]{1,0:T(8,128)(2,1)S(1)}, u32[]{:S(2)}, u32[]{:S(2)}) collective-permute-start(bf16[512,256]{1,0:T(8,128)(2,1)S(1)} %add_convert_fusion), channel_id=1, source_target_pairs={{0,224},{32,0},{64,32},{96,64},{128,96},{160,128},{192,160},{224,1... | collective-permute-start | bytes 786440 | tf_op jit(solution)/shard_map/ppermute | solution.py:287
  86.2 8.0 %collective-permute-start.30 = (bf16[512,256]{1,0:T(8,128)(2,1)S(1)}, bf16[512,256]{1,0:T(8,128)(2,1)S(1)}, u32[]{:S(2)}, u32[]{:S(2)}) collective-permute-start(bf16[512,256]{1,0:T(8,128)(2,1)S(1)} %get-tuple-element.54), channel_id=1, source_target_pairs={{0,8},{8,0},{1,9},{9,1},{2,10},{10,2},{3,11},{11,3},{4,12},{12,4},... | collective-permute-start | bytes 786440 | tf_op jit(solution)/shard_map/ppermute | solution.py:276
  94.3 7.2 %collective-permute-start.31 = (bf16[512,256]{1,0:T(8,128)(2,1)S(1)}, bf16[512,256]{1,0:T(8,128)(2,1)S(1)}, u32[]{:S(2)}, u32[]{:S(2)}) collective-permute-start(bf16[512,256]{1,0:T(8,128)(2,1)S(1)} %fusion), channel_id=1, source_target_pairs={{0,224},{32,0},{64,32},{96,64},{128,96},{160,128},{192,160},{224,1... | collective-permute-start | bytes 786440 | tf_op jit(solution)/shard_map/ppermute | solution.py:287
  101.7 1.4 %collective-permute-start.32 = (bf16[256,256]{1,0:T(8,128)(2,1)S(1)}, bf16[256,256]{1,0:T(8,128)(2,1)S(1)}, u32[]{:S(2)}, u32[]{:S(2)}) collective-permute-start(bf16[256,256]{1,0:T(8,128)(2,1)S(1)} %select_convert_fusion), channel_id=1, source_target_pairs={{0,8},{8,0},{1,9},{9,1},{2,10},{10,2},{3,11},{11,3},{4,12},{12,4},... | collective-permute-start | bytes 393224 | tf_op jit(solution)/shard_map/ppermute | solution.py:276
  103.2 3.6 %collective-permute-start.33 = (bf16[128,256]{1,0:T(8,128)(2,1)S(1)}, bf16[128,256]{1,0:T(8,128)(2,1)S(1)}, u32[]{:S(2)}, u32[]{:S(2)}) collective-permute-start(bf16[128,256]{1,0:T(8,128)(2,1)S(1)} %select_convert_fusion.1), channel_id=1, source_target_pairs={{0,16},{16,0},{1,17},{17,1},{2,18},{18,2},{3,19},{19,3},{4,20},{20... | collective-permute-start | bytes 196616 | tf_op jit(solution)/shard_map/ppermute | solution.py:276
